TPU v7x, 256 devices: a whole 4x4x8 slice. The times are simulated.
256 devices in a mesh: row: 8 (over y, core), col: 32 (over x, z).
Axes of the slice: x: 4, y: 4, z: 8, core: 2. Of those that a mesh axis runs over, the one named last changes fastest.
Arguments:
- observed: float32 [16, 64, 4096], P(None, 'row', 'col'), may hold values from -6 to 6
- coef_maps: float32 [96, 64, 4096], P(None, 'row', 'col'), may hold values from -1.2 to 1.2
- dictionary: float32 [96, 784], replicated, may hold values from -9 to 9
- consensus: float32 [96, 784], replicated, may hold values from -4 to 4
- dual_vars: float32 [96, 784], replicated, may hold values from -1.8 to 1.8
Outputs:
- new_maps: float32 [96, 64, 4096], P(None, 'row', 'col')
- new_dictionary: float32 [96, 784], replicated
- new_consensus: float32 [96, 784], replicated
- new_duals: float32 [96, 784], replicated
All inputs are finite; a program needn't handle non-finite values.
Results may differ from a plain program's by a relative error of at most 0.0003.
Values sent between devices are 32-bit elements; how exact they have to be, the bound alone decides.
No kernel may reach another device: no remote copies, remote signals or barrier semaphores. Data moves between devices by JAX's collectives and lax.ppermute only.
A program may use at most 128 MiB of HBM per device.

v0:
```python
import math

import jax
import jax.numpy as jnp
from jax import lax
from jax.sharding import PartitionSpec as P

M = 96
C = 16
K = 7
ITERS = 2


step_coef = 0.5
sparsity = 0.1
dict_step = 0.08
penalty = 2.0
HIGH = lax.Precision.HIGHEST


def with_halo(block, sides, width):
    for axis, dim in sides:
        count = lax.axis_size(axis)
        forward = [(i, i + 1) for i in range(count - 1)]
        backward = [(target, source) for source, target in forward]
        low = lax.ppermute(
            lax.slice_in_dim(block, block.shape[dim] - width, None, axis=dim), axis, forward
        )
        high = lax.ppermute(lax.slice_in_dim(block, 0, width, axis=dim), axis, backward)
        block = jnp.concatenate([low, block, high], axis=dim)
    return block


def recon_tile(padded, flat_filters, out_rows, out_cols):
    taps = K * K
    pad_rows = padded.shape[1]
    pad_cols = padded.shape[2]
    flat_maps = padded.reshape(M, pad_rows * pad_cols)
    bands = []
    for band in range(C):
        weights = flat_filters[:, band * taps : (band + 1) * taps]
        planes = lax.dot_general(
            weights,
            flat_maps,
            (((0,), (0,)), ((), ())),
            precision=HIGH,
            preferred_element_type=jnp.float32,
        )
        planes = planes.reshape(taps, pad_rows, pad_cols)
        summed = jnp.zeros((out_rows, out_cols), jnp.float32)
        for row_tap in range(K):
            for col_tap in range(K):
                summed = (
                    summed
                    + planes[
                        row_tap * K + col_tap,
                        row_tap : row_tap + out_rows,
                        col_tap : col_tap + out_cols,
                    ]
                )
        bands.append(summed)
    return jnp.stack(bands, axis=0)


def corr_and_grad(maps_tile, resid_pad, flat_filters, out_rows, out_cols):
    reach = K // 2
    taps = K * K
    flat_maps = maps_tile.reshape(M, out_rows * out_cols)
    corr = jnp.zeros((M, out_rows * out_cols), jnp.float32)
    grad_parts = []
    for band in range(C):
        windows = []
        for row_tap in range(K):
            for col_tap in range(K):
                first_row = 2 * reach - row_tap
                first_col = 2 * reach - col_tap
                windows.append(
                    resid_pad[
                        band, first_row : first_row + out_rows, first_col : first_col + out_cols
                    ].reshape(out_rows * out_cols)
                )
        stacked = jnp.stack(windows, axis=0)
        weights = flat_filters[:, band * taps : (band + 1) * taps]
        corr = corr + jnp.dot(weights, stacked, precision=HIGH, preferred_element_type=jnp.float32)
        grad_parts.append(
            lax.dot_general(
                flat_maps,
                stacked,
                (((1,), (1,)), ((), ())),
                precision=HIGH,
                preferred_element_type=jnp.float32,
            )
        )
    return (corr.reshape(M, out_rows, out_cols), jnp.concatenate(grad_parts, axis=1))


def update_filters(filt_now, cons_now, duals_now, summed_grad):
    filt_next = filt_now - dict_step * (summed_grad + penalty * (filt_now - cons_now + duals_now))
    joined = filt_next + duals_now
    spread = jnp.sqrt(jnp.mean(joined * joined, axis=1, keepdims=True))
    cons_next = joined / jnp.maximum(1.0, spread)
    duals_next = duals_now + filt_next - cons_next
    return (filt_next, cons_next, duals_next)


def local(observed, coef_maps, dictionary, consensus, dual_vars):
    reach = K // 2
    norm_scale = 1.0 / math.sqrt(M * K * K)
    tile_rows = observed.shape[1]
    tile_cols = observed.shape[2]
    maps_now = coef_maps
    filt_now = dictionary
    cons_now = consensus
    duals_now = dual_vars
    for sweep in range(ITERS):
        padded = with_halo(maps_now, (("row", 1), ("col", 2)), reach)
        recon = norm_scale * recon_tile(padded, filt_now, tile_rows, tile_cols)
        resid = recon - observed
        resid_pad = with_halo(resid, (("row", 1), ("col", 2)), reach)
        corr_raw, grad_raw = corr_and_grad(maps_now, resid_pad, filt_now, tile_rows, tile_cols)
        corr = norm_scale * corr_raw
        local_grad = norm_scale * grad_raw
        moved = maps_now - step_coef * corr
        limit = step_coef * sparsity
        maps_now = moved - jnp.clip(moved, -limit, limit)
        summed_grad = lax.psum(local_grad, ("row", "col"))
        filt_now, cons_now, duals_now = update_filters(filt_now, cons_now, duals_now, summed_grad)
    return (maps_now, filt_now, cons_now, duals_now)


def solution(mesh):
    return jax.shard_map(
        local,
        mesh=mesh,
        in_specs=(P(None, "row", "col"), P(None, "row", "col"), P(), P(), P()),
        out_specs=(P(None, "row", "col"), P(), P(), P()),
        check_vma=False,
    )
```

profile of v0, /device:TPU:1, one launch (start us, length us, event | category | flops | bytes accessed | tf_op | source)
XLA Modules:
  0.0 991.5 jit_solution(18126164702819386299)
XLA Ops:
  8.5 4.6 collective-permute-start
  16.4 4.4 collective-permute-done.1
  20.9 3.5 collective-permute-start.2
  25.7 3.4 collective-permute-done.3
  29.8 2.0 convolution_bitcast_fusion
  36.2 2.0 convolution_bitcast_fusion.2
  66.2 2.0 convolution_bitcast_fusion.8
  76.4 2.0 convolution_bitcast_fusion.10
  91.7 2.0 convolution_bitcast_fusion.13
  117.5 3.0 collective-permute-start.4
  122.4 3.2 collective-permute-done.5
  125.7 3.6 collective-permute-start.7
  172.4 3.9 stack.149
  180.7 5.3 stack.148
  187.2 9.6 stack.145
  196.8 2.1 convolution_bitcast_fusion.21
  198.9 9.6 stack.144
  208.5 2.1 convolution_bitcast_fusion.22
  210.6 9.6 stack.138
  220.2 2.1 convolution_bitcast_fusion.28
  222.3 9.6 stack.135
  231.9 2.1 convolution_bitcast_fusion.31
  234.0 9.6 stack.137
  243.6 2.1 convolution_bitcast_fusion.29
  245.8 8.1 stack.147
  253.9 2.1 convolution_bitcast_fusion.19
  267.4 2.7 collective-permute-start.8
  272.2 2.2 concatenate.1585
  277.8 4.9 collective-permute-start.10
  284.0 242.9 %all-reduce.3.cloned.1.call-done = f32[96,784]{0,1:T(8,128)} async-done(((f32[96,784]{0,1:T(8,128)}), f32[96,784]{0,1:T(8,128)}) %all-reduce.3.cloned.1.call-update) | async-done | bytes 301072 | tf_op jit(solution)/shard_map/psum | solution.py:126
  529.6 2.1 fusion.118
  531.6 2.1 fusion.120
  533.7 2.1 fusion.122
  535.8 2.1 fusion.124
  537.9 2.1 fusion.126
  540.0 2.1 fusion.128
  542.1 2.1 fusion.130
  544.2 2.1 fusion.132
  546.3 2.5 fusion.134
  548.8 2.1 fusion.136
  550.9 2.1 fusion.138
  553.0 2.1 fusion.140
  555.1 2.1 fusion.142
  557.2 2.1 fusion.144
  559.3 2.1 fusion.146
  561.4 2.1 fusion.148
  570.6 3.7 collective-permute-start.12
  576.9 2.6 collective-permute-done.13
  579.6 2.5 collective-permute-start.15
  624.9 3.2 stack.166
  632.4 5.4 stack.165
  638.9 9.5 stack.162
  648.4 2.0 fusion.14
  650.5 9.5 stack.161
  660.0 2.0 fusion.16
  662.1 9.6 stack.155
  671.7 2.0 fusion.28
  673.8 9.6 stack.152
  683.4 2.0 fusion.34
  685.4 9.6 stack.154
  695.0 2.0 fusion.30
  697.1 8.7 stack.164
  707.8 21.7 %concatenate.1593 = f32[96,784]{0,1:T(8,128)} concatenate(f32[96,49]{0,1:T(8,128)} %fusion.34, f32[96,49]{0,1:T(8,128)S(1)} %fusion.32, f32[96,49]{0,1:T(8,128)} %fusion.30, f32[96,49]{0,1:T(8,128)} %fusion.28, f32[96,49]{0,1:T(8,128)} %fusion.26, f32[96,49]{0,1:T(8,128)} %fusion.24, f32[96,49]{0,1:T(8,128)S(1)} %fusion.22, f32[96,49]{0,1:T(8,128)} %fusion.20, ...), dimensions={1} | concatenate | bytes 602112 | tf_op jit(solution)/shard_map/concatenate | solution.py:94
  742.9 237.3 %all-reduce.5.cloned.1.call-done = f32[96,784]{0,1:T(8,128)} async-done(((f32[96,784]{0,1:T(8,128)}), f32[96,784]{0,1:T(8,128)}) %all-reduce.5.cloned.1.call-update) | async-done | bytes 301072 | tf_op jit(solution)/shard_map/psum | solution.py:126
  (1014 shorter events, 228.1 us)
Async XLA Ops:
  7.2 519.7 %all-reduce.3.cloned.1.call-start = ((), (), s32[]{:S(2)}) async-start(), calls=%async_computation | async-start | bytes 802816 | tf_op jit(solution)/shard_map/psum | solution.py:126
  8.5 7.9 collective-permute-start
  13.1 7.7 collective-permute-start.1
  20.9 4.9 collective-permute-start.2
  24.4 4.8 collective-permute-start.3
  117.5 4.9 collective-permute-start.4
  120.5 5.1 collective-permute-start.5
  125.7 11.3 %collective-permute-start.7 = (f32[16,14,3]{2,0,1:T(8,128)S(1)}, f32[16,14,3]{2,0,1:T(8,128)S(1)}, u32[]{:S(2)}, u32[]{:S(2)}) collective-permute-start(f32[16,14,3]{2,0,1:T(8,128)S(1)} %get-tuple-element.2170), channel_id=1, source_target_pairs={{0,1},{1,2},{2,3},{3,4},{4,5},{5,6},{6,7},{7,8},{8,9},{9,10},{10,1... | collective-permute-start | bytes 8072 | tf_op jit(solution)/shard_map/ppermute | solution.py:26
  129.3 7.7 collective-permute-start.6
  180.7 18.2 %copy-start.59 = (f32[1,1024]{1,0:T(1,128)S(1)}, f32[1,1024]{1,0:T(1,128)}, u32[]{:S(2)}) copy-start(f32[1,1024]{1,0:T(1,128)} %get-tuple-element.2347) | copy-start | bytes 12292
  180.7 18.2 %copy-start.60 = (f32[1,1024]{1,0:T(1,128)S(1)}, f32[1,1024]{1,0:T(1,128)}, u32[]{:S(2)}) copy-start(f32[1,1024]{1,0:T(1,128)} %get-tuple-element.2348) | copy-start | bytes 12292
  187.2 23.4 %copy-start.53 = (f32[1,1024]{1,0:T(1,128)S(1)}, f32[1,1024]{1,0:T(1,128)}, u32[]{:S(2)}) copy-start(f32[1,1024]{1,0:T(1,128)} %get-tuple-element.2306) | copy-start | bytes 12292
  187.2 23.4 %copy-start.54 = (f32[1,1024]{1,0:T(1,128)S(1)}, f32[1,1024]{1,0:T(1,128)}, u32[]{:S(2)}) copy-start(f32[1,1024]{1,0:T(1,128)} %get-tuple-element.2307) | copy-start | bytes 12292
  187.2 23.4 %copy-start.55 = (f32[1,1024]{1,0:T(1,128)S(1)}, f32[1,1024]{1,0:T(1,128)}, u32[]{:S(2)}) copy-start(f32[1,1024]{1,0:T(1,128)} %get-tuple-element.2308) | copy-start | bytes 12292
  198.9 23.4 %copy-start.47 = (f32[1,1024]{1,0:T(1,128)S(1)}, f32[1,1024]{1,0:T(1,128)}, u32[]{:S(2)}) copy-start(f32[1,1024]{1,0:T(1,128)} %get-tuple-element.2269) | copy-start | bytes 12292
  198.9 23.4 %copy-start.48 = (f32[1,1024]{1,0:T(1,128)S(1)}, f32[1,1024]{1,0:T(1,128)}, u32[]{:S(2)}) copy-start(f32[1,1024]{1,0:T(1,128)} %get-tuple-element.2270) | copy-start | bytes 12292
  198.9 23.4 %copy-start.49 = (f32[1,1024]{1,0:T(1,128)S(1)}, f32[1,1024]{1,0:T(1,128)}, u32[]{:S(2)}) copy-start(f32[1,1024]{1,0:T(1,128)} %get-tuple-element.2271) | copy-start | bytes 12292
  210.6 23.4 %copy-start.43 = (f32[1,1024]{1,0:T(1,128)S(1)}, f32[1,1024]{1,0:T(1,128)}, u32[]{:S(2)}) copy-start(f32[1,1024]{1,0:T(1,128)} %get-tuple-element.2401) | copy-start | bytes 12292
  222.3 23.4 %copy-start.66 = (f32[1,1024]{1,0:T(1,128)S(1)}, f32[1,1024]{1,0:T(1,128)}, u32[]{:S(2)}) copy-start(f32[1,1024]{1,0:T(1,128)} %get-tuple-element.1652) | copy-start | bytes 12292
  222.3 23.4 %copy-start.67 = (f32[1,1024]{1,0:T(1,128)S(1)}, f32[1,1024]{1,0:T(1,128)}, u32[]{:S(2)}) copy-start(f32[1,1024]{1,0:T(1,128)} %get-tuple-element.1653) | copy-start | bytes 12292
  222.3 23.4 %copy-start.68 = (f32[1,1024]{1,0:T(1,128)S(1)}, f32[1,1024]{1,0:T(1,128)}, u32[]{:S(2)}) copy-start(f32[1,1024]{1,0:T(1,128)} %get-tuple-element.1654) | copy-start | bytes 12292
  231.9 13.9 %copy-start.90 = (f32[1,1024]{1,0:T(1,128)S(1)}, f32[1,1024]{1,0:T(1,128)}, u32[]{:S(2)}) copy-start(f32[1,1024]{1,0:T(1,128)} %get-tuple-element.1613) | copy-start | bytes 12292
  231.9 13.9 %copy-start.91 = (f32[1,1024]{1,0:T(1,128)S(1)}, f32[1,1024]{1,0:T(1,128)}, u32[]{:S(2)}) copy-start(f32[1,1024]{1,0:T(1,128)} %get-tuple-element.1614) | copy-start | bytes 12292
  231.9 13.9 %copy-start.92 = (f32[1,1024]{1,0:T(1,128)S(1)}, f32[1,1024]{1,0:T(1,128)}, u32[]{:S(2)}) copy-start(f32[1,1024]{1,0:T(1,128)} %get-tuple-element.1615) | copy-start | bytes 12292
  231.9 13.9 %copy-start.93 = (f32[1,1024]{1,0:T(1,128)S(1)}, f32[1,1024]{1,0:T(1,128)}, u32[]{:S(2)}) copy-start(f32[1,1024]{1,0:T(1,128)} %get-tuple-element.1616) | copy-start | bytes 12292
  231.9 13.9 %copy-start.94 = (f32[1,1024]{1,0:T(1,128)S(1)}, f32[1,1024]{1,0:T(1,128)}, u32[]{:S(2)}) copy-start(f32[1,1024]{1,0:T(1,128)} %get-tuple-element.1617) | copy-start | bytes 12292
  231.9 13.9 %copy-start.95 = (f32[1,1024]{1,0:T(1,128)S(1)}, f32[1,1024]{1,0:T(1,128)}, u32[]{:S(2)}) copy-start(f32[1,1024]{1,0:T(1,128)} %get-tuple-element.1618) | copy-start | bytes 12292
  267.4 9.3 collective-permute-start.8
  270.1 7.7 collective-permute-start.9
  275.3 704.9 %all-reduce.5.cloned.1.call-start = ((), (), s32[]{:S(2)}) async-start(), calls=%async_computation.1 | async-start | bytes 802816 | tf_op jit(solution)/shard_map/psum | solution.py:126
  277.8 251.0 %collective-permute-start.10 = (f32[96,14,3]{0,1,2:T(8,128)S(1)}, f32[96,14,3]{0,1,2:T(8,128)S(1)}, u32[]{:S(2)}, u32[]{:S(2)}) collective-permute-start(f32[96,14,3]{0,1,2:T(8,128)S(1)} %get-tuple-element.26), channel_id=1, source_target_pairs={{0,1},{1,2},{2,3},{3,4},{4,5},{5,6},{6,7},{7,8},{8,9},{9,10},{10,1... | collective-permute-start | bytes 48392 | tf_op jit(solution)/shard_map/ppermute | solution.py:26
  282.7 246.1 %collective-permute-start.11 = (f32[96,14,3]{0,1,2:T(8,128)S(1)}, f32[96,14,3]{0,1,2:T(8,128)S(1)}, u32[]{:S(2)}, u32[]{:S(2)}) collective-permute-start(f32[96,14,3]{0,1,2:T(8,128)S(1)} %get-tuple-element.27), channel_id=1, source_target_pairs={{1,0},{2,1},{3,2},{4,3},{5,4},{6,5},{7,6},{8,7},{9,8},{10,9},{11,1... | collective-permute-start | bytes 48392 | tf_op jit(solution)/shard_map/ppermute | solution.py:29
  570.6 6.2 collective-permute-start.12
  574.3 5.1 collective-permute-start.13
  579.6 10.7 %collective-permute-start.15 = (f32[16,14,3]{2,0,1:T(8,128)S(1)}, f32[16,14,3]{2,0,1:T(8,128)S(1)}, u32[]{:S(2)}, u32[]{:S(2)}) collective-permute-start(f32[16,14,3]{2,0,1:T(8,128)S(1)} %get-tuple-element.2166), channel_id=1, source_target_pairs={{0,1},{1,2},{2,3},{3,4},{4,5},{5,6},{6,7},{7,8},{8,9},{9,10},{10,1... | collective-permute-start | bytes 8072 | tf_op jit(solution)/shard_map/ppermute | solution.py:26
  582.1 8.2 collective-permute-start.14
  632.3 18.1 %copy-start.56 = (f32[1,1024]{1,0:T(1,128)S(1)}, f32[1,1024]{1,0:T(1,128)}, u32[]{:S(2)}) copy-start(f32[1,1024]{1,0:T(1,128)} %get-tuple-element.2251) | copy-start | bytes 12292
  632.3 18.0 %copy-start.57 = (f32[1,1024]{1,0:T(1,128)S(1)}, f32[1,1024]{1,0:T(1,128)}, u32[]{:S(2)}) copy-start(f32[1,1024]{1,0:T(1,128)} %get-tuple-element.2252) | copy-start | bytes 12292
  632.4 18.0 %copy-start.58 = (f32[1,1024]{1,0:T(1,128)S(1)}, f32[1,1024]{1,0:T(1,128)}, u32[]{:S(2)}) copy-start(f32[1,1024]{1,0:T(1,128)} %get-tuple-element.2253) | copy-start | bytes 12292
  632.4 18.0 %copy-start.70 = (f32[1,1024]{1,0:T(1,128)S(1)}, f32[1,1024]{1,0:T(1,128)}, u32[]{:S(2)}) copy-start(f32[1,1024]{1,0:T(1,128)} %get-tuple-element.2230) | copy-start | bytes 12292
  632.4 18.0 %copy-start.71 = (f32[1,1024]{1,0:T(1,128)S(1)}, f32[1,1024]{1,0:T(1,128)}, u32[]{:S(2)}) copy-start(f32[1,1024]{1,0:T(1,128)} %get-tuple-element.2231) | copy-start | bytes 12292
  632.4 18.0 %copy-start.72 = (f32[1,1024]{1,0:T(1,128)S(1)}, f32[1,1024]{1,0:T(1,128)}, u32[]{:S(2)}) copy-start(f32[1,1024]{1,0:T(1,128)} %get-tuple-element.2232) | copy-start | bytes 12292
  638.9 23.1 %copy-start.50 = (f32[1,1024]{1,0:T(1,128)S(1)}, f32[1,1024]{1,0:T(1,128)}, u32[]{:S(2)}) copy-start(f32[1,1024]{1,0:T(1,128)} %get-tuple-element.2210) | copy-start | bytes 12292
  638.9 23.1 %copy-start.51 = (f32[1,1024]{1,0:T(1,128)S(1)}, f32[1,1024]{1,0:T(1,128)}, u32[]{:S(2)}) copy-start(f32[1,1024]{1,0:T(1,128)} %get-tuple-element.2211) | copy-start | bytes 12292
  638.9 23.1 %copy-start.52 = (f32[1,1024]{1,0:T(1,128)S(1)}, f32[1,1024]{1,0:T(1,128)}, u32[]{:S(2)}) copy-start(f32[1,1024]{1,0:T(1,128)} %get-tuple-element.2212) | copy-start | bytes 12292
  650.4 23.3 %copy-start.35 = (f32[1,1024]{1,0:T(1,128)S(1)}, f32[1,1024]{1,0:T(1,128)}, u32[]{:S(2)}) copy-start(f32[1,1024]{1,0:T(1,128)} %get-tuple-element.2382) | copy-start | bytes 12292
  650.4 23.2 %copy-start.38 = (f32[1,1024]{1,0:T(1,128)S(1)}, f32[1,1024]{1,0:T(1,128)}, u32[]{:S(2)}) copy-start(f32[1,1024]{1,0:T(1,128)} %get-tuple-element.2200) | copy-start | bytes 12292
  650.4 23.2 %copy-start.39 = (f32[1,1024]{1,0:T(1,128)S(1)}, f32[1,1024]{1,0:T(1,128)}, u32[]{:S(2)}) copy-start(f32[1,1024]{1,0:T(1,128)} %get-tuple-element.2201) | copy-start | bytes 12292
  650.5 23.2 %copy-start.40 = (f32[1,1024]{1,0:T(1,128)S(1)}, f32[1,1024]{1,0:T(1,128)}, u32[]{:S(2)}) copy-start(f32[1,1024]{1,0:T(1,128)} %get-tuple-element.2202) | copy-start | bytes 12292
  650.5 23.2 %copy-start.44 = (f32[1,1024]{1,0:T(1,128)S(1)}, f32[1,1024]{1,0:T(1,128)}, u32[]{:S(2)}) copy-start(f32[1,1024]{1,0:T(1,128)} %get-tuple-element.2173) | copy-start | bytes 12292
  650.5 23.2 %copy-start.45 = (f32[1,1024]{1,0:T(1,128)S(1)}, f32[1,1024]{1,0:T(1,128)}, u32[]{:S(2)}) copy-start(f32[1,1024]{1,0:T(1,128)} %get-tuple-element.2174) | copy-start | bytes 12292
  650.5 23.2 %copy-start.46 = (f32[1,1024]{1,0:T(1,128)S(1)}, f32[1,1024]{1,0:T(1,128)}, u32[]{:S(2)}) copy-start(f32[1,1024]{1,0:T(1,128)} %get-tuple-element.2175) | copy-start | bytes 12292
  662.0 23.4 %copy-start.30 = (f32[1,1024]{1,0:T(1,128)S(1)}, f32[1,1024]{1,0:T(1,128)}, u32[]{:S(2)}) copy-start(f32[1,1024]{1,0:T(1,128)} %get-tuple-element.2207) | copy-start | bytes 12292
  662.0 23.4 %copy-start.31 = (f32[1,1024]{1,0:T(1,128)S(1)}, f32[1,1024]{1,0:T(1,128)}, u32[]{:S(2)}) copy-start(f32[1,1024]{1,0:T(1,128)} %get-tuple-element.2209) | copy-start | bytes 12292
  662.0 23.4 %copy-start.36 = (f32[1,1024]{1,0:T(1,128)S(1)}, f32[1,1024]{1,0:T(1,128)}, u32[]{:S(2)}) copy-start(f32[1,1024]{1,0:T(1,128)} %get-tuple-element.2179) | copy-start | bytes 12292
  662.0 23.4 %copy-start.37 = (f32[1,1024]{1,0:T(1,128)S(1)}, f32[1,1024]{1,0:T(1,128)}, u32[]{:S(2)}) copy-start(f32[1,1024]{1,0:T(1,128)} %get-tuple-element.2180) | copy-start | bytes 12292
  662.1 23.4 %copy-start.41 = (f32[1,1024]{1,0:T(1,128)S(1)}, f32[1,1024]{1,0:T(1,128)}, u32[]{:S(2)}) copy-start(f32[1,1024]{1,0:T(1,128)} %get-tuple-element.2182) | copy-start | bytes 12292
  662.1 23.4 %copy-start.42 = (f32[1,1024]{1,0:T(1,128)S(1)}, f32[1,1024]{1,0:T(1,128)}, u32[]{:S(2)}) copy-start(f32[1,1024]{1,0:T(1,128)} %get-tuple-element.2380) | copy-start | bytes 12292
  673.7 23.3 %copy-start.32 = (f32[1,1024]{1,0:T(1,128)S(1)}, f32[1,1024]{1,0:T(1,128)}, u32[]{:S(2)}) copy-start(f32[1,1024]{1,0:T(1,128)} %get-tuple-element.2261) | copy-start | bytes 12292
  673.7 23.3 %copy-start.33 = (f32[1,1024]{1,0:T(1,128)S(1)}, f32[1,1024]{1,0:T(1,128)}, u32[]{:S(2)}) copy-start(f32[1,1024]{1,0:T(1,128)} %get-tuple-element.2262) | copy-start | bytes 12292
  673.7 23.3 %copy-start.34 = (f32[1,1024]{1,0:T(1,128)S(1)}, f32[1,1024]{1,0:T(1,128)}, u32[]{:S(2)}) copy-start(f32[1,1024]{1,0:T(1,128)} %get-tuple-element.2263) | copy-start | bytes 12292
  707.8 23.6 %copy-start.8 = (f32[49,1024]{1,0:T(8,128)S(1)}, f32[49,1024]{1,0:T(8,128)}, u32[]{:S(2)}) copy-start(f32[49,1024]{1,0:T(8,128)} %stack.152) | copy-start | bytes 602116
  741.8 238.3 %copy-start.11 = (f32[96,784]{0,1:T(8,128)S(1)}, f32[96,784]{0,1:T(8,128)}, u32[]{:S(2)}) copy-start(f32[96,784]{0,1:T(8,128)} %get-tuple-element.24) | copy-start | bytes 903172
  741.8 238.3 %copy-start.335 = (f32[96]{0:T(128)S(1)}, f32[96]{0:T(128)}, u32[]{:S(2)}) copy-start(f32[96]{0:T(128)} %sqrt_maximum_fusion.1) | copy-start | bytes 1156
  (290 other events, 1208.9 us)
Sparse Core Ops, SparseCore 0:
  275.4 251.3 all-reduce.2
  731.5 248.6 all-reduce.4
where the time goes:
time: 1010 us; the launch traced here: 991 us
  waiting for transfers between devices  496 us (49%)
  local copies, waits for them, and re-layouts  263 us (26%)
  matrix products  131 us (13%)
  starting transfers between devices  41.6 us (4%)
  other arithmetic  38.8 us (4%)
  between operations  20.5 us (2%)
    psum x2, waiting for transfers between devices, local(): summed_grad = lax.psum(local_grad, ('row', 'col'))  480 us
    another operation x107, local copies, waits for them, and re-layouts, corr_and_grad(): stacked = jnp.stack(windows, axis=0)  186 us
    dot_general x32, matrix products, recon_tile(): lax.dot_general(weights, flat_maps, (((0,), (0,)), ((), ())), precision=H...  64.1 us
    dot_general x32, matrix products, corr_and_grad(): lax.dot_general(flat_maps, stacked, (((1,), (1,)), ((), ())), precision=H...  45.1 us
    ppermute x8, starting transfers between devices, with_halo(): lax.ppermute(lax.slice_in_dim(block, block.shape[dim] - width, None, axis...  28.5 us
    slice x48, local copies, waits for them, and re-layouts, recon_tile(): planes[row_tap * K + col_tap, row_tap:row_tap + out_rows, col_tap:col_tap...  26.7 us
    concatenate x2, local copies, waits for them, and re-layouts, corr_and_grad(): jnp.concatenate(grad_parts, axis=1)  23.9 us
    dot_general x32, matrix products, corr_and_grad(): jnp.dot(weights, stacked, precision=HIGH, preferred_element_type=jnp.floa...  22.3 us
  transfers between devices with their start and end apart: 18, of which 8 were waited for; matrix products, arithmetic and copies ran while one was open for 3% of the time, Pallas kernels for 0%

commit v1 on v0

v1 whole, which is shorter than its diff:
```python
import functools
import math

import jax
import jax.numpy as jnp
from jax import lax
from jax.experimental import pallas as pl
from jax.experimental.pallas import tpu as pltpu
from jax.sharding import PartitionSpec as P

M = 96
C = 16
K = 7
REACH = 3
ITERS = 2
ROWS = 8
LANES = 128
PAD_ROWS = ROWS + 2 * REACH
TAPS = K * K
FLAT = C * TAPS
WIDE = K * LANES
D_ROWS = K * M
G_ROWS = 704
SLAB = 8 * M

step_coef = 0.5
sparsity = 0.1
dict_step = 0.08
penalty = 2.0
norm_scale = 1.0 / math.sqrt(M * K * K)

F32 = jnp.float32
BF16 = jnp.bfloat16


def shape(*dims):
    return jax.ShapeDtypeStruct(dims, F32)


def call(kernel, outs, scratch=()):
    return pl.pallas_call(
        kernel,
        out_shape=outs,
        scratch_shapes=list(scratch),
        compiler_params=pltpu.CompilerParams(vmem_limit_bytes=28 * 1024 * 1024),
    )


def split2(value):
    high = value.astype(BF16)
    return high, (value - high.astype(F32)).astype(BF16)


def split3(value):
    high = value.astype(BF16)
    rest = value - high.astype(F32)
    mid = rest.astype(BF16)
    return high, mid, (rest - mid.astype(F32)).astype(BF16)


def roll(value, shift):
    shift = shift % LANES
    return value if shift == 0 else pltpu.roll(value, shift, 1)


def lane_of(rows):
    return lax.broadcasted_iota(jnp.int32, (rows, LANES), 1)


def matmul(a, b):
    return jnp.dot(a, b, preferred_element_type=F32)


def matmul_nt(a, b):
    return lax.dot_general(a, b, (((1,), (1,)), ((), ())), preferred_element_type=F32)


def rows_kernel(maps, by_row, top, bottom):
    for y in range(ROWS):
        value = maps[:, y, :]
        by_row[y * M : (y + 1) * M, :] = value
        if y < REACH:
            top[y * M : (y + 1) * M, :] = value
        if y >= ROWS - REACH:
            at = (y - ROWS + REACH) * M
            bottom[at : at + M, :] = value


def flat_of(lane):
    row_tap = lane >> 7
    col_tap = (lane >> 4) & 7
    band = lane & 15
    return jnp.where(col_tap < K, band * TAPS + row_tap * K + col_tap, -1)


def to_rows_kernel(filt, cons, duals, filt_out, cons_out, duals_out, stacked):
    stacked[:, 6 * LANES :] = jnp.zeros((9 * M, LANES), BF16)
    for i, ref in enumerate((filt, cons, duals)):
        for j, part in enumerate(split3(ref[...])):
            at = (3 * i + j) * M
            stacked[at : at + M, :FLAT] = part
    source = lax.broadcasted_iota(jnp.int32, (WIDE, LANES), 0)
    lane = lane_of(WIDE)
    for a in range(K):
        pick = (source == flat_of(lane + a * LANES)).astype(F32).astype(BF16)
        moved = matmul(stacked[...], pick)
        for i, ref in enumerate((filt_out, cons_out, duals_out)):
            at = 3 * i * M
            ref[a * M : (a + 1) * M, :] = (
                moved[at : at + M] + moved[at + M : at + 2 * M] + moved[at + 2 * M : at + 3 * M]
            )


def padded_row(y, size, own, above, below):
    if y < REACH:
        return above[y * size : (y + 1) * size, :]
    if y < REACH + ROWS:
        at = (y - REACH) * size
        return own[at : at + size, :]
    at = (y - REACH - ROWS) * size
    return below[at : at + size, :]


def pack_kernel(size, own, above, below, left_edge, right_edge):
    lane = lane_of(size)
    left = jnp.zeros((size, LANES), F32)
    right = jnp.zeros((size, LANES), F32)
    for y in range(PAD_ROWS):
        value = padded_row(y, size, own, above, below)
        here = (lane >= 3 * y) & (lane < 3 * y + 3)
        left = jnp.where(here, roll(value, 3 * y), left)
        right = jnp.where(here, roll(value, 3 * y + 3), right)
    left_edge[...] = left
    right_edge[...] = right


def neighbours(axis, toward_high, toward_low):
    count = lax.axis_size(axis)
    up = [(i, i + 1) for i in range(count - 1)]
    down = [(i + 1, i) for i in range(count - 1)]
    return lax.ppermute(toward_high, axis, up), lax.ppermute(toward_low, axis, down)


def halos(size, own, top, bottom):
    above, below = neighbours("row", bottom, top)
    left_edge, right_edge = call(
        functools.partial(pack_kernel, size), [shape(size, LANES)] * 2
    )(own, above, below)
    left, right = neighbours("col", right_edge, left_edge)
    return above, below, left, right


def recon_and_grad(
    maps, above, below, left, right, observed, filt,
    resid_out, top, bottom, grad, x_hi, x_lo, h_hi, h_lo, r_all, r_edge,
):
    for y in range(PAD_ROWS):
        hi, lo = split2(padded_row(y, M, maps, above, below))
        for ref, part in ((x_hi, hi), (x_lo, lo)):
            ref[y * M : (y + 1) * M, :LANES] = part
            if y > 0:
                ref[(y - 1) * M : y * M, LANES:] = part
    for ref in (x_hi, x_lo):
        ref[(PAD_ROWS - 1) * M :, LANES:] = jnp.zeros((M, LANES), BF16)
    edge = jnp.where(lane_of(M) < 64, right[...], roll(left[...], 64))
    for a in range(K):
        hi, lo = split2(roll(edge, -3 * a))
        h_hi[a * M : (a + 1) * M, :] = hi
        h_lo[a * M : (a + 1) * M, :] = lo
    for ref in (h_hi, h_lo):
        ref[D_ROWS:, :] = jnp.zeros((SLAB - D_ROWS, LANES), BF16)

    turned = jnp.concatenate([filt, jnp.zeros((SLAB - D_ROWS, LANES), F32)], axis=0).T
    d_hi, d_lo = split2(turned)
    d_both = jnp.concatenate([d_hi, d_lo], axis=0)

    def apply(hi, lo):
        both = matmul(d_both, hi)
        return both[:LANES] + both[LANES:] + matmul(d_hi, lo)

    lane = lane_of(C)
    at_edge = apply(h_hi[...], h_lo[...])
    resid = []
    for y in range(0, ROWS, 2):
        planes = apply(x_hi[y * M : y * M + SLAB, :], x_lo[y * M : y * M + SLAB, :])
        for k in range(2):
            row = y + k
            total = jnp.zeros((C, LANES), F32)
            for b in range(K):
                d = b - REACH
                own = roll(planes[b * C : (b + 1) * C, k * LANES : (k + 1) * LANES], -d)
                band_edge = at_edge[b * C : (b + 1) * C, :]
                if d > 0:
                    moved = roll(band_edge, 131 - b - 3 * row)
                    own = jnp.where(lane >= LANES - d, moved, own)
                elif d < 0:
                    moved = roll(band_edge, -(64 + 3 * row) - b)
                    own = jnp.where(lane < -d, moved, own)
                total = total + own
            value = norm_scale * total - observed[:, row, :]
            resid.append(value)
            resid_out[row * C : (row + 1) * C, :] = value
            if row < REACH:
                top[row * C : (row + 1) * C, :] = value
            if row >= ROWS - REACH:
                at = (row - ROWS + REACH) * C
                bottom[at : at + C, :] = value

    zero16 = jnp.zeros((C, LANES), F32)
    for b in range(K):
        d = b - REACH
        near = zero16
        for row in range(ROWS):
            moved = roll(resid[row], d)
            if d > 0:
                moved = jnp.where(lane >= d, moved, 0.0)
                here = (lane >= 3 * row) & (lane < 3 * row + d)
                near = jnp.where(here, roll(resid[row], 3 * row - 131 + b), near)
            elif d < 0:
                moved = jnp.where(lane < LANES + d, moved, 0.0)
                here = (lane >= 64 + 3 * row + b) & (lane < 64 + 3 * row + 3)
                near = jnp.where(here, roll(resid[row], 64 + 3 * row + b), near)
            hi, lo = split2(moved)
            r_all[b * C : (b + 1) * C, row * LANES : (row + 1) * LANES] = hi
            r_all[LANES + b * C : LANES + (b + 1) * C, row * LANES : (row + 1) * LANES] = lo
        hi, lo = split2(near)
        r_edge[b * C : (b + 1) * C, :] = hi
        r_edge[LANES + b * C : LANES + (b + 1) * C, :] = lo
    for at in (K * C, LANES + K * C):
        r_all[at : at + C, :] = jnp.zeros((C, ROWS * LANES), BF16)
        r_edge[at : at + C, :] = jnp.zeros((C, LANES), BF16)

    def gather(hi, lo, spread):
        both = matmul_nt(hi, spread)
        return both[:, :LANES] + both[:, LANES:] + matmul_nt(lo, spread[:LANES])

    total = gather(h_hi[:D_ROWS, :], h_lo[:D_ROWS, :], r_edge[...])
    for y in range(0, ROWS, 2):
        total = total + gather(
            x_hi[y * M : y * M + D_ROWS, :],
            x_lo[y * M : y * M + D_ROWS, :],
            r_all[:, y * LANES : (y + 2) * LANES],
        )
    grad[:D_ROWS, :] = total
    grad[D_ROWS:, :] = jnp.zeros((G_ROWS - D_ROWS, LANES), F32)


RECON_OUT = [shape(ROWS * C, LANES), shape(3 * C, LANES), shape(3 * C, LANES), shape(G_ROWS, LANES)]
RECON_SCRATCH = [
    pltpu.VMEM((PAD_ROWS * M, 2 * LANES), BF16),
    pltpu.VMEM((PAD_ROWS * M, 2 * LANES), BF16),
    pltpu.VMEM((SLAB, LANES), BF16),
    pltpu.VMEM((SLAB, LANES), BF16),
    pltpu.VMEM((2 * LANES, ROWS * LANES), BF16),
    pltpu.VMEM((2 * LANES, LANES), BF16),
]


def updated(summed, filt, cons, duals, keep):
    squares = jnp.zeros((M, LANES), F32)
    for a in range(K):
        at = slice(a * M, (a + 1) * M)
        now, dual = filt[at, :], duals[at, :]
        after = now - dict_step * (norm_scale * summed[at, :] + penalty * (now - cons[at, :] + dual))
        joined = after + dual
        squares = squares + joined * joined
        keep(0, a, after)
        keep(1, a, joined)
    spread = jnp.sqrt(jnp.sum(squares, axis=1, keepdims=True) / FLAT)
    return 1.0 / jnp.maximum(1.0, spread)


def first_kernel(maps, above, below, left, right, observed, filt, *rest):
    recon_and_grad(maps, above, below, left, right, observed, filt[...], *rest)


def next_kernel(
    summed, filt, cons, duals, maps, above, below, left, right, observed,
    filt_out, cons_out, duals_out, *rest,
):
    update_into(summed, filt, cons, duals, filt_out, cons_out, duals_out)
    recon_and_grad(maps, above, below, left, right, observed, filt_out[...], *rest)


def update_into(summed, filt, cons, duals, filt_out, cons_out, duals_out):
    refs = (filt_out, cons_out)

    def keep(which, a, value):
        refs[which][a * M : (a + 1) * M, :] = value

    factor = updated(summed, filt, cons, duals, keep)
    for a in range(K):
        at = slice(a * M, (a + 1) * M)
        joined = cons_out[at, :]
        projected = joined * factor
        cons_out[at, :] = projected
        duals_out[at, :] = joined - projected


def last_kernel(summed, filt, cons, duals, filt_out, cons_out, duals_out, new, stacked):
    update_into(summed, filt, cons, duals, new.at[0], new.at[1], new.at[2])
    for i in range(3):
        for a in range(K):
            for j, part in enumerate(split3(new[i, a * M : (a + 1) * M, :])):
                at = (3 * i + j) * M
                stacked[at : at + M, a * LANES : (a + 1) * LANES] = part
    source = lax.broadcasted_iota(jnp.int32, (WIDE, LANES), 0)
    wanted = flat_of(source)
    for block in range(K):
        target = lane_of(WIDE) + block * LANES
        pick = (wanted == target).astype(F32).astype(BF16)
        moved = matmul(stacked[...], pick)
        width = min(LANES, FLAT - block * LANES)
        for i, ref in enumerate((filt_out, cons_out, duals_out)):
            at = 3 * i * M
            value = moved[at : at + M] + moved[at + M : at + 2 * M] + moved[at + 2 * M : at + 3 * M]
            ref[:, block * LANES : block * LANES + width] = value[:, :width]


def corr_kernel(last, resid, above, below, left, right, filt, maps, *rest):
    if last:
        maps_out, s_hi, s_lo = rest
    else:
        maps_out, top, bottom, s_hi, s_lo = rest
    lane = lane_of(C)
    for y in range(PAD_ROWS - 1 + 1):
        own = padded_row(y, C, resid, above, below)
        edge = jnp.where(lane < 3, roll(right[...], -3 * y), roll(left[...], 125 - 3 * y))
        for b in range(K + 1):
            if b < K:
                d = b - REACH
                value = own
                if d > 0:
                    value = jnp.where(lane >= LANES - d, edge, own)
                elif d < 0:
                    value = jnp.where(lane < -d, edge, own)
                hi, lo = split2(roll(value, d))
            else:
                hi = lo = jnp.zeros((C, LANES), BF16)
            for ref, part in ((s_hi, hi), (s_lo, lo)):
                at = y * LANES + b * C
                if y < PAD_ROWS - 1:
                    ref[at : at + C, :LANES] = part
                if y > 0:
                    ref[at - LANES : at - LANES + C, LANES:] = part

    across = jnp.concatenate([filt[(6 - q) * M : (7 - q) * M, :] for q in range(K)], axis=1)
    d_hi, d_lo = split2(across)
    d_both = jnp.concatenate([d_hi, d_lo], axis=0)
    limit = step_coef * sparsity
    for y in range(0, ROWS, 2):
        slab = slice(y * LANES, y * LANES + WIDE)
        both = matmul(d_both, s_hi[slab, :])
        corr = both[:M] + both[M:] + matmul(d_hi, s_lo[slab, :])
        for k in range(2):
            row = y + k
            moved = maps[row * M : (row + 1) * M, :] - (step_coef * norm_scale) * corr[
                :, k * LANES : (k + 1) * LANES
            ]
            value = moved - jnp.clip(moved, -limit, limit)
            if last:
                maps_out[:, row, :] = value
                continue
            maps_out[row * M : (row + 1) * M, :] = value
            if row < REACH:
                top[row * M : (row + 1) * M, :] = value
            if row >= ROWS - REACH:
                at = (row - ROWS + REACH) * M
                bottom[at : at + M, :] = value


CORR_SCRATCH = [pltpu.VMEM(((PAD_ROWS - 1) * LANES, 2 * LANES), BF16)] * 2


def pairs_row(change):
    return [(i, change(i // 2, i % 2)) for i in range(8)]


def pairs_col(change):
    return [(i, change(i // 8, i % 8)) for i in range(32)]


def swap_even(i):
    return i ^ 1


def swap_odd(i, count):
    return (i + 1) % count if i % 2 == 1 else (i - 1) % count


THIRD = {2: 5, 5: 2, 1: 6, 6: 1, 3: 0, 0: 3, 4: 7, 7: 4}
CORE = pairs_row(lambda y, core: y * 2 + 1 - core)
Y_EVEN = pairs_row(lambda y, core: swap_even(y) * 2 + core)
Y_ODD = pairs_row(lambda y, core: swap_odd(y, 4) * 2 + core)
COLS = [
    pairs_col(lambda x, z: swap_even(x) * 8 + z),
    pairs_col(lambda x, z: swap_odd(x, 4) * 8 + z),
    pairs_col(lambda x, z: x * 8 + swap_even(z)),
    pairs_col(lambda x, z: x * 8 + swap_odd(z, 8)),
    pairs_col(lambda x, z: x * 8 + THIRD[z]),
]


def halves(value, bit):
    half = value.shape[0] // 2
    low, high = value[:half], value[half:]
    return jnp.where(bit == 0, high, low), jnp.where(bit == 0, low, high)


def joined(mine, other, bit):
    return jnp.where(
        bit == 0, jnp.concatenate([mine, other]), jnp.concatenate([other, mine])
    )


def sum_all(grad):
    row = lax.axis_index("row")
    y = row // 2
    bits = [(row % 2, CORE), ((y == 1) | (y == 2), Y_EVEN), ((y == 2) | (y == 3), Y_ODD)]
    bits = [(bit.astype(jnp.int32), pairs) for bit, pairs in bits]
    value = grad
    for bit, pairs in bits:
        sent, kept = halves(value, bit)
        value = kept + lax.ppermute(sent, "row", pairs)
    for pairs in COLS:
        value = value + lax.ppermute(value, "col", pairs)
    for bit, pairs in reversed(bits):
        value = joined(value, lax.ppermute(value, "row", pairs), bit)
    return value


def local(observed, coef_maps, dictionary, consensus, dual_vars):
    map_rows = [shape(ROWS * M, LANES), shape(3 * M, LANES), shape(3 * M, LANES)]
    filters = [shape(D_ROWS, LANES)] * 3
    maps, top, bottom = call(rows_kernel, map_rows)(coef_maps)
    filt, cons, duals = call(to_rows_kernel, filters, [pltpu.VMEM((9 * M, WIDE), BF16)])(
        dictionary, consensus, dual_vars
    )
    edges = halos(M, maps, top, bottom)
    resid, r_top, r_bottom, grad = call(first_kernel, RECON_OUT, RECON_SCRATCH)(
        maps, *edges, observed, filt
    )
    summed = sum_all(grad)
    r_edges = halos(C, resid, r_top, r_bottom)
    maps, top, bottom = call(functools.partial(corr_kernel, False), map_rows, CORR_SCRATCH)(
        resid, *r_edges, filt, maps
    )
    edges = halos(M, maps, top, bottom)
    filt, cons, duals, resid, r_top, r_bottom, grad = call(
        next_kernel, filters + RECON_OUT, RECON_SCRATCH
    )(summed, filt, cons, duals, maps, *edges, observed)
    summed = sum_all(grad)
    r_edges = halos(C, resid, r_top, r_bottom)
    new_maps = call(functools.partial(corr_kernel, True), shape(M, ROWS, LANES), CORR_SCRATCH)(
        resid, *r_edges, filt, maps
    )
    new = call(
        last_kernel,
        [shape(M, FLAT)] * 3,
        [pltpu.VMEM((3, D_ROWS, LANES), F32), pltpu.VMEM((9 * M, WIDE), BF16)],
    )(summed, filt, cons, duals)
    return (new_maps, *new)


def solution(mesh):
    return jax.shard_map(
        local,
        mesh=mesh,
        in_specs=(P(None, "row", "col"), P(None, "row", "col"), P(), P(), P()),
        out_specs=(P(None, "row", "col"), P(), P(), P()),
        check_vma=False,
    )
```

time: 1010 us -> 180 us (0.18); the launches traced: 991 us -> 179 us
  waiting for transfers between devices: 496 us -> 68.3 us
  local copies, waits for them, and re-layouts: 263 us -> 1.01 us
  matrix products: 131 us -> 0 us
  starting transfers between devices: 41.6 us -> 91.9 us
  other arithmetic: 38.8 us -> 0.37 us
  between operations: 20.5 us -> 1.12 us
  Pallas kernels: 0 us -> 16.8 us
    psum x2 -> x0, waiting for transfers between devices: 480 us -> none  [local(): summed_grad = lax.psum(local_grad, ('row', 'col'))]
    another operation x109 -> x0, local copies, waits for them, and re-layouts: 186 us -> none  [the longest x107 186 us: corr_and_grad(): stacked = jnp.stack(windows, axis=0)]
    dot_general x96 -> x0, matrix products: 131 us -> none  [the longest x32 64.1 us: recon_tile(): lax.dot_general(weights, flat_maps, (((0,), (0,)), ((), ())), precision=H...]
    ppermute x16 -> x38, waiting for transfers between devices: 16.2 us -> 68.3 us  [the longest x8 26.2 us: neighbours(): lax.ppermute(toward_low, axis, down)]
    ppermute x16 -> x38, starting transfers between devices: 41.5 us -> 91.9 us  [the longest x8 33.8 us: neighbours(): lax.ppermute(toward_high, axis, up)]
    slice x54 -> x0, local copies, waits for them, and re-layouts: 27.8 us -> none  [the longest x48 26.7 us: recon_tile(): planes[row_tap * K + col_tap, row_tap:row_tap + out_rows, col_tap:col_tap...]
    concatenate x4 -> x0, local copies, waits for them, and re-layouts: 24.6 us -> none  [the longest x2 23.9 us: corr_and_grad(): jnp.concatenate(grad_parts, axis=1)]
    add x32 -> x16, other arithmetic: 18.3 us -> 0.18 us  [the longest x6 0.11 us: sum_all(): value = kept + lax.ppermute(sent, 'row', pairs)]
  transfers between devices with their start and end apart: 18 -> 38, of which waited for: 8 -> 29; matrix products, arithmetic and copies ran while one was open for 3% -> 0% of each run, Pallas kernels for 0% -> 4%
where the time goes in v1:
time: 180 us; the launch traced here: 179 us
  starting transfers between devices  91.9 us (51%)
  waiting for transfers between devices  68.3 us (38%)
  Pallas kernels  16.8 us (9%)
    ppermute x8, starting transfers between devices, neighbours(): lax.ppermute(toward_high, axis, up)  33.8 us
    ppermute x8, waiting for transfers between devices, neighbours(): lax.ppermute(toward_low, axis, down)  26.2 us
    ppermute x10, starting transfers between devices, sum_all(): value = value + lax.ppermute(value, 'col', pairs)  25.4 us
    ppermute x10, waiting for transfers between devices, sum_all(): value = value + lax.ppermute(value, 'col', pairs)  19.4 us
    ppermute x8, starting transfers between devices, neighbours(): lax.ppermute(toward_low, axis, down)  13.6 us
    ppermute x6, waiting for transfers between devices, sum_all(): value = kept + lax.ppermute(sent, 'row', pairs)  13 us
    ppermute x6, starting transfers between devices, sum_all(): value = joined(value, lax.ppermute(value, 'row', pairs), bit)  12.5 us
    ppermute x6, waiting for transfers between devices, sum_all(): value = joined(value, lax.ppermute(value, 'row', pairs), bit)  9.39 us
  transfers between devices with their start and end apart: 38, of which 29 were waited for; matrix products, arithmetic and copies ran while one was open for 0% of the time, Pallas kernels for 4%

profile of v1, /device:TPU:1, one launch (start us, length us, event | category | flops | bytes accessed | tf_op | source)
XLA Modules:
  0.0 179.5 jit_solution(1983103534505356087)
XLA Ops:
  0.6 1.0 copy-done
  1.9 4.6 %collective-permute-start = (f32[288,128]{1,0:T(8,128)S(1)}, f32[288,128]{1,0:T(8,128)S(1)}, u32[]{:S(2)}, u32[]{:S(2)}) collective-permute-start(f32[288,128]{1,0:T(8,128)S(1)} %get-tuple-element.36), channel_id=1, source_target_pairs={{0,32},{32,64},{64,96},{96,128},{128,160},{160,192},{192,224},{1,3... | collective-permute-start | bytes 442376 | tf_op jit(solution)/shard_map/ppermute | solution.py:141
  6.5 1.9 %collective-permute-start.1 = (f32[288,128]{1,0:T(8,128)S(1)}, f32[288,128]{1,0:T(8,128)S(1)}, u32[]{:S(2)}, u32[]{:S(2)}) collective-permute-start(f32[288,128]{1,0:T(8,128)S(1)} %get-tuple-element.37), channel_id=1, source_target_pairs={{32,0},{64,32},{96,64},{128,96},{160,128},{192,160},{224,192},{33,... | collective-permute-start | bytes 442376 | tf_op jit(solution)/shard_map/ppermute | solution.py:141
  8.5 4.4 %collective-permute-done.1.below = f32[288,128]{1,0:T(8,128)S(1)} collective-permute-done((f32[288,128]{1,0:T(8,128)S(1)}, f32[288,128]{1,0:T(8,128)S(1)}, u32[]{:S(2)}, u32[]{:S(2)}) %collective-permute-start.1) | collective-permute-done | bytes 147488 | tf_op jit(solution)/shard_map/ppermute | solution.py:141
  13.3 3.5 %collective-permute-start.2 = (f32[96,128]{1,0:T(8,128)S(1)}, f32[96,128]{1,0:T(8,128)S(1)}, u32[]{:S(2)}, u32[]{:S(2)}) collective-permute-start(f32[96,128]{1,0:T(8,128)S(1)} %get-tuple-element.38), channel_id=1, source_target_pairs={{0,1},{1,2},{2,3},{3,4},{4,5},{5,6},{6,7},{7,8},{8,9},{9,10},{10,1... | collective-permute-start | bytes 147464 | tf_op jit(solution)/shard_map/ppermute | solution.py:141
  16.9 1.3 collective-permute-start.3
  18.2 3.0 %shard_map.86 = (f32[672,128]{1,0:T(8,128)S(1)}, f32[672,128]{1,0:T(8,128)S(1)}, f32[672,128]{1,0:T(8,128)S(1)}) custom-call(f32[96,784]{1,0:T(8,128)S(1)} %copy-done.1, f32[96,784]{1,0:T(8,128)S(1)} %copy-done.2, f32[96,784]{1,0:T(8,128)S(1)} %copy-done.3), custom_call_target="tpu_custom_call" | custom-call | tf_op jit(solution)/shard_map/pallas_call | solution.py:436
  21.9 2.5 %shard_map.87 = (f32[128,128]{1,0:T(8,128)S(1)}, f32[48,128]{1,0:T(8,128)S(1)}, f32[48,128]{1,0:T(8,128)S(1)}, f32[704,128]{1,0:T(8,128)S(1)}) custom-call(f32[768,128]{1,0:T(8,128)S(1)} %get-tuple-element.35.own.maps, f32[288,128]{1,0:T(8,128)S(1)} %collective-permute-done.above, f32[288,128]{1,0:T(8,128)S(1)} %collective-permute-done.1.below, ...), custom_call_target="tpu_custom_call" | custom-call | tf_op jit(solution)/shard_map/pallas_call | solution.py:440
  24.6 1.4 collective-permute-done.4
  26.0 1.4 collective-permute-start.5
  27.4 2.8 %collective-permute-done.5 = f32[176,128]{1,0:T(8,128)S(1)} collective-permute-done((f32[176,128]{1,0:T(8,128)S(1)}, f32[176,128]{1,0:T(8,128)S(1)}, u32[]{:S(2)}, u32[]{:S(2)}) %collective-permute-start.5) | collective-permute-done | bytes 90144 | tf_op jit(solution)/shard_map/ppermute | solution.py:424
  30.2 2.1 %collective-permute-start.6 = (f32[88,128]{1,0:T(8,128)S(1)}, f32[88,128]{1,0:T(8,128)S(1)}, u32[]{:S(2)}, u32[]{:S(2)}) collective-permute-start(f32[88,128]{1,0:T(8,128)S(1)} %slice_select_fusion.5), channel_id=1, source_target_pairs={{0,192},{32,224},{64,128},{96,160},{128,64},{160,96},{192,0},{224,... | collective-permute-start | bytes 135176 | tf_op jit(solution)/shard_map/ppermute | solution.py:424
  32.3 2.1 %collective-permute-done.6 = f32[88,128]{1,0:T(8,128)S(1)} collective-permute-done((f32[88,128]{1,0:T(8,128)S(1)}, f32[88,128]{1,0:T(8,128)S(1)}, u32[]{:S(2)}, u32[]{:S(2)}) %collective-permute-start.6) | collective-permute-done | bytes 45088 | tf_op jit(solution)/shard_map/ppermute | solution.py:424
  34.4 5.2 %collective-permute-start.7 = (f32[88,128]{1,0:T(8,128)S(1)}, f32[88,128]{1,0:T(8,128)S(1)}, u32[]{:S(2)}, u32[]{:S(2)}) collective-permute-start(f32[88,128]{1,0:T(8,128)S(1)} %select_add_fusion.5), channel_id=1, source_target_pairs={{0,8},{1,9},{2,10},{3,11},{4,12},{5,13},{6,14},{7,15},{8,0},{9,1},... | collective-permute-start | bytes 135176 | tf_op jit(solution)/shard_map/ppermute | solution.py:426
  39.7 1.4 collective-permute-done.7
  41.1 3.1 %collective-permute-start.8 = (f32[88,128]{1,0:T(8,128)S(1)}, f32[88,128]{1,0:T(8,128)S(1)}, u32[]{:S(2)}, u32[]{:S(2)}) collective-permute-start(f32[88,128]{1,0:T(8,128)S(1)} %add.58), channel_id=1, source_target_pairs={{0,24},{1,25},{2,26},{3,27},{4,28},{5,29},{6,30},{7,31},{8,16},{9,... | collective-permute-start | bytes 135176 | tf_op jit(solution)/shard_map/ppermute | solution.py:426
  44.2 1.4 collective-permute-done.8
  45.7 3.2 %collective-permute-done.9 = f32[88,128]{1,0:T(8,128)S(1)} collective-permute-done((f32[88,128]{1,0:T(8,128)S(1)}, f32[88,128]{1,0:T(8,128)S(1)}, u32[]{:S(2)}, u32[]{:S(2)}) %collective-permute-start.9) | collective-permute-done | bytes 45088 | tf_op jit(solution)/shard_map/ppermute | solution.py:426
  48.9 1.6 collective-permute-start.10
  50.6 2.5 %collective-permute-done.10 = f32[88,128]{1,0:T(8,128)S(1)} collective-permute-done((f32[88,128]{1,0:T(8,128)S(1)}, f32[88,128]{1,0:T(8,128)S(1)}, u32[]{:S(2)}, u32[]{:S(2)}) %collective-permute-start.10) | collective-permute-done | bytes 45088 | tf_op jit(solution)/shard_map/ppermute | solution.py:426
  53.1 2.3 %collective-permute-start.11 = (f32[88,128]{1,0:T(8,128)S(1)}, f32[88,128]{1,0:T(8,128)S(1)}, u32[]{:S(2)}, u32[]{:S(2)}) collective-permute-start(f32[88,128]{1,0:T(8,128)S(1)} %add.61), channel_id=1, source_target_pairs={{0,3},{1,6},{2,5},{3,0},{4,7},{5,2},{6,1},{7,4},{8,11},{9,14},{10,... | collective-permute-start | bytes 135176 | tf_op jit(solution)/shard_map/ppermute | solution.py:426
  55.5 2.4 %collective-permute-done.11 = f32[88,128]{1,0:T(8,128)S(1)} collective-permute-done((f32[88,128]{1,0:T(8,128)S(1)}, f32[88,128]{1,0:T(8,128)S(1)}, u32[]{:S(2)}, u32[]{:S(2)}) %collective-permute-start.11) | collective-permute-done | bytes 45088 | tf_op jit(solution)/shard_map/ppermute | solution.py:426
  57.9 1.4 collective-permute-start.12
  59.4 2.7 %collective-permute-done.12 = f32[88,128]{1,0:T(8,128)S(1)} collective-permute-done((f32[88,128]{1,0:T(8,128)S(1)}, f32[88,128]{1,0:T(8,128)S(1)}, u32[]{:S(2)}, u32[]{:S(2)}) %collective-permute-start.12) | collective-permute-done | bytes 45088 | tf_op jit(solution)/shard_map/ppermute | solution.py:428
  62.2 11.9 %collective-permute-start.15 = (f32[48,128]{1,0:T(8,128)S(1)}, f32[48,128]{1,0:T(8,128)S(1)}, u32[]{:S(2)}, u32[]{:S(2)}) collective-permute-start(f32[48,128]{1,0:T(8,128)S(1)} %get-tuple-element.45), channel_id=1, source_target_pairs={{0,32},{32,64},{64,96},{96,128},{128,160},{160,192},{192,224},{1,3... | collective-permute-start | bytes 73736 | tf_op jit(solution)/shard_map/ppermute | solution.py:141
  74.2 1.9 %collective-permute-start.16 = (f32[48,128]{1,0:T(8,128)S(1)}, f32[48,128]{1,0:T(8,128)S(1)}, u32[]{:S(2)}, u32[]{:S(2)}) collective-permute-start(f32[48,128]{1,0:T(8,128)S(1)} %get-tuple-element.46), channel_id=1, source_target_pairs={{32,0},{64,32},{96,64},{128,96},{160,128},{192,160},{224,192},{33,... | collective-permute-start | bytes 73736 | tf_op jit(solution)/shard_map/ppermute | solution.py:141
  76.4 2.9 %collective-permute-done.16.below = f32[48,128]{1,0:T(8,128)S(1)} collective-permute-done((f32[48,128]{1,0:T(8,128)S(1)}, f32[48,128]{1,0:T(8,128)S(1)}, u32[]{:S(2)}, u32[]{:S(2)}) %collective-permute-start.16) | collective-permute-done | bytes 24608 | tf_op jit(solution)/shard_map/ppermute | solution.py:141
  79.4 1.8 %collective-permute-start.17 = (f32[16,128]{1,0:T(8,128)S(1)}, f32[16,128]{1,0:T(8,128)S(1)}, u32[]{:S(2)}, u32[]{:S(2)}) collective-permute-start(f32[16,128]{1,0:T(8,128)S(1)} %get-tuple-element.47), channel_id=1, source_target_pairs={{0,1},{1,2},{2,3},{3,4},{4,5},{5,6},{6,7},{7,8},{8,9},{9,10},{10,1... | collective-permute-start | bytes 24584 | tf_op jit(solution)/shard_map/ppermute | solution.py:141
  81.3 1.3 collective-permute-start.18
  82.6 3.4 %collective-permute-done.18.right = f32[16,128]{1,0:T(8,128)S(1)} collective-permute-done((f32[16,128]{1,0:T(8,128)S(1)}, f32[16,128]{1,0:T(8,128)S(1)}, u32[]{:S(2)}, u32[]{:S(2)}) %collective-permute-start.18) | collective-permute-done | bytes 8224 | tf_op jit(solution)/shard_map/ppermute | solution.py:141
  85.9 1.2 shard_map.89
  87.1 3.1 %collective-permute-start.19 = (f32[288,128]{1,0:T(8,128)S(1)}, f32[288,128]{1,0:T(8,128)S(1)}, u32[]{:S(2)}, u32[]{:S(2)}) collective-permute-start(f32[288,128]{1,0:T(8,128)S(1)} %get-tuple-element.50), channel_id=1, source_target_pairs={{0,32},{32,64},{64,96},{96,128},{128,160},{160,192},{192,224},{1,3... | collective-permute-start | bytes 442376 | tf_op jit(solution)/shard_map/ppermute | solution.py:141
  90.2 1.9 %collective-permute-start.20 = (f32[288,128]{1,0:T(8,128)S(1)}, f32[288,128]{1,0:T(8,128)S(1)}, u32[]{:S(2)}, u32[]{:S(2)}) collective-permute-start(f32[288,128]{1,0:T(8,128)S(1)} %get-tuple-element.51), channel_id=1, source_target_pairs={{32,0},{64,32},{96,64},{128,96},{160,128},{192,160},{224,192},{33,... | collective-permute-start | bytes 442376 | tf_op jit(solution)/shard_map/ppermute | solution.py:141
  92.3 4.4 %collective-permute-done.20.below = f32[288,128]{1,0:T(8,128)S(1)} collective-permute-done((f32[288,128]{1,0:T(8,128)S(1)}, f32[288,128]{1,0:T(8,128)S(1)}, u32[]{:S(2)}, u32[]{:S(2)}) %collective-permute-start.20) | collective-permute-done | bytes 147488 | tf_op jit(solution)/shard_map/ppermute | solution.py:141
  97.1 3.6 %collective-permute-start.21 = (f32[96,128]{1,0:T(8,128)S(1)}, f32[96,128]{1,0:T(8,128)S(1)}, u32[]{:S(2)}, u32[]{:S(2)}) collective-permute-start(f32[96,128]{1,0:T(8,128)S(1)} %get-tuple-element.52), channel_id=1, source_target_pairs={{0,1},{1,2},{2,3},{3,4},{4,5},{5,6},{6,7},{7,8},{8,9},{9,10},{10,1... | collective-permute-start | bytes 147464 | tf_op jit(solution)/shard_map/ppermute | solution.py:141
  100.7 1.3 collective-permute-start.22
  102.1 4.2 %collective-permute-done.22.right = f32[96,128]{1,0:T(8,128)S(1)} collective-permute-done((f32[96,128]{1,0:T(8,128)S(1)}, f32[96,128]{1,0:T(8,128)S(1)}, u32[]{:S(2)}, u32[]{:S(2)}) %collective-permute-start.22) | collective-permute-done | bytes 49184 | tf_op jit(solution)/shard_map/ppermute | solution.py:141
  106.3 2.6 %shard_map.91 = (f32[672,128]{1,0:T(8,128)S(1)}, f32[672,128]{1,0:T(8,128)S(1)}, f32[672,128]{1,0:T(8,128)S(1)}, f32[128,128]{1,0:T(8,128)S(1)}, f32[48,128]{1,0...) custom-call(f32[704,128]{1,0:T(8,128)S(1)} %maximum_select_fusion.summed, ...), custom_call_target="tpu_custom_call" | custom-call | tf_op jit(solution)/shard_map/pallas_call | solution.py:449
  109.0 1.4 collective-permute-done.27
  110.4 1.5 collective-permute-start.28
  112.0 2.6 %collective-permute-done.28 = f32[176,128]{1,0:T(8,128)S(1)} collective-permute-done((f32[176,128]{1,0:T(8,128)S(1)}, f32[176,128]{1,0:T(8,128)S(1)}, u32[]{:S(2)}, u32[]{:S(2)}) %collective-permute-start.28) | collective-permute-done | bytes 90144 | tf_op jit(solution)/shard_map/ppermute | solution.py:424
  114.6 1.5 collective-permute-start.29
  116.1 2.7 %collective-permute-done.29 = f32[88,128]{1,0:T(8,128)S(1)} collective-permute-done((f32[88,128]{1,0:T(8,128)S(1)}, f32[88,128]{1,0:T(8,128)S(1)}, u32[]{:S(2)}, u32[]{:S(2)}) %collective-permute-start.29) | collective-permute-done | bytes 45088 | tf_op jit(solution)/shard_map/ppermute | solution.py:424
  118.8 1.9 %collective-permute-start.30 = (f32[88,128]{1,0:T(8,128)S(1)}, f32[88,128]{1,0:T(8,128)S(1)}, u32[]{:S(2)}, u32[]{:S(2)}) collective-permute-start(f32[88,128]{1,0:T(8,128)S(1)} %select_add_fusion.4), channel_id=1, source_target_pairs={{0,8},{1,9},{2,10},{3,11},{4,12},{5,13},{6,14},{7,15},{8,0},{9,1},... | collective-permute-start | bytes 135176 | tf_op jit(solution)/shard_map/ppermute | solution.py:426
  120.7 1.4 collective-permute-done.30
  122.1 4.4 %collective-permute-start.31 = (f32[88,128]{1,0:T(8,128)S(1)}, f32[88,128]{1,0:T(8,128)S(1)}, u32[]{:S(2)}, u32[]{:S(2)}) collective-permute-start(f32[88,128]{1,0:T(8,128)S(1)} %add.66), channel_id=1, source_target_pairs={{0,24},{1,25},{2,26},{3,27},{4,28},{5,29},{6,30},{7,31},{8,16},{9,... | collective-permute-start | bytes 135176 | tf_op jit(solution)/shard_map/ppermute | solution.py:426
  126.5 1.4 collective-permute-done.31
  128.0 1.1 collective-permute-start.32
  129.1 2.2 %collective-permute-done.32 = f32[88,128]{1,0:T(8,128)S(1)} collective-permute-done((f32[88,128]{1,0:T(8,128)S(1)}, f32[88,128]{1,0:T(8,128)S(1)}, u32[]{:S(2)}, u32[]{:S(2)}) %collective-permute-start.32) | collective-permute-done | bytes 45088 | tf_op jit(solution)/shard_map/ppermute | solution.py:426
  131.2 2.8 %collective-permute-start.33 = (f32[88,128]{1,0:T(8,128)S(1)}, f32[88,128]{1,0:T(8,128)S(1)}, u32[]{:S(2)}, u32[]{:S(2)}) collective-permute-start(f32[88,128]{1,0:T(8,128)S(1)} %add.68), channel_id=1, source_target_pairs={{0,7},{1,2},{2,1},{3,4},{4,3},{5,6},{6,5},{7,0},{8,15},{9,10},{10,... | collective-permute-start | bytes 135176 | tf_op jit(solution)/shard_map/ppermute | solution.py:426
  134.0 1.4 collective-permute-done.33
  135.5 2.9 %collective-permute-start.34 = (f32[88,128]{1,0:T(8,128)S(1)}, f32[88,128]{1,0:T(8,128)S(1)}, u32[]{:S(2)}, u32[]{:S(2)}) collective-permute-start(f32[88,128]{1,0:T(8,128)S(1)} %add.69), channel_id=1, source_target_pairs={{0,3},{1,6},{2,5},{3,0},{4,7},{5,2},{6,1},{7,4},{8,11},{9,14},{10,... | collective-permute-start | bytes 135176 | tf_op jit(solution)/shard_map/ppermute | solution.py:426
  138.3 1.9 %collective-permute-done.34 = f32[88,128]{1,0:T(8,128)S(1)} collective-permute-done((f32[88,128]{1,0:T(8,128)S(1)}, f32[88,128]{1,0:T(8,128)S(1)}, u32[]{:S(2)}, u32[]{:S(2)}) %collective-permute-start.34) | collective-permute-done | bytes 45088 | tf_op jit(solution)/shard_map/ppermute | solution.py:426
  141.1 3.3 %collective-permute-done.35 = f32[88,128]{1,0:T(8,128)S(1)} collective-permute-done((f32[88,128]{1,0:T(8,128)S(1)}, f32[88,128]{1,0:T(8,128)S(1)}, u32[]{:S(2)}, u32[]{:S(2)}) %collective-permute-start.35) | collective-permute-done | bytes 45088 | tf_op jit(solution)/shard_map/ppermute | solution.py:428
  144.5 3.4 %collective-permute-done.36 = f32[176,128]{1,0:T(8,128)S(1)} collective-permute-done((f32[176,128]{1,0:T(8,128)S(1)}, f32[176,128]{1,0:T(8,128)S(1)}, u32[]{:S(2)}, u32[]{:S(2)}) %collective-permute-start.36) | collective-permute-done | bytes 90144 | tf_op jit(solution)/shard_map/ppermute | solution.py:428
  147.9 9.6 %collective-permute-start.37 = (f32[352,128]{1,0:T(8,128)S(1)}, f32[352,128]{1,0:T(8,128)S(1)}, u32[]{:S(2)}, u32[]{:S(2)}) collective-permute-start(f32[352,128]{1,0:T(8,128)S(1)} %maximum_select_fusion.3), channel_id=1, source_target_pairs={{0,32},{32,0},{64,96},{96,64},{128,160},{160,128},{192,224},{224,1... | collective-permute-start | bytes 540680 | tf_op jit(solution)/shard_map/ppermute | solution.py:428
  157.6 1.9 %collective-permute-start.23 = (f32[48,128]{1,0:T(8,128)S(1)}, f32[48,128]{1,0:T(8,128)S(1)}, u32[]{:S(2)}, u32[]{:S(2)}) collective-permute-start(f32[48,128]{1,0:T(8,128)S(1)} %get-tuple-element.55), channel_id=1, source_target_pairs={{0,32},{32,64},{64,96},{96,128},{128,160},{160,192},{192,224},{1,3... | collective-permute-start | bytes 73736 | tf_op jit(solution)/shard_map/ppermute | solution.py:141
  159.5 2.4 %collective-permute-start.24 = (f32[48,128]{1,0:T(8,128)S(1)}, f32[48,128]{1,0:T(8,128)S(1)}, u32[]{:S(2)}, u32[]{:S(2)}) collective-permute-start(f32[48,128]{1,0:T(8,128)S(1)} %get-tuple-element.56), channel_id=1, source_target_pairs={{32,0},{64,32},{96,64},{128,96},{160,128},{192,160},{224,192},{33,... | collective-permute-start | bytes 73736 | tf_op jit(solution)/shard_map/ppermute | solution.py:141
  161.9 2.7 %collective-permute-done.24.below = f32[48,128]{1,0:T(8,128)S(1)} collective-permute-done((f32[48,128]{1,0:T(8,128)S(1)}, f32[48,128]{1,0:T(8,128)S(1)}, u32[]{:S(2)}, u32[]{:S(2)}) %collective-permute-start.24) | collective-permute-done | bytes 24608 | tf_op jit(solution)/shard_map/ppermute | solution.py:141
  164.8 3.3 %collective-permute-start.25 = (f32[16,128]{1,0:T(8,128)S(1)}, f32[16,128]{1,0:T(8,128)S(1)}, u32[]{:S(2)}, u32[]{:S(2)}) collective-permute-start(f32[16,128]{1,0:T(8,128)S(1)} %get-tuple-element.57), channel_id=1, source_target_pairs={{0,1},{1,2},{2,3},{3,4},{4,5},{5,6},{6,7},{7,8},{8,9},{9,10},{10,1... | collective-permute-start | bytes 24584 | tf_op jit(solution)/shard_map/ppermute | solution.py:141
  168.0 1.5 collective-permute-start.26
  169.6 3.7 %collective-permute-done.26.right = f32[16,128]{1,0:T(8,128)S(1)} collective-permute-done((f32[16,128]{1,0:T(8,128)S(1)}, f32[16,128]{1,0:T(8,128)S(1)}, u32[]{:S(2)}, u32[]{:S(2)}) %collective-permute-start.26) | collective-permute-done | bytes 8224 | tf_op jit(solution)/shard_map/ppermute | solution.py:141
  173.2 2.0 %shard_map.93 = f32[96,8,128]{2,1,0:T(8,128)} custom-call(f32[128,128]{1,0:T(8,128)S(1)} %get-tuple-element.54.own.resid, f32[48,128]{1,0:T(8,128)S(1)} %collective-permute-done.23.above, f32[48,128]{1,0:T(8,128)S(1)} %collective-permute-done.24.below, f32[16,128]{1,0:T(8,128)S(1)} %collective-permute-done.25.left, ...), custom_call_target="tpu_custom_call" | custom-call | tf_op jit(solution)/shard_map/pallas_call | solution.py:454
  175.3 4.2 %shard_map.94 = (f32[96,784]{1,0:T(8,128)}, f32[96,784]{1,0:T(8,128)}, f32[96,784]{1,0:T(8,128)}) custom-call(f32[704,128]{1,0:T(8,128)S(1)} %maximum_select_fusion.1.summed, f32[672,128]{1,0:T(8,128)S(1)} %get-tuple-element.59.filt, f32[672,128]{1,0:T(8,128)S(1)} %get-tuple-element.61.cons, f32[672,128]{1,0:T(8,128)S(1)} %get-tuple-element.62.duals), custom_call_target="tpu_custom_call" | custom-call | tf_op jit(solution)/shard_map/pallas_call | solution.py:457
  (61 shorter events, 4.3 us)
Async XLA Ops:
  0.6 1.0 copy-start
  1.6 16.6 %copy-start.3 = (f32[96,784]{1,0:T(8,128)S(1)}, f32[96,784]{1,0:T(8,128)}, u32[]{:S(2)}) copy-start(f32[96,784]{1,0:T(8,128)} %duals.1) | copy-start | bytes 903172
  1.9 6.7 %collective-permute-start = (f32[288,128]{1,0:T(8,128)S(1)}, f32[288,128]{1,0:T(8,128)S(1)}, u32[]{:S(2)}, u32[]{:S(2)}) collective-permute-start(f32[288,128]{1,0:T(8,128)S(1)} %get-tuple-element.36), channel_id=1, source_target_pairs={{0,32},{32,64},{64,96},{96,128},{128,160},{160,192},{192,224},{1,3... | collective-permute-start | bytes 442376 | tf_op jit(solution)/shard_map/ppermute | solution.py:141
  6.5 6.5 %collective-permute-start.1 = (f32[288,128]{1,0:T(8,128)S(1)}, f32[288,128]{1,0:T(8,128)S(1)}, u32[]{:S(2)}, u32[]{:S(2)}) collective-permute-start(f32[288,128]{1,0:T(8,128)S(1)} %get-tuple-element.37), channel_id=1, source_target_pairs={{32,0},{64,32},{96,64},{128,96},{160,128},{192,160},{224,192},{33,... | collective-permute-start | bytes 442376 | tf_op jit(solution)/shard_map/ppermute | solution.py:141
  12.9 5.3 %copy-start.1 = (f32[96,784]{1,0:T(8,128)S(1)}, f32[96,784]{1,0:T(8,128)}, u32[]{:S(2)}) copy-start(f32[96,784]{1,0:T(8,128)} %filt.1) | copy-start | bytes 903172
  12.9 5.3 %copy-start.2 = (f32[96,784]{1,0:T(8,128)S(1)}, f32[96,784]{1,0:T(8,128)}, u32[]{:S(2)}) copy-start(f32[96,784]{1,0:T(8,128)} %cons.1) | copy-start | bytes 903172
  13.3 7.9 %collective-permute-start.2 = (f32[96,128]{1,0:T(8,128)S(1)}, f32[96,128]{1,0:T(8,128)S(1)}, u32[]{:S(2)}, u32[]{:S(2)}) collective-permute-start(f32[96,128]{1,0:T(8,128)S(1)} %get-tuple-element.38), channel_id=1, source_target_pairs={{0,1},{1,2},{2,3},{3,4},{4,5},{5,6},{6,7},{7,8},{8,9},{9,10},{10,1... | collective-permute-start | bytes 147464 | tf_op jit(solution)/shard_map/ppermute | solution.py:141
  16.9 5.0 %collective-permute-start.3 = (f32[96,128]{1,0:T(8,128)S(1)}, f32[96,128]{1,0:T(8,128)S(1)}, u32[]{:S(2)}, u32[]{:S(2)}) collective-permute-start(f32[96,128]{1,0:T(8,128)S(1)} %get-tuple-element.39), channel_id=1, source_target_pairs={{1,0},{2,1},{3,2},{4,3},{5,4},{6,5},{7,6},{8,7},{9,8},{10,9},{11,1... | collective-permute-start | bytes 147464 | tf_op jit(solution)/shard_map/ppermute | solution.py:141
  18.2 3.7 %copy-start.4 = (f32[16,8,128]{2,1,0:T(8,128)S(1)}, f32[16,8,128]{2,1,0:T(8,128)}, u32[]{:S(2)}) copy-start(f32[16,8,128]{2,1,0:T(8,128)} %observed.3) | copy-start | bytes 196612
  24.5 1.5 collective-permute-start.4
  26.0 4.2 %collective-permute-start.5 = (f32[176,128]{1,0:T(8,128)S(1)}, f32[176,128]{1,0:T(8,128)S(1)}, u32[]{:S(2)}, u32[]{:S(2)}) collective-permute-start(f32[176,128]{1,0:T(8,128)S(1)} %slice_select_fusion.3), channel_id=1, source_target_pairs={{0,64},{32,96},{64,0},{96,32},{128,192},{160,224},{192,128},{224,1... | collective-permute-start | bytes 270344 | tf_op jit(solution)/shard_map/ppermute | solution.py:424
  30.2 4.2 %collective-permute-start.6 = (f32[88,128]{1,0:T(8,128)S(1)}, f32[88,128]{1,0:T(8,128)S(1)}, u32[]{:S(2)}, u32[]{:S(2)}) collective-permute-start(f32[88,128]{1,0:T(8,128)S(1)} %slice_select_fusion.5), channel_id=1, source_target_pairs={{0,192},{32,224},{64,128},{96,160},{128,64},{160,96},{192,0},{224,... | collective-permute-start | bytes 135176 | tf_op jit(solution)/shard_map/ppermute | solution.py:424
  34.4 6.7 %collective-permute-start.7 = (f32[88,128]{1,0:T(8,128)S(1)}, f32[88,128]{1,0:T(8,128)S(1)}, u32[]{:S(2)}, u32[]{:S(2)}) collective-permute-start(f32[88,128]{1,0:T(8,128)S(1)} %select_add_fusion.5), channel_id=1, source_target_pairs={{0,8},{1,9},{2,10},{3,11},{4,12},{5,13},{6,14},{7,15},{8,0},{9,1},... | collective-permute-start | bytes 135176 | tf_op jit(solution)/shard_map/ppermute | solution.py:426
  41.1 4.5 %collective-permute-start.8 = (f32[88,128]{1,0:T(8,128)S(1)}, f32[88,128]{1,0:T(8,128)S(1)}, u32[]{:S(2)}, u32[]{:S(2)}) collective-permute-start(f32[88,128]{1,0:T(8,128)S(1)} %add.58), channel_id=1, source_target_pairs={{0,24},{1,25},{2,26},{3,27},{4,28},{5,29},{6,30},{7,31},{8,16},{9,... | collective-permute-start | bytes 135176 | tf_op jit(solution)/shard_map/ppermute | solution.py:426
  45.6 3.3 %collective-permute-start.9 = (f32[88,128]{1,0:T(8,128)S(1)}, f32[88,128]{1,0:T(8,128)S(1)}, u32[]{:S(2)}, u32[]{:S(2)}) collective-permute-start(f32[88,128]{1,0:T(8,128)S(1)} %add.59), channel_id=1, source_target_pairs={{0,1},{1,0},{2,3},{3,2},{4,5},{5,4},{6,7},{7,6},{8,9},{9,8},{10,11... | collective-permute-start | bytes 135176 | tf_op jit(solution)/shard_map/ppermute | solution.py:426
  48.9 4.2 %collective-permute-start.10 = (f32[88,128]{1,0:T(8,128)S(1)}, f32[88,128]{1,0:T(8,128)S(1)}, u32[]{:S(2)}, u32[]{:S(2)}) collective-permute-start(f32[88,128]{1,0:T(8,128)S(1)} %add.60), channel_id=1, source_target_pairs={{0,7},{1,2},{2,1},{3,4},{4,3},{5,6},{6,5},{7,0},{8,15},{9,10},{10,... | collective-permute-start | bytes 135176 | tf_op jit(solution)/shard_map/ppermute | solution.py:426
  53.1 4.8 %collective-permute-start.11 = (f32[88,128]{1,0:T(8,128)S(1)}, f32[88,128]{1,0:T(8,128)S(1)}, u32[]{:S(2)}, u32[]{:S(2)}) collective-permute-start(f32[88,128]{1,0:T(8,128)S(1)} %add.61), channel_id=1, source_target_pairs={{0,3},{1,6},{2,5},{3,0},{4,7},{5,2},{6,1},{7,4},{8,11},{9,14},{10,... | collective-permute-start | bytes 135176 | tf_op jit(solution)/shard_map/ppermute | solution.py:426
  57.9 4.2 %collective-permute-start.12 = (f32[88,128]{1,0:T(8,128)S(1)}, f32[88,128]{1,0:T(8,128)S(1)}, u32[]{:S(2)}, u32[]{:S(2)}) collective-permute-start(f32[88,128]{1,0:T(8,128)S(1)} %add.62), channel_id=1, source_target_pairs={{0,192},{32,224},{64,128},{96,160},{128,64},{160,96},{192,0},{224,... | collective-permute-start | bytes 135176 | tf_op jit(solution)/shard_map/ppermute | solution.py:428
  62.1 14.0 %collective-permute-start.13 = (f32[176,128]{1,0:T(8,128)S(1)}, f32[176,128]{1,0:T(8,128)S(1)}, u32[]{:S(2)}, u32[]{:S(2)}) collective-permute-start(f32[176,128]{1,0:T(8,128)S(1)} %maximum_select_fusion.4), channel_id=1, source_target_pairs={{0,64},{32,96},{64,0},{96,32},{128,192},{160,224},{192,128},{224,1... | collective-permute-start | bytes 270344 | tf_op jit(solution)/shard_map/ppermute | solution.py:428
  62.2 14.2 %collective-permute-start.15 = (f32[48,128]{1,0:T(8,128)S(1)}, f32[48,128]{1,0:T(8,128)S(1)}, u32[]{:S(2)}, u32[]{:S(2)}) collective-permute-start(f32[48,128]{1,0:T(8,128)S(1)} %get-tuple-element.45), channel_id=1, source_target_pairs={{0,32},{32,64},{64,96},{96,128},{128,160},{160,192},{192,224},{1,3... | collective-permute-start | bytes 73736 | tf_op jit(solution)/shard_map/ppermute | solution.py:141
  74.2 5.1 %collective-permute-start.16 = (f32[48,128]{1,0:T(8,128)S(1)}, f32[48,128]{1,0:T(8,128)S(1)}, u32[]{:S(2)}, u32[]{:S(2)}) collective-permute-start(f32[48,128]{1,0:T(8,128)S(1)} %get-tuple-element.46), channel_id=1, source_target_pairs={{32,0},{64,32},{96,64},{128,96},{160,128},{192,160},{224,192},{33,... | collective-permute-start | bytes 73736 | tf_op jit(solution)/shard_map/ppermute | solution.py:141
  76.1 25.9 %collective-permute-start.14 = (f32[352,128]{1,0:T(8,128)S(1)}, f32[352,128]{1,0:T(8,128)S(1)}, u32[]{:S(2)}, u32[]{:S(2)}) collective-permute-start(f32[352,128]{1,0:T(8,128)S(1)} %maximum_select_fusion.2), channel_id=1, source_target_pairs={{0,32},{32,0},{64,96},{96,64},{128,160},{160,128},{192,224},{224,1... | collective-permute-start | bytes 540680 | tf_op jit(solution)/shard_map/ppermute | solution.py:428
  79.4 3.1 %collective-permute-start.17 = (f32[16,128]{1,0:T(8,128)S(1)}, f32[16,128]{1,0:T(8,128)S(1)}, u32[]{:S(2)}, u32[]{:S(2)}) collective-permute-start(f32[16,128]{1,0:T(8,128)S(1)} %get-tuple-element.47), channel_id=1, source_target_pairs={{0,1},{1,2},{2,3},{3,4},{4,5},{5,6},{6,7},{7,8},{8,9},{9,10},{10,1... | collective-permute-start | bytes 24584 | tf_op jit(solution)/shard_map/ppermute | solution.py:141
  81.3 4.7 %collective-permute-start.18 = (f32[16,128]{1,0:T(8,128)S(1)}, f32[16,128]{1,0:T(8,128)S(1)}, u32[]{:S(2)}, u32[]{:S(2)}) collective-permute-start(f32[16,128]{1,0:T(8,128)S(1)} %get-tuple-element.48), channel_id=1, source_target_pairs={{1,0},{2,1},{3,2},{4,3},{5,4},{6,5},{7,6},{8,7},{9,8},{10,9},{11,1... | collective-permute-start | bytes 24584 | tf_op jit(solution)/shard_map/ppermute | solution.py:141
  87.1 5.2 %collective-permute-start.19 = (f32[288,128]{1,0:T(8,128)S(1)}, f32[288,128]{1,0:T(8,128)S(1)}, u32[]{:S(2)}, u32[]{:S(2)}) collective-permute-start(f32[288,128]{1,0:T(8,128)S(1)} %get-tuple-element.50), channel_id=1, source_target_pairs={{0,32},{32,64},{64,96},{96,128},{128,160},{160,192},{192,224},{1,3... | collective-permute-start | bytes 442376 | tf_op jit(solution)/shard_map/ppermute | solution.py:141
  90.2 6.5 %collective-permute-start.20 = (f32[288,128]{1,0:T(8,128)S(1)}, f32[288,128]{1,0:T(8,128)S(1)}, u32[]{:S(2)}, u32[]{:S(2)}) collective-permute-start(f32[288,128]{1,0:T(8,128)S(1)} %get-tuple-element.51), channel_id=1, source_target_pairs={{32,0},{64,32},{96,64},{128,96},{160,128},{192,160},{224,192},{33,... | collective-permute-start | bytes 442376 | tf_op jit(solution)/shard_map/ppermute | solution.py:141
  97.1 5.0 %collective-permute-start.21 = (f32[96,128]{1,0:T(8,128)S(1)}, f32[96,128]{1,0:T(8,128)S(1)}, u32[]{:S(2)}, u32[]{:S(2)}) collective-permute-start(f32[96,128]{1,0:T(8,128)S(1)} %get-tuple-element.52), channel_id=1, source_target_pairs={{0,1},{1,2},{2,3},{3,4},{4,5},{5,6},{6,7},{7,8},{8,9},{9,10},{10,1... | collective-permute-start | bytes 147464 | tf_op jit(solution)/shard_map/ppermute | solution.py:141
  100.7 5.5 %collective-permute-start.22 = (f32[96,128]{1,0:T(8,128)S(1)}, f32[96,128]{1,0:T(8,128)S(1)}, u32[]{:S(2)}, u32[]{:S(2)}) collective-permute-start(f32[96,128]{1,0:T(8,128)S(1)} %get-tuple-element.53), channel_id=1, source_target_pairs={{1,0},{2,1},{3,2},{4,3},{5,4},{6,5},{7,6},{8,7},{9,8},{10,9},{11,1... | collective-permute-start | bytes 147464 | tf_op jit(solution)/shard_map/ppermute | solution.py:141
  108.9 1.5 collective-permute-start.27
  110.4 4.2 %collective-permute-start.28 = (f32[176,128]{1,0:T(8,128)S(1)}, f32[176,128]{1,0:T(8,128)S(1)}, u32[]{:S(2)}, u32[]{:S(2)}) collective-permute-start(f32[176,128]{1,0:T(8,128)S(1)} %slice_select_fusion.2), channel_id=1, source_target_pairs={{0,64},{32,96},{64,0},{96,32},{128,192},{160,224},{192,128},{224,1... | collective-permute-start | bytes 270344 | tf_op jit(solution)/shard_map/ppermute | solution.py:424
  114.6 4.2 %collective-permute-start.29 = (f32[88,128]{1,0:T(8,128)S(1)}, f32[88,128]{1,0:T(8,128)S(1)}, u32[]{:S(2)}, u32[]{:S(2)}) collective-permute-start(f32[88,128]{1,0:T(8,128)S(1)} %slice_select_fusion.4), channel_id=1, source_target_pairs={{0,192},{32,224},{64,128},{96,160},{128,64},{160,96},{192,0},{224,... | collective-permute-start | bytes 135176 | tf_op jit(solution)/shard_map/ppermute | solution.py:424
  118.8 3.3 %collective-permute-start.30 = (f32[88,128]{1,0:T(8,128)S(1)}, f32[88,128]{1,0:T(8,128)S(1)}, u32[]{:S(2)}, u32[]{:S(2)}) collective-permute-start(f32[88,128]{1,0:T(8,128)S(1)} %select_add_fusion.4), channel_id=1, source_target_pairs={{0,8},{1,9},{2,10},{3,11},{4,12},{5,13},{6,14},{7,15},{8,0},{9,1},... | collective-permute-start | bytes 135176 | tf_op jit(solution)/shard_map/ppermute | solution.py:426
  122.1 5.8 %collective-permute-start.31 = (f32[88,128]{1,0:T(8,128)S(1)}, f32[88,128]{1,0:T(8,128)S(1)}, u32[]{:S(2)}, u32[]{:S(2)}) collective-permute-start(f32[88,128]{1,0:T(8,128)S(1)} %add.66), channel_id=1, source_target_pairs={{0,24},{1,25},{2,26},{3,27},{4,28},{5,29},{6,30},{7,31},{8,16},{9,... | collective-permute-start | bytes 135176 | tf_op jit(solution)/shard_map/ppermute | solution.py:426
  128.0 3.3 %collective-permute-start.32 = (f32[88,128]{1,0:T(8,128)S(1)}, f32[88,128]{1,0:T(8,128)S(1)}, u32[]{:S(2)}, u32[]{:S(2)}) collective-permute-start(f32[88,128]{1,0:T(8,128)S(1)} %add.67), channel_id=1, source_target_pairs={{0,1},{1,0},{2,3},{3,2},{4,5},{5,4},{6,7},{7,6},{8,9},{9,8},{10,11... | collective-permute-start | bytes 135176 | tf_op jit(solution)/shard_map/ppermute | solution.py:426
  131.2 4.2 %collective-permute-start.33 = (f32[88,128]{1,0:T(8,128)S(1)}, f32[88,128]{1,0:T(8,128)S(1)}, u32[]{:S(2)}, u32[]{:S(2)}) collective-permute-start(f32[88,128]{1,0:T(8,128)S(1)} %add.68), channel_id=1, source_target_pairs={{0,7},{1,2},{2,1},{3,4},{4,3},{5,6},{6,5},{7,0},{8,15},{9,10},{10,... | collective-permute-start | bytes 135176 | tf_op jit(solution)/shard_map/ppermute | solution.py:426
  135.5 4.8 %collective-permute-start.34 = (f32[88,128]{1,0:T(8,128)S(1)}, f32[88,128]{1,0:T(8,128)S(1)}, u32[]{:S(2)}, u32[]{:S(2)}) collective-permute-start(f32[88,128]{1,0:T(8,128)S(1)} %add.69), channel_id=1, source_target_pairs={{0,3},{1,6},{2,5},{3,0},{4,7},{5,2},{6,1},{7,4},{8,11},{9,14},{10,... | collective-permute-start | bytes 135176 | tf_op jit(solution)/shard_map/ppermute | solution.py:426
  140.2 4.2 %collective-permute-start.35 = (f32[88,128]{1,0:T(8,128)S(1)}, f32[88,128]{1,0:T(8,128)S(1)}, u32[]{:S(2)}, u32[]{:S(2)}) collective-permute-start(f32[88,128]{1,0:T(8,128)S(1)} %add.70), channel_id=1, source_target_pairs={{0,192},{32,224},{64,128},{96,160},{128,64},{160,96},{192,0},{224,... | collective-permute-start | bytes 135176 | tf_op jit(solution)/shard_map/ppermute | solution.py:428
  144.4 3.5 %collective-permute-start.36 = (f32[176,128]{1,0:T(8,128)S(1)}, f32[176,128]{1,0:T(8,128)S(1)}, u32[]{:S(2)}, u32[]{:S(2)}) collective-permute-start(f32[176,128]{1,0:T(8,128)S(1)} %maximum_select_fusion.5), channel_id=1, source_target_pairs={{0,64},{32,96},{64,0},{96,32},{128,192},{160,224},{192,128},{224,1... | collective-permute-start | bytes 270344 | tf_op jit(solution)/shard_map/ppermute | solution.py:428
  147.9 27.3 %collective-permute-start.37 = (f32[352,128]{1,0:T(8,128)S(1)}, f32[352,128]{1,0:T(8,128)S(1)}, u32[]{:S(2)}, u32[]{:S(2)}) collective-permute-start(f32[352,128]{1,0:T(8,128)S(1)} %maximum_select_fusion.3), channel_id=1, source_target_pairs={{0,32},{32,0},{64,96},{96,64},{128,160},{160,128},{192,224},{224,1... | collective-permute-start | bytes 540680 | tf_op jit(solution)/shard_map/ppermute | solution.py:428
  157.6 4.3 %collective-permute-start.23 = (f32[48,128]{1,0:T(8,128)S(1)}, f32[48,128]{1,0:T(8,128)S(1)}, u32[]{:S(2)}, u32[]{:S(2)}) collective-permute-start(f32[48,128]{1,0:T(8,128)S(1)} %get-tuple-element.55), channel_id=1, source_target_pairs={{0,32},{32,64},{64,96},{96,128},{128,160},{160,192},{192,224},{1,3... | collective-permute-start | bytes 73736 | tf_op jit(solution)/shard_map/ppermute | solution.py:141
  159.5 5.1 %collective-permute-start.24 = (f32[48,128]{1,0:T(8,128)S(1)}, f32[48,128]{1,0:T(8,128)S(1)}, u32[]{:S(2)}, u32[]{:S(2)}) collective-permute-start(f32[48,128]{1,0:T(8,128)S(1)} %get-tuple-element.56), channel_id=1, source_target_pairs={{32,0},{64,32},{96,64},{128,96},{160,128},{192,160},{224,192},{33,... | collective-permute-start | bytes 73736 | tf_op jit(solution)/shard_map/ppermute | solution.py:141
  164.8 4.8 %collective-permute-start.25 = (f32[16,128]{1,0:T(8,128)S(1)}, f32[16,128]{1,0:T(8,128)S(1)}, u32[]{:S(2)}, u32[]{:S(2)}) collective-permute-start(f32[16,128]{1,0:T(8,128)S(1)} %get-tuple-element.57), channel_id=1, source_target_pairs={{0,1},{1,2},{2,3},{3,4},{4,5},{5,6},{6,7},{7,8},{8,9},{9,10},{10,1... | collective-permute-start | bytes 24584 | tf_op jit(solution)/shard_map/ppermute | solution.py:141
  168.0 5.2 %collective-permute-start.26 = (f32[16,128]{1,0:T(8,128)S(1)}, f32[16,128]{1,0:T(8,128)S(1)}, u32[]{:S(2)}, u32[]{:S(2)}) collective-permute-start(f32[16,128]{1,0:T(8,128)S(1)} %get-tuple-element.58), channel_id=1, source_target_pairs={{1,0},{2,1},{3,2},{4,3},{5,4},{6,5},{7,6},{8,7},{9,8},{10,9},{11,1... | collective-permute-start | bytes 24584 | tf_op jit(solution)/shard_map/ppermute | solution.py:141

commit v2 on v1

--- a/solution.py
+++ b/solution.py
@@ -141,11 +141,13 @@
     return lax.ppermute(toward_high, axis, up), lax.ppermute(toward_low, axis, down)
 
 
+def pack(size, own, above, below):
+    return call(functools.partial(pack_kernel, size), [shape(size, LANES)] * 2)(own, above, below)
+
+
 def halos(size, own, top, bottom):
     above, below = neighbours("row", bottom, top)
-    left_edge, right_edge = call(
-        functools.partial(pack_kernel, size), [shape(size, LANES)] * 2
-    )(own, above, below)
+    left_edge, right_edge = pack(size, own, above, below)
     left, right = neighbours("col", right_edge, left_edge)
     return above, below, left, right
 
@@ -372,14 +374,6 @@
 CORR_SCRATCH = [pltpu.VMEM(((PAD_ROWS - 1) * LANES, 2 * LANES), BF16)] * 2
 
 
-def pairs_row(change):
-    return [(i, change(i // 2, i % 2)) for i in range(8)]
-
-
-def pairs_col(change):
-    return [(i, change(i // 8, i % 8)) for i in range(32)]
-
-
 def swap_even(i):
     return i ^ 1
 
@@ -389,9 +383,17 @@
 
 
 THIRD = {2: 5, 5: 2, 1: 6, 6: 1, 3: 0, 0: 3, 4: 7, 7: 4}
-CORE = pairs_row(lambda y, core: y * 2 + 1 - core)
-Y_EVEN = pairs_row(lambda y, core: swap_even(y) * 2 + core)
-Y_ODD = pairs_row(lambda y, core: swap_odd(y, 4) * 2 + core)
+INWARD = [(2 * y, 2 * y + 1) for y in range(4)]
+OUTWARD = [(2 * y + 1, 2 * y) for y in range(4)]
+Y_EVEN = [(2 * y + 1, 2 * swap_even(y) + 1) for y in range(4)]
+Y_ODD = [(2 * y + 1, 2 * swap_odd(y, 4) + 1) for y in range(4)]
+
+
+def pairs_col(change):
+    pairs = [(8 * x + z, change(x, z)) for x in range(4) for z in range(8)]
+    return [(32 * row + i, 32 * row + j) for row in (1, 3, 5, 7) for i, j in pairs]
+
+
 COLS = [
     pairs_col(lambda x, z: swap_even(x) * 8 + z),
     pairs_col(lambda x, z: swap_odd(x, 4) * 8 + z),
@@ -404,29 +406,42 @@
 def halves(value, bit):
     half = value.shape[0] // 2
     low, high = value[:half], value[half:]
-    return jnp.where(bit == 0, high, low), jnp.where(bit == 0, low, high)
+    return jnp.where(bit, low, high), jnp.where(bit, high, low)
 
 
 def joined(mine, other, bit):
-    return jnp.where(
-        bit == 0, jnp.concatenate([mine, other]), jnp.concatenate([other, mine])
-    )
-
-
-def sum_all(grad):
+    return jnp.where(bit, jnp.concatenate([other, mine]), jnp.concatenate([mine, other]))
+
+
+def sum_all(grad, state, side):
     row = lax.axis_index("row")
     y = row // 2
-    bits = [(row % 2, CORE), ((y == 1) | (y == 2), Y_EVEN), ((y == 2) | (y == 3), Y_ODD)]
-    bits = [(bit.astype(jnp.int32), pairs) for bit, pairs in bits]
+    upper = (y == 1) | (y == 2)
+    later = (y == 2) | (y == 3)
     value = grad
-    for bit, pairs in bits:
+
+    def beside(k, sent, axes, pairs, kept):
+        nonlocal state
+        sent, kept, state = lax.optimization_barrier((sent, kept, state))
+        other = lax.ppermute(sent, axes, pairs)
+        if k in side:
+            state = side[k](state)
+        return kept, other
+
+    kept, other = beside(0, value, "row", INWARD, value)
+    value = kept + other
+    for k, bit, pairs in ((1, upper, Y_EVEN), (2, later, Y_ODD)):
         sent, kept = halves(value, bit)
-        value = kept + lax.ppermute(sent, "row", pairs)
-    for pairs in COLS:
-        value = value + lax.ppermute(value, "col", pairs)
-    for bit, pairs in reversed(bits):
-        value = joined(value, lax.ppermute(value, "row", pairs), bit)
-    return value
+        kept, other = beside(k, sent, "row", pairs, kept)
+        value = kept + other
+    for k, pairs in enumerate(COLS):
+        kept, other = beside(3 + k, value, ("row", "col"), pairs, value)
+        value = kept + other
+    for k, bit, pairs in ((8, later, Y_ODD), (9, upper, Y_EVEN)):
+        kept, other = beside(k, value, "row", pairs, value)
+        value = joined(kept, other, bit)
+    kept, other = beside(10, value, "row", OUTWARD, value)
+    return jnp.where(row % 2 == 0, other, kept), state
 
 
 def local(observed, coef_maps, dictionary, consensus, dual_vars):
@@ -440,19 +455,56 @@
     resid, r_top, r_bottom, grad = call(first_kernel, RECON_OUT, RECON_SCRATCH)(
         maps, *edges, observed, filt
     )
-    summed = sum_all(grad)
-    r_edges = halos(C, resid, r_top, r_bottom)
-    maps, top, bottom = call(functools.partial(corr_kernel, False), map_rows, CORR_SCRATCH)(
-        resid, *r_edges, filt, maps
+
+    def resid_rows(state):
+        resid, top, bottom, filt, maps = state
+        return resid, neighbours("row", bottom, top), filt, maps
+
+    def resid_columns(state):
+        resid, around, filt, maps = state
+        left_edge, right_edge = pack(C, resid, *around)
+        return resid, (*around, *neighbours("col", right_edge, left_edge)), filt, maps
+
+    def threshold(last, outs):
+        def run(state):
+            resid, around, filt, maps = state
+            return call(functools.partial(corr_kernel, last), outs, CORR_SCRATCH)(
+                resid, *around, filt, maps
+            )
+
+        return run
+
+    def map_rows_out(state):
+        maps, top, bottom = state
+        return maps, neighbours("row", bottom, top)
+
+    def map_pack(state):
+        maps, around = state
+        return maps, around, pack(M, maps, *around)
+
+    def map_columns(state):
+        maps, around, (left_edge, right_edge) = state
+        return maps, (*around, *neighbours("col", right_edge, left_edge))
+
+    summed, (maps, edges) = sum_all(
+        grad,
+        (resid, r_top, r_bottom, filt, maps),
+        {
+            0: resid_rows,
+            1: resid_columns,
+            2: threshold(False, map_rows),
+            3: map_rows_out,
+            5: map_pack,
+            8: map_columns,
+        },
     )
-    edges = halos(M, maps, top, bottom)
     filt, cons, duals, resid, r_top, r_bottom, grad = call(
         next_kernel, filters + RECON_OUT, RECON_SCRATCH
     )(summed, filt, cons, duals, maps, *edges, observed)
-    summed = sum_all(grad)
-    r_edges = halos(C, resid, r_top, r_bottom)
-    new_maps = call(functools.partial(corr_kernel, True), shape(M, ROWS, LANES), CORR_SCRATCH)(
-        resid, *r_edges, filt, maps
+    summed, new_maps = sum_all(
+        grad,
+        (resid, r_top, r_bottom, filt, maps),
+        {0: resid_rows, 3: resid_columns, 5: threshold(True, shape(M, ROWS, LANES))},
     )
     new = call(
         last_kernel,

time: 180 us -> 196 us (1.089)
  starting transfers between devices: 91.9 us -> 111 us
  waiting for transfers between devices: 68.3 us -> 64.7 us
    ppermute x22, starting transfers between devices: 44.6 us -> 72.4 us  [beside(): other = lax.ppermute(sent, axes, pairs)]
    ppermute x8, starting transfers between devices: 33.8 us -> 24.9 us  [neighbours(): lax.ppermute(toward_high, axis, up)]
    ppermute x8, waiting for transfers between devices: 26.2 us -> 21 us  [neighbours(): lax.ppermute(toward_low, axis, down)]
  transfers between devices with their start and end apart: 38 -> 38, of which waited for: 29 -> 26; matrix products, arithmetic and copies ran while one was open for 0% -> 0% of each run, Pallas kernels for 4% -> 4%
where the time goes in v2:
time: 196 us; the launch traced here: 195 us
  starting transfers between devices  111 us (57%)
  waiting for transfers between devices  64.7 us (33%)
  Pallas kernels  16.8 us (9%)
    ppermute x22, starting transfers between devices, beside(): other = lax.ppermute(sent, axes, pairs)  72.4 us
    ppermute x22, waiting for transfers between devices, beside(): other = lax.ppermute(sent, axes, pairs)  43.6 us
    ppermute x8, starting transfers between devices, neighbours(): lax.ppermute(toward_high, axis, up)  24.9 us
    ppermute x8, waiting for transfers between devices, neighbours(): lax.ppermute(toward_low, axis, down)  21 us
    ppermute x8, starting transfers between devices, neighbours(): lax.ppermute(toward_low, axis, down)  13.5 us
    pallas_call x1, Pallas kernels, local(): call(last_kernel, [shape(M, FLAT)] * 3, [pltpu.VMEM((3, D_ROWS, LANES), F...  4.17 us
  transfers between devices with their start and end apart: 38, of which 26 were waited for; matrix products, arithmetic and copies ran while one was open for 0% of the time, Pallas kernels for 4%

profile of v2, /device:TPU:1, one launch (start us, length us, event | category | flops | bytes accessed | tf_op | source)
XLA Modules:
  0.0 195.0 jit_solution(4883056211867349461)
XLA Ops:
  1.9 4.6 %collective-permute-start = (f32[288,128]{1,0:T(8,128)S(1)}, f32[288,128]{1,0:T(8,128)S(1)}, u32[]{:S(2)}, u32[]{:S(2)}) collective-permute-start(f32[288,128]{1,0:T(8,128)S(1)} %get-tuple-element.170), channel_id=1, source_target_pairs={{0,32},{32,64},{64,96},{96,128},{128,160},{160,192},{192,224},{1,3... | collective-permute-start | bytes 442376 | tf_op jit(solution)/shard_map/ppermute | solution.py:141
  6.5 1.9 collective-permute-start.1
  8.5 4.4 %collective-permute-done.1.below = f32[288,128]{1,0:T(8,128)S(1)} collective-permute-done((f32[288,128]{1,0:T(8,128)S(1)}, f32[288,128]{1,0:T(8,128)S(1)}, u32[]{:S(2)}, u32[]{:S(2)}) %collective-permute-start.1) | collective-permute-done | bytes 147488 | tf_op jit(solution)/shard_map/ppermute | solution.py:141
  13.3 3.5 %collective-permute-start.2 = (f32[96,128]{1,0:T(8,128)S(1)}, f32[96,128]{1,0:T(8,128)S(1)}, u32[]{:S(2)}, u32[]{:S(2)}) collective-permute-start(f32[96,128]{1,0:T(8,128)S(1)} %get-tuple-element.172), channel_id=1, source_target_pairs={{0,1},{1,2},{2,3},{3,4},{4,5},{5,6},{6,7},{7,8},{8,9},{9,10},{10,1... | collective-permute-start | bytes 147464 | tf_op jit(solution)/shard_map/ppermute | solution.py:141
  16.9 1.4 collective-permute-start.3
  18.4 3.0 %shard_map.86 = (f32[672,128]{1,0:T(8,128)S(1)}, f32[672,128]{1,0:T(8,128)S(1)}, f32[672,128]{1,0:T(8,128)S(1)}) custom-call(f32[96,784]{1,0:T(8,128)S(1)} %copy-done.1, f32[96,784]{1,0:T(8,128)S(1)} %copy-done.2, f32[96,784]{1,0:T(8,128)S(1)} %copy-done.3), custom_call_target="tpu_custom_call" | custom-call | tf_op jit(solution)/shard_map/pallas_call | solution.py:451
  22.0 2.5 %shard_map.87 = (f32[128,128]{1,0:T(8,128)S(1)}, f32[48,128]{1,0:T(8,128)S(1)}, f32[48,128]{1,0:T(8,128)S(1)}, f32[704,128]{1,0:T(8,128)S(1)}) custom-call(f32[768,128]{1,0:T(8,128)S(1)} %get-tuple-element.203.own.maps, f32[288,128]{1,0:T(8,128)S(1)} %collective-permute-done.above, f32[288,128]{1,0:T(8,128)S(1)} %collective-permute-done.1.below, ...), custom_call_target="tpu_custom_call" | custom-call | tf_op jit(solution)/shard_map/pallas_call | solution.py:455
  24.6 1.3 collective-permute-start.4
  25.9 4.2 %collective-permute-start.5 = (f32[48,128]{1,0:T(8,128)S(1)}, f32[48,128]{1,0:T(8,128)S(1)}, u32[]{:S(2)}, u32[]{:S(2)}) collective-permute-start(f32[48,128]{1,0:T(8,128)S(1)} %get-tuple-element.182), channel_id=1, source_target_pairs={{0,32},{32,64},{64,96},{96,128},{128,160},{160,192},{192,224},{1,3... | collective-permute-start | bytes 73736 | tf_op jit(solution)/shard_map/ppermute | solution.py:141
  30.2 1.9 collective-permute-start.6
  32.2 3.1 %collective-permute-done.6.below = f32[48,128]{1,0:T(8,128)S(1)} collective-permute-done((f32[48,128]{1,0:T(8,128)S(1)}, f32[48,128]{1,0:T(8,128)S(1)}, u32[]{:S(2)}, u32[]{:S(2)}) %collective-permute-start.6) | collective-permute-done | bytes 24608 | tf_op jit(solution)/shard_map/ppermute | solution.py:141
  35.3 2.9 %collective-permute-start.7 = (f32[352,128]{1,0:T(8,128)S(1)}, f32[352,128]{1,0:T(8,128)S(1)}, u32[]{:S(2)}, u32[]{:S(2)}) collective-permute-start(f32[352,128]{1,0:T(8,128)S(1)} %get-tuple-element.187), channel_id=1, source_target_pairs={{32,96},{96,32},{160,224},{224,160},{33,97},{97,33},{161,225},{225... | collective-permute-start | bytes 540680 | tf_op jit(solution)/shard_map/ppermute | solution.py:426
  38.4 3.6 %collective-permute-start.8 = (f32[16,128]{1,0:T(8,128)S(1)}, f32[16,128]{1,0:T(8,128)S(1)}, u32[]{:S(2)}, u32[]{:S(2)}) collective-permute-start(f32[16,128]{1,0:T(8,128)S(1)} %get-tuple-element.191), channel_id=1, source_target_pairs={{0,1},{1,2},{2,3},{3,4},{4,5},{5,6},{6,7},{7,8},{8,9},{9,10},{10,1... | collective-permute-start | bytes 24584 | tf_op jit(solution)/shard_map/ppermute | solution.py:141
  41.9 1.3 collective-permute-start.9
  43.3 4.4 %collective-permute-done.9.right = f32[16,128]{1,0:T(8,128)S(1)} collective-permute-done((f32[16,128]{1,0:T(8,128)S(1)}, f32[16,128]{1,0:T(8,128)S(1)}, u32[]{:S(2)}, u32[]{:S(2)}) %collective-permute-start.9) | collective-permute-done | bytes 8224 | tf_op jit(solution)/shard_map/ppermute | solution.py:141
  47.7 2.5 %collective-permute-start.10 = (f32[176,128]{1,0:T(8,128)S(1)}, f32[176,128]{1,0:T(8,128)S(1)}, u32[]{:S(2)}, u32[]{:S(2)}) collective-permute-start(f32[176,128]{1,0:T(8,128)S(1)} %get-tuple-element.196), channel_id=1, source_target_pairs={{32,224},{96,160},{160,96},{224,32},{33,225},{97,161},{161,97},{22... | collective-permute-start | bytes 270344 | tf_op jit(solution)/shard_map/ppermute | solution.py:426
  51.4 2.8 %collective-permute-done.10 = f32[176,128]{1,0:T(8,128)S(1)} collective-permute-done((f32[176,128]{1,0:T(8,128)S(1)}, f32[176,128]{1,0:T(8,128)S(1)}, u32[]{:S(2)}, u32[]{:S(2)}) %collective-permute-start.10) | collective-permute-done | bytes 90144 | tf_op jit(solution)/shard_map/ppermute | solution.py:426
  54.2 1.9 collective-permute-start.12
  56.1 2.4 %collective-permute-start.13 = (f32[288,128]{1,0:T(8,128)S(1)}, f32[288,128]{1,0:T(8,128)S(1)}, u32[]{:S(2)}, u32[]{:S(2)}) collective-permute-start(f32[288,128]{1,0:T(8,128)S(1)} %get-tuple-element.211), channel_id=1, source_target_pairs={{32,0},{64,32},{96,64},{128,96},{160,128},{192,160},{224,192},{33,... | collective-permute-start | bytes 442376 | tf_op jit(solution)/shard_map/ppermute | solution.py:141
  58.5 5.9 %collective-permute-start.11 = (f32[176,128]{1,0:T(8,128)S(1)}, f32[176,128]{1,0:T(8,128)S(1)}, u32[]{:S(2)}, u32[]{:S(2)}) collective-permute-start(f32[176,128]{1,0:T(8,128)S(1)} %add.57), channel_id=1, source_target_pairs={{32,40},{33,41},{34,42},{35,43},{36,44},{37,45},{38,46},{39,47},{4... | collective-permute-start | bytes 270344 | tf_op jit(solution)/shard_map/ppermute | solution.py:426
  64.4 1.9 collective-permute-done.11
  66.3 4.9 %collective-permute-start.14 = (f32[176,128]{1,0:T(8,128)S(1)}, f32[176,128]{1,0:T(8,128)S(1)}, u32[]{:S(2)}, u32[]{:S(2)}) collective-permute-start(f32[176,128]{1,0:T(8,128)S(1)} %add.58), channel_id=1, source_target_pairs={{32,56},{33,57},{34,58},{35,59},{36,60},{37,61},{38,62},{39,63},{4... | collective-permute-start | bytes 270344 | tf_op jit(solution)/shard_map/ppermute | solution.py:426
  71.2 1.9 collective-permute-done.14
  73.2 2.0 %collective-permute-start.15 = (f32[176,128]{1,0:T(8,128)S(1)}, f32[176,128]{1,0:T(8,128)S(1)}, u32[]{:S(2)}, u32[]{:S(2)}) collective-permute-start(f32[176,128]{1,0:T(8,128)S(1)} %add.59), channel_id=1, source_target_pairs={{32,33},{33,32},{34,35},{35,34},{36,37},{37,36},{38,39},{39,38},{4... | collective-permute-start | bytes 270344 | tf_op jit(solution)/shard_map/ppermute | solution.py:426
  75.5 2.9 %collective-permute-done.15 = f32[176,128]{1,0:T(8,128)S(1)} collective-permute-done((f32[176,128]{1,0:T(8,128)S(1)}, f32[176,128]{1,0:T(8,128)S(1)}, u32[]{:S(2)}, u32[]{:S(2)}) %collective-permute-start.15) | collective-permute-done | bytes 90144 | tf_op jit(solution)/shard_map/ppermute | solution.py:426
  78.5 5.6 %collective-permute-start.16 = (f32[176,128]{1,0:T(8,128)S(1)}, f32[176,128]{1,0:T(8,128)S(1)}, u32[]{:S(2)}, u32[]{:S(2)}) collective-permute-start(f32[176,128]{1,0:T(8,128)S(1)} %add.60), channel_id=1, source_target_pairs={{32,39},{33,34},{34,33},{35,36},{36,35},{37,38},{38,37},{39,32},{4... | collective-permute-start | bytes 270344 | tf_op jit(solution)/shard_map/ppermute | solution.py:426
  84.1 1.9 collective-permute-done.16
  86.0 4.4 %collective-permute-start.17 = (f32[176,128]{1,0:T(8,128)S(1)}, f32[176,128]{1,0:T(8,128)S(1)}, u32[]{:S(2)}, u32[]{:S(2)}) collective-permute-start(f32[176,128]{1,0:T(8,128)S(1)} %add.61), channel_id=1, source_target_pairs={{32,35},{33,38},{34,37},{35,32},{36,39},{37,34},{38,33},{39,36},{4... | collective-permute-start | bytes 270344 | tf_op jit(solution)/shard_map/ppermute | solution.py:426
  90.4 2.8 %collective-permute-done.17 = f32[176,128]{1,0:T(8,128)S(1)} collective-permute-done((f32[176,128]{1,0:T(8,128)S(1)}, f32[176,128]{1,0:T(8,128)S(1)}, u32[]{:S(2)}, u32[]{:S(2)}) %collective-permute-start.17) | collective-permute-done | bytes 90144 | tf_op jit(solution)/shard_map/ppermute | solution.py:426
  93.2 1.9 collective-permute-start.18
  95.1 2.0 %collective-permute-start.19 = (f32[96,128]{1,0:T(8,128)S(1)}, f32[96,128]{1,0:T(8,128)S(1)}, u32[]{:S(2)}, u32[]{:S(2)}) collective-permute-start(f32[96,128]{1,0:T(8,128)S(1)} %get-tuple-element.243), channel_id=1, source_target_pairs={{0,1},{1,2},{2,3},{3,4},{4,5},{5,6},{6,7},{7,8},{8,9},{9,10},{10,1... | collective-permute-start | bytes 147464 | tf_op jit(solution)/shard_map/ppermute | solution.py:141
  97.1 1.3 collective-permute-start.20
  99.7 2.3 %collective-permute-done.20.right = f32[96,128]{1,0:T(8,128)S(1)} collective-permute-done((f32[96,128]{1,0:T(8,128)S(1)}, f32[96,128]{1,0:T(8,128)S(1)}, u32[]{:S(2)}, u32[]{:S(2)}) %collective-permute-start.20) | collective-permute-done | bytes 49184 | tf_op jit(solution)/shard_map/ppermute | solution.py:141
  102.0 2.6 %collective-permute-start.21 = (f32[352,128]{1,0:T(8,128)S(1)}, f32[352,128]{1,0:T(8,128)S(1)}, u32[]{:S(2)}, u32[]{:S(2)}) collective-permute-start(f32[352,128]{1,0:T(8,128)S(1)} %maximum_select_fusion.2), channel_id=1, source_target_pairs={{32,96},{96,32},{160,224},{224,160},{33,97},{97,33},{161,225},{225... | collective-permute-start | bytes 540680 | tf_op jit(solution)/shard_map/ppermute | solution.py:426
  104.6 3.6 %collective-permute-done.21 = f32[352,128]{1,0:T(8,128)S(1)} collective-permute-done((f32[352,128]{1,0:T(8,128)S(1)}, f32[352,128]{1,0:T(8,128)S(1)}, u32[]{:S(2)}, u32[]{:S(2)}) %collective-permute-start.21) | collective-permute-done | bytes 180256 | tf_op jit(solution)/shard_map/ppermute | solution.py:426
  108.2 1.3 collective-permute-start.22
  110.8 2.6 %shard_map.91 = (f32[672,128]{1,0:T(8,128)S(1)}, f32[672,128]{1,0:T(8,128)S(1)}, f32[672,128]{1,0:T(8,128)S(1)}, f32[128,128]{1,0:T(8,128)S(1)}, f32[48,128]{1,0...) custom-call(f32[704,128]{1,0:T(8,128)S(1)} %broadcast_select_fusion.1.summed, ...), custom_call_target="tpu_custom_call" | custom-call | tf_op jit(solution)/shard_map/pallas_call | solution.py:501
  113.4 1.3 collective-permute-start.23
  114.7 3.7 %collective-permute-start.24 = (f32[48,128]{1,0:T(8,128)S(1)}, f32[48,128]{1,0:T(8,128)S(1)}, u32[]{:S(2)}, u32[]{:S(2)}) collective-permute-start(f32[48,128]{1,0:T(8,128)S(1)} %get-tuple-element.269), channel_id=1, source_target_pairs={{0,32},{32,64},{64,96},{96,128},{128,160},{160,192},{192,224},{1,3... | collective-permute-start | bytes 73736 | tf_op jit(solution)/shard_map/ppermute | solution.py:141
  118.4 1.9 collective-permute-start.25
  120.5 3.1 %collective-permute-done.25.below = f32[48,128]{1,0:T(8,128)S(1)} collective-permute-done((f32[48,128]{1,0:T(8,128)S(1)}, f32[48,128]{1,0:T(8,128)S(1)}, u32[]{:S(2)}, u32[]{:S(2)}) %collective-permute-start.25) | collective-permute-done | bytes 24608 | tf_op jit(solution)/shard_map/ppermute | solution.py:141
  123.6 3.2 %collective-permute-start.26 = (f32[352,128]{1,0:T(8,128)S(1)}, f32[352,128]{1,0:T(8,128)S(1)}, u32[]{:S(2)}, u32[]{:S(2)}) collective-permute-start(f32[352,128]{1,0:T(8,128)S(1)} %get-tuple-element.274), channel_id=1, source_target_pairs={{32,96},{96,32},{160,224},{224,160},{33,97},{97,33},{161,225},{225... | collective-permute-start | bytes 540680 | tf_op jit(solution)/shard_map/ppermute | solution.py:426
  126.8 3.0 %collective-permute-done.26 = f32[352,128]{1,0:T(8,128)S(1)} collective-permute-done((f32[352,128]{1,0:T(8,128)S(1)}, f32[352,128]{1,0:T(8,128)S(1)}, u32[]{:S(2)}, u32[]{:S(2)}) %collective-permute-start.26) | collective-permute-done | bytes 180256 | tf_op jit(solution)/shard_map/ppermute | solution.py:426
  129.8 3.8 %collective-permute-start.27 = (f32[176,128]{1,0:T(8,128)S(1)}, f32[176,128]{1,0:T(8,128)S(1)}, u32[]{:S(2)}, u32[]{:S(2)}) collective-permute-start(f32[176,128]{1,0:T(8,128)S(1)} %get-tuple-element.281), channel_id=1, source_target_pairs={{32,224},{96,160},{160,96},{224,32},{33,225},{97,161},{161,97},{22... | collective-permute-start | bytes 270344 | tf_op jit(solution)/shard_map/ppermute | solution.py:426
  133.7 2.6 %collective-permute-done.27 = f32[176,128]{1,0:T(8,128)S(1)} collective-permute-done((f32[176,128]{1,0:T(8,128)S(1)}, f32[176,128]{1,0:T(8,128)S(1)}, u32[]{:S(2)}, u32[]{:S(2)}) %collective-permute-start.27) | collective-permute-done | bytes 90144 | tf_op jit(solution)/shard_map/ppermute | solution.py:426
  136.3 4.4 %collective-permute-start.28 = (f32[176,128]{1,0:T(8,128)S(1)}, f32[176,128]{1,0:T(8,128)S(1)}, u32[]{:S(2)}, u32[]{:S(2)}) collective-permute-start(f32[176,128]{1,0:T(8,128)S(1)} %add.65), channel_id=1, source_target_pairs={{32,40},{33,41},{34,42},{35,43},{36,44},{37,45},{38,46},{39,47},{4... | collective-permute-start | bytes 270344 | tf_op jit(solution)/shard_map/ppermute | solution.py:426
  140.9 1.3 collective-permute-start.29
  142.2 1.3 collective-permute-start.30
  143.6 3.1 %collective-permute-done.30.right = f32[16,128]{1,0:T(8,128)S(1)} collective-permute-done((f32[16,128]{1,0:T(8,128)S(1)}, f32[16,128]{1,0:T(8,128)S(1)}, u32[]{:S(2)}, u32[]{:S(2)}) %collective-permute-start.30) | collective-permute-done | bytes 8224 | tf_op jit(solution)/shard_map/ppermute | solution.py:141
  146.6 5.9 %collective-permute-start.31 = (f32[176,128]{1,0:T(8,128)S(1)}, f32[176,128]{1,0:T(8,128)S(1)}, u32[]{:S(2)}, u32[]{:S(2)}) collective-permute-start(f32[176,128]{1,0:T(8,128)S(1)} %add.66), channel_id=1, source_target_pairs={{32,56},{33,57},{34,58},{35,59},{36,60},{37,61},{38,62},{39,63},{4... | collective-permute-start | bytes 270344 | tf_op jit(solution)/shard_map/ppermute | solution.py:426
  152.6 1.7 collective-permute-done.31
  154.3 2.2 %collective-permute-start.32 = (f32[176,128]{1,0:T(8,128)S(1)}, f32[176,128]{1,0:T(8,128)S(1)}, u32[]{:S(2)}, u32[]{:S(2)}) collective-permute-start(f32[176,128]{1,0:T(8,128)S(1)} %add.67), channel_id=1, source_target_pairs={{32,33},{33,32},{34,35},{35,34},{36,37},{37,36},{38,39},{39,38},{4... | collective-permute-start | bytes 270344 | tf_op jit(solution)/shard_map/ppermute | solution.py:426
  156.5 2.0 %shard_map.93 = f32[96,8,128]{2,1,0:T(8,128)} custom-call(f32[128,128]{1,0:T(8,128)S(1)} %get-tuple-element.307.own.resid, f32[48,128]{1,0:T(8,128)S(1)} %collective-permute-done.24.above, f32[48,128]{1,0:T(8,128)S(1)} %collective-permute-done.25.below, f32[16,128]{1,0:T(8,128)S(1)} %collective-permute-done.29.left, ...), custom_call_target="tpu_custom_call" | custom-call | tf_op jit(solution)/shard_map/pallas_call | solution.py:471
  159.6 6.6 %collective-permute-start.33 = (f32[176,128]{1,0:T(8,128)S(1)}, f32[176,128]{1,0:T(8,128)S(1)}, u32[]{:S(2)}, u32[]{:S(2)}) collective-permute-start(f32[176,128]{1,0:T(8,128)S(1)} %add.68), channel_id=1, source_target_pairs={{32,39},{33,34},{34,33},{35,36},{36,35},{37,38},{38,37},{39,32},{4... | collective-permute-start | bytes 270344 | tf_op jit(solution)/shard_map/ppermute | solution.py:426
  166.2 1.9 collective-permute-done.33
  168.2 2.4 %collective-permute-start.34 = (f32[176,128]{1,0:T(8,128)S(1)}, f32[176,128]{1,0:T(8,128)S(1)}, u32[]{:S(2)}, u32[]{:S(2)}) collective-permute-start(f32[176,128]{1,0:T(8,128)S(1)} %add.69), channel_id=1, source_target_pairs={{32,35},{33,38},{34,37},{35,32},{36,39},{37,34},{38,33},{39,36},{4... | collective-permute-start | bytes 270344 | tf_op jit(solution)/shard_map/ppermute | solution.py:426
  170.6 4.8 %collective-permute-done.34 = f32[176,128]{1,0:T(8,128)S(1)} collective-permute-done((f32[176,128]{1,0:T(8,128)S(1)}, f32[176,128]{1,0:T(8,128)S(1)}, u32[]{:S(2)}, u32[]{:S(2)}) %collective-permute-start.34) | collective-permute-done | bytes 90144 | tf_op jit(solution)/shard_map/ppermute | solution.py:426
  175.4 3.9 %collective-permute-start.35 = (f32[176,128]{1,0:T(8,128)S(1)}, f32[176,128]{1,0:T(8,128)S(1)}, u32[]{:S(2)}, u32[]{:S(2)}) collective-permute-start(f32[176,128]{1,0:T(8,128)S(1)} %add.70), channel_id=1, source_target_pairs={{32,224},{96,160},{160,96},{224,32},{33,225},{97,161},{161,97},{22... | collective-permute-start | bytes 270344 | tf_op jit(solution)/shard_map/ppermute | solution.py:426
  179.3 2.6 %collective-permute-done.35 = f32[176,128]{1,0:T(8,128)S(1)} collective-permute-done((f32[176,128]{1,0:T(8,128)S(1)}, f32[176,128]{1,0:T(8,128)S(1)}, u32[]{:S(2)}, u32[]{:S(2)}) %collective-permute-start.35) | collective-permute-done | bytes 90144 | tf_op jit(solution)/shard_map/ppermute | solution.py:426
  181.9 1.9 collective-permute-start.36
  183.9 4.3 %collective-permute-done.36 = f32[352,128]{1,0:T(8,128)S(1)} collective-permute-done((f32[352,128]{1,0:T(8,128)S(1)}, f32[352,128]{1,0:T(8,128)S(1)}, u32[]{:S(2)}, u32[]{:S(2)}) %collective-permute-start.36) | collective-permute-done | bytes 180256 | tf_op jit(solution)/shard_map/ppermute | solution.py:426
  188.2 1.3 collective-permute-start.37
  189.5 1.3 collective-permute-done.37
  190.8 4.2 %shard_map.94 = (f32[96,784]{1,0:T(8,128)}, f32[96,784]{1,0:T(8,128)}, f32[96,784]{1,0:T(8,128)}) custom-call(f32[704,128]{1,0:T(8,128)S(1)} %broadcast_select_fusion.summed, f32[672,128]{1,0:T(8,128)S(1)} %get-tuple-element.312.filt, f32[672,128]{1,0:T(8,128)S(1)} %get-tuple-element.329.cons, f32[672,128]{1,0:T(8,128)S(1)} %get-tuple-element.330.duals), custom_call_target="tpu_custom_call" | custom-call | tf_op jit(solution)/shard_map/pallas_call | solution.py:509
  (59 shorter events, 8.4 us)
Async XLA Ops:
  0.6 1.0 copy-start
  1.6 16.7 %copy-start.3 = (f32[96,784]{1,0:T(8,128)S(1)}, f32[96,784]{1,0:T(8,128)}, u32[]{:S(2)}) copy-start(f32[96,784]{1,0:T(8,128)} %duals.1) | copy-start | bytes 903172
  1.9 6.7 %collective-permute-start = (f32[288,128]{1,0:T(8,128)S(1)}, f32[288,128]{1,0:T(8,128)S(1)}, u32[]{:S(2)}, u32[]{:S(2)}) collective-permute-start(f32[288,128]{1,0:T(8,128)S(1)} %get-tuple-element.170), channel_id=1, source_target_pairs={{0,32},{32,64},{64,96},{96,128},{128,160},{160,192},{192,224},{1,3... | collective-permute-start | bytes 442376 | tf_op jit(solution)/shard_map/ppermute | solution.py:141
  6.5 6.5 %collective-permute-start.1 = (f32[288,128]{1,0:T(8,128)S(1)}, f32[288,128]{1,0:T(8,128)S(1)}, u32[]{:S(2)}, u32[]{:S(2)}) collective-permute-start(f32[288,128]{1,0:T(8,128)S(1)} %get-tuple-element.171), channel_id=1, source_target_pairs={{32,0},{64,32},{96,64},{128,96},{160,128},{192,160},{224,192},{33,... | collective-permute-start | bytes 442376 | tf_op jit(solution)/shard_map/ppermute | solution.py:141
  12.9 5.4 %copy-start.1 = (f32[96,784]{1,0:T(8,128)S(1)}, f32[96,784]{1,0:T(8,128)}, u32[]{:S(2)}) copy-start(f32[96,784]{1,0:T(8,128)} %filt.1) | copy-start | bytes 903172
  12.9 5.4 %copy-start.2 = (f32[96,784]{1,0:T(8,128)S(1)}, f32[96,784]{1,0:T(8,128)}, u32[]{:S(2)}) copy-start(f32[96,784]{1,0:T(8,128)} %cons.1) | copy-start | bytes 903172
  13.3 8.0 %collective-permute-start.2 = (f32[96,128]{1,0:T(8,128)S(1)}, f32[96,128]{1,0:T(8,128)S(1)}, u32[]{:S(2)}, u32[]{:S(2)}) collective-permute-start(f32[96,128]{1,0:T(8,128)S(1)} %get-tuple-element.172), channel_id=1, source_target_pairs={{0,1},{1,2},{2,3},{3,4},{4,5},{5,6},{6,7},{7,8},{8,9},{9,10},{10,1... | collective-permute-start | bytes 147464 | tf_op jit(solution)/shard_map/ppermute | solution.py:141
  16.9 5.2 %copy-start.4 = (f32[16,8,128]{2,1,0:T(8,128)S(1)}, f32[16,8,128]{2,1,0:T(8,128)}, u32[]{:S(2)}) copy-start(f32[16,8,128]{2,1,0:T(8,128)} %observed.3) | copy-start | bytes 196612
  16.9 5.2 %collective-permute-start.3 = (f32[96,128]{1,0:T(8,128)S(1)}, f32[96,128]{1,0:T(8,128)S(1)}, u32[]{:S(2)}, u32[]{:S(2)}) collective-permute-start(f32[96,128]{1,0:T(8,128)S(1)} %get-tuple-element.173), channel_id=1, source_target_pairs={{1,0},{2,1},{3,2},{4,3},{5,4},{6,5},{7,6},{8,7},{9,8},{10,9},{11,1... | collective-permute-start | bytes 147464 | tf_op jit(solution)/shard_map/ppermute | solution.py:141
  24.6 7.5 %collective-permute-start.4 = (f32[704,128]{1,0:T(8,128)S(1)}, f32[704,128]{1,0:T(8,128)S(1)}, u32[]{:S(2)}, u32[]{:S(2)}) collective-permute-start(f32[704,128]{1,0:T(8,128)S(1)} %get-tuple-element.180), channel_id=1, source_target_pairs={{0,32},{64,96},{128,160},{192,224},{1,33},{65,97},{129,161},{193,2... | collective-permute-start | bytes 1081352 | tf_op jit(solution)/shard_map/ppermute | solution.py:426
  25.9 6.3 %collective-permute-start.5 = (f32[48,128]{1,0:T(8,128)S(1)}, f32[48,128]{1,0:T(8,128)S(1)}, u32[]{:S(2)}, u32[]{:S(2)}) collective-permute-start(f32[48,128]{1,0:T(8,128)S(1)} %get-tuple-element.182), channel_id=1, source_target_pairs={{0,32},{32,64},{64,96},{96,128},{128,160},{160,192},{192,224},{1,3... | collective-permute-start | bytes 73736 | tf_op jit(solution)/shard_map/ppermute | solution.py:141
  30.2 5.1 %collective-permute-start.6 = (f32[48,128]{1,0:T(8,128)S(1)}, f32[48,128]{1,0:T(8,128)S(1)}, u32[]{:S(2)}, u32[]{:S(2)}) collective-permute-start(f32[48,128]{1,0:T(8,128)S(1)} %get-tuple-element.183), channel_id=1, source_target_pairs={{32,0},{64,32},{96,64},{128,96},{160,128},{192,160},{224,192},{33,... | collective-permute-start | bytes 73736 | tf_op jit(solution)/shard_map/ppermute | solution.py:141
  35.3 7.9 %collective-permute-start.7 = (f32[352,128]{1,0:T(8,128)S(1)}, f32[352,128]{1,0:T(8,128)S(1)}, u32[]{:S(2)}, u32[]{:S(2)}) collective-permute-start(f32[352,128]{1,0:T(8,128)S(1)} %get-tuple-element.187), channel_id=1, source_target_pairs={{32,96},{96,32},{160,224},{224,160},{33,97},{97,33},{161,225},{225... | collective-permute-start | bytes 540680 | tf_op jit(solution)/shard_map/ppermute | solution.py:426
  38.4 4.9 %collective-permute-start.8 = (f32[16,128]{1,0:T(8,128)S(1)}, f32[16,128]{1,0:T(8,128)S(1)}, u32[]{:S(2)}, u32[]{:S(2)}) collective-permute-start(f32[16,128]{1,0:T(8,128)S(1)} %get-tuple-element.191), channel_id=1, source_target_pairs={{0,1},{1,2},{2,3},{3,4},{4,5},{5,6},{6,7},{7,8},{8,9},{9,10},{10,1... | collective-permute-start | bytes 24584 | tf_op jit(solution)/shard_map/ppermute | solution.py:141
  41.9 5.7 %collective-permute-start.9 = (f32[16,128]{1,0:T(8,128)S(1)}, f32[16,128]{1,0:T(8,128)S(1)}, u32[]{:S(2)}, u32[]{:S(2)}) collective-permute-start(f32[16,128]{1,0:T(8,128)S(1)} %get-tuple-element.192), channel_id=1, source_target_pairs={{1,0},{2,1},{3,2},{4,3},{5,4},{6,5},{7,6},{8,7},{9,8},{10,9},{11,1... | collective-permute-start | bytes 24584 | tf_op jit(solution)/shard_map/ppermute | solution.py:141
  47.7 6.5 %collective-permute-start.10 = (f32[176,128]{1,0:T(8,128)S(1)}, f32[176,128]{1,0:T(8,128)S(1)}, u32[]{:S(2)}, u32[]{:S(2)}) collective-permute-start(f32[176,128]{1,0:T(8,128)S(1)} %get-tuple-element.196), channel_id=1, source_target_pairs={{32,224},{96,160},{160,96},{224,32},{33,225},{97,161},{161,97},{22... | collective-permute-start | bytes 270344 | tf_op jit(solution)/shard_map/ppermute | solution.py:426
  54.2 12.1 %collective-permute-start.12 = (f32[288,128]{1,0:T(8,128)S(1)}, f32[288,128]{1,0:T(8,128)S(1)}, u32[]{:S(2)}, u32[]{:S(2)}) collective-permute-start(f32[288,128]{1,0:T(8,128)S(1)} %get-tuple-element.210), channel_id=1, source_target_pairs={{0,32},{32,64},{64,96},{96,128},{128,160},{160,192},{192,224},{1,3... | collective-permute-start | bytes 442376 | tf_op jit(solution)/shard_map/ppermute | solution.py:141
  56.1 10.2 %collective-permute-start.13 = (f32[288,128]{1,0:T(8,128)S(1)}, f32[288,128]{1,0:T(8,128)S(1)}, u32[]{:S(2)}, u32[]{:S(2)}) collective-permute-start(f32[288,128]{1,0:T(8,128)S(1)} %get-tuple-element.211), channel_id=1, source_target_pairs={{32,0},{64,32},{96,64},{128,96},{160,128},{192,160},{224,192},{33,... | collective-permute-start | bytes 442376 | tf_op jit(solution)/shard_map/ppermute | solution.py:141
  58.5 7.8 %collective-permute-start.11 = (f32[176,128]{1,0:T(8,128)S(1)}, f32[176,128]{1,0:T(8,128)S(1)}, u32[]{:S(2)}, u32[]{:S(2)}) collective-permute-start(f32[176,128]{1,0:T(8,128)S(1)} %add.57), channel_id=1, source_target_pairs={{32,40},{33,41},{34,42},{35,43},{36,44},{37,45},{38,46},{39,47},{4... | collective-permute-start | bytes 270344 | tf_op jit(solution)/shard_map/ppermute | solution.py:426
  66.3 6.8 %collective-permute-start.14 = (f32[176,128]{1,0:T(8,128)S(1)}, f32[176,128]{1,0:T(8,128)S(1)}, u32[]{:S(2)}, u32[]{:S(2)}) collective-permute-start(f32[176,128]{1,0:T(8,128)S(1)} %add.58), channel_id=1, source_target_pairs={{32,56},{33,57},{34,58},{35,59},{36,60},{37,61},{38,62},{39,63},{4... | collective-permute-start | bytes 270344 | tf_op jit(solution)/shard_map/ppermute | solution.py:426
  73.2 5.3 %collective-permute-start.15 = (f32[176,128]{1,0:T(8,128)S(1)}, f32[176,128]{1,0:T(8,128)S(1)}, u32[]{:S(2)}, u32[]{:S(2)}) collective-permute-start(f32[176,128]{1,0:T(8,128)S(1)} %add.59), channel_id=1, source_target_pairs={{32,33},{33,32},{34,35},{35,34},{36,37},{37,36},{38,39},{39,38},{4... | collective-permute-start | bytes 270344 | tf_op jit(solution)/shard_map/ppermute | solution.py:426
  78.5 7.6 %collective-permute-start.16 = (f32[176,128]{1,0:T(8,128)S(1)}, f32[176,128]{1,0:T(8,128)S(1)}, u32[]{:S(2)}, u32[]{:S(2)}) collective-permute-start(f32[176,128]{1,0:T(8,128)S(1)} %add.60), channel_id=1, source_target_pairs={{32,39},{33,34},{34,33},{35,36},{36,35},{37,38},{38,37},{39,32},{4... | collective-permute-start | bytes 270344 | tf_op jit(solution)/shard_map/ppermute | solution.py:426
  86.0 7.1 %collective-permute-start.17 = (f32[176,128]{1,0:T(8,128)S(1)}, f32[176,128]{1,0:T(8,128)S(1)}, u32[]{:S(2)}, u32[]{:S(2)}) collective-permute-start(f32[176,128]{1,0:T(8,128)S(1)} %add.61), channel_id=1, source_target_pairs={{32,35},{33,38},{34,37},{35,32},{36,39},{37,34},{38,33},{39,36},{4... | collective-permute-start | bytes 270344 | tf_op jit(solution)/shard_map/ppermute | solution.py:426
  93.2 6.5 %collective-permute-start.18 = (f32[176,128]{1,0:T(8,128)S(1)}, f32[176,128]{1,0:T(8,128)S(1)}, u32[]{:S(2)}, u32[]{:S(2)}) collective-permute-start(f32[176,128]{1,0:T(8,128)S(1)} %add.62), channel_id=1, source_target_pairs={{32,224},{96,160},{160,96},{224,32},{33,225},{97,161},{161,97},{22... | collective-permute-start | bytes 270344 | tf_op jit(solution)/shard_map/ppermute | solution.py:426
  95.1 4.6 %collective-permute-start.19 = (f32[96,128]{1,0:T(8,128)S(1)}, f32[96,128]{1,0:T(8,128)S(1)}, u32[]{:S(2)}, u32[]{:S(2)}) collective-permute-start(f32[96,128]{1,0:T(8,128)S(1)} %get-tuple-element.243), channel_id=1, source_target_pairs={{0,1},{1,2},{2,3},{3,4},{4,5},{5,6},{6,7},{7,8},{8,9},{9,10},{10,1... | collective-permute-start | bytes 147464 | tf_op jit(solution)/shard_map/ppermute | solution.py:141
  97.1 4.8 %collective-permute-start.20 = (f32[96,128]{1,0:T(8,128)S(1)}, f32[96,128]{1,0:T(8,128)S(1)}, u32[]{:S(2)}, u32[]{:S(2)}) collective-permute-start(f32[96,128]{1,0:T(8,128)S(1)} %get-tuple-element.244), channel_id=1, source_target_pairs={{1,0},{2,1},{3,2},{4,3},{5,4},{6,5},{7,6},{8,7},{9,8},{10,9},{11,1... | collective-permute-start | bytes 147464 | tf_op jit(solution)/shard_map/ppermute | solution.py:141
  102.0 6.2 %collective-permute-start.21 = (f32[352,128]{1,0:T(8,128)S(1)}, f32[352,128]{1,0:T(8,128)S(1)}, u32[]{:S(2)}, u32[]{:S(2)}) collective-permute-start(f32[352,128]{1,0:T(8,128)S(1)} %maximum_select_fusion.2), channel_id=1, source_target_pairs={{32,96},{96,32},{160,224},{224,160},{33,97},{97,33},{161,225},{225... | collective-permute-start | bytes 540680 | tf_op jit(solution)/shard_map/ppermute | solution.py:426
  108.2 2.6 %collective-permute-start.22 = (f32[704,128]{1,0:T(8,128)S(1)}, f32[704,128]{1,0:T(8,128)S(1)}, u32[]{:S(2)}, u32[]{:S(2)}) collective-permute-start(f32[704,128]{1,0:T(8,128)S(1)} %maximum_select_fusion), channel_id=1, source_target_pairs={{32,0},{96,64},{160,128},{224,192},{33,1},{97,65},{161,129},{225,1... | collective-permute-start | bytes 1081352 | tf_op jit(solution)/shard_map/ppermute | solution.py:426
  113.4 6.9 %collective-permute-start.23 = (f32[704,128]{1,0:T(8,128)S(1)}, f32[704,128]{1,0:T(8,128)S(1)}, u32[]{:S(2)}, u32[]{:S(2)}) collective-permute-start(f32[704,128]{1,0:T(8,128)S(1)} %get-tuple-element.267), channel_id=1, source_target_pairs={{0,32},{64,96},{128,160},{192,224},{1,33},{65,97},{129,161},{193,2... | collective-permute-start | bytes 1081352 | tf_op jit(solution)/shard_map/ppermute | solution.py:426
  114.7 5.7 %collective-permute-start.24 = (f32[48,128]{1,0:T(8,128)S(1)}, f32[48,128]{1,0:T(8,128)S(1)}, u32[]{:S(2)}, u32[]{:S(2)}) collective-permute-start(f32[48,128]{1,0:T(8,128)S(1)} %get-tuple-element.269), channel_id=1, source_target_pairs={{0,32},{32,64},{64,96},{96,128},{128,160},{160,192},{192,224},{1,3... | collective-permute-start | bytes 73736 | tf_op jit(solution)/shard_map/ppermute | solution.py:141
  118.4 5.1 %collective-permute-start.25 = (f32[48,128]{1,0:T(8,128)S(1)}, f32[48,128]{1,0:T(8,128)S(1)}, u32[]{:S(2)}, u32[]{:S(2)}) collective-permute-start(f32[48,128]{1,0:T(8,128)S(1)} %get-tuple-element.270), channel_id=1, source_target_pairs={{32,0},{64,32},{96,64},{128,96},{160,128},{192,160},{224,192},{33,... | collective-permute-start | bytes 73736 | tf_op jit(solution)/shard_map/ppermute | solution.py:141
  123.6 6.2 %collective-permute-start.26 = (f32[352,128]{1,0:T(8,128)S(1)}, f32[352,128]{1,0:T(8,128)S(1)}, u32[]{:S(2)}, u32[]{:S(2)}) collective-permute-start(f32[352,128]{1,0:T(8,128)S(1)} %get-tuple-element.274), channel_id=1, source_target_pairs={{32,96},{96,32},{160,224},{224,160},{33,97},{97,33},{161,225},{225... | collective-permute-start | bytes 540680 | tf_op jit(solution)/shard_map/ppermute | solution.py:426
  129.8 6.5 %collective-permute-start.27 = (f32[176,128]{1,0:T(8,128)S(1)}, f32[176,128]{1,0:T(8,128)S(1)}, u32[]{:S(2)}, u32[]{:S(2)}) collective-permute-start(f32[176,128]{1,0:T(8,128)S(1)} %get-tuple-element.281), channel_id=1, source_target_pairs={{32,224},{96,160},{160,96},{224,32},{33,225},{97,161},{161,97},{22... | collective-permute-start | bytes 270344 | tf_op jit(solution)/shard_map/ppermute | solution.py:426
  136.3 7.2 %collective-permute-start.28 = (f32[176,128]{1,0:T(8,128)S(1)}, f32[176,128]{1,0:T(8,128)S(1)}, u32[]{:S(2)}, u32[]{:S(2)}) collective-permute-start(f32[176,128]{1,0:T(8,128)S(1)} %add.65), channel_id=1, source_target_pairs={{32,40},{33,41},{34,42},{35,43},{36,44},{37,45},{38,46},{39,47},{4... | collective-permute-start | bytes 270344 | tf_op jit(solution)/shard_map/ppermute | solution.py:426
  140.9 2.7 %collective-permute-start.29 = (f32[16,128]{1,0:T(8,128)S(1)}, f32[16,128]{1,0:T(8,128)S(1)}, u32[]{:S(2)}, u32[]{:S(2)}) collective-permute-start(f32[16,128]{1,0:T(8,128)S(1)} %get-tuple-element.292), channel_id=1, source_target_pairs={{0,1},{1,2},{2,3},{3,4},{4,5},{5,6},{6,7},{7,8},{8,9},{9,10},{10,1... | collective-permute-start | bytes 24584 | tf_op jit(solution)/shard_map/ppermute | solution.py:141
  142.2 4.4 %collective-permute-start.30 = (f32[16,128]{1,0:T(8,128)S(1)}, f32[16,128]{1,0:T(8,128)S(1)}, u32[]{:S(2)}, u32[]{:S(2)}) collective-permute-start(f32[16,128]{1,0:T(8,128)S(1)} %get-tuple-element.293), channel_id=1, source_target_pairs={{1,0},{2,1},{3,2},{4,3},{5,4},{6,5},{7,6},{8,7},{9,8},{10,9},{11,1... | collective-permute-start | bytes 24584 | tf_op jit(solution)/shard_map/ppermute | solution.py:141
  146.6 7.7 %collective-permute-start.31 = (f32[176,128]{1,0:T(8,128)S(1)}, f32[176,128]{1,0:T(8,128)S(1)}, u32[]{:S(2)}, u32[]{:S(2)}) collective-permute-start(f32[176,128]{1,0:T(8,128)S(1)} %add.66), channel_id=1, source_target_pairs={{32,56},{33,57},{34,58},{35,59},{36,60},{37,61},{38,62},{39,63},{4... | collective-permute-start | bytes 270344 | tf_op jit(solution)/shard_map/ppermute | solution.py:426
  154.3 5.3 %collective-permute-start.32 = (f32[176,128]{1,0:T(8,128)S(1)}, f32[176,128]{1,0:T(8,128)S(1)}, u32[]{:S(2)}, u32[]{:S(2)}) collective-permute-start(f32[176,128]{1,0:T(8,128)S(1)} %add.67), channel_id=1, source_target_pairs={{32,33},{33,32},{34,35},{35,34},{36,37},{37,36},{38,39},{39,38},{4... | collective-permute-start | bytes 270344 | tf_op jit(solution)/shard_map/ppermute | solution.py:426
  159.6 8.5 %collective-permute-start.33 = (f32[176,128]{1,0:T(8,128)S(1)}, f32[176,128]{1,0:T(8,128)S(1)}, u32[]{:S(2)}, u32[]{:S(2)}) collective-permute-start(f32[176,128]{1,0:T(8,128)S(1)} %add.68), channel_id=1, source_target_pairs={{32,39},{33,34},{34,33},{35,36},{36,35},{37,38},{38,37},{39,32},{4... | collective-permute-start | bytes 270344 | tf_op jit(solution)/shard_map/ppermute | solution.py:426
  168.2 7.3 %collective-permute-start.34 = (f32[176,128]{1,0:T(8,128)S(1)}, f32[176,128]{1,0:T(8,128)S(1)}, u32[]{:S(2)}, u32[]{:S(2)}) collective-permute-start(f32[176,128]{1,0:T(8,128)S(1)} %add.69), channel_id=1, source_target_pairs={{32,35},{33,38},{34,37},{35,32},{36,39},{37,34},{38,33},{39,36},{4... | collective-permute-start | bytes 270344 | tf_op jit(solution)/shard_map/ppermute | solution.py:426
  175.4 6.5 %collective-permute-start.35 = (f32[176,128]{1,0:T(8,128)S(1)}, f32[176,128]{1,0:T(8,128)S(1)}, u32[]{:S(2)}, u32[]{:S(2)}) collective-permute-start(f32[176,128]{1,0:T(8,128)S(1)} %add.70), channel_id=1, source_target_pairs={{32,224},{96,160},{160,96},{224,32},{33,225},{97,161},{161,97},{22... | collective-permute-start | bytes 270344 | tf_op jit(solution)/shard_map/ppermute | solution.py:426
  181.9 6.2 %collective-permute-start.36 = (f32[352,128]{1,0:T(8,128)S(1)}, f32[352,128]{1,0:T(8,128)S(1)}, u32[]{:S(2)}, u32[]{:S(2)}) collective-permute-start(f32[352,128]{1,0:T(8,128)S(1)} %maximum_select_fusion.3), channel_id=1, source_target_pairs={{32,96},{96,32},{160,224},{224,160},{33,97},{97,33},{161,225},{225... | collective-permute-start | bytes 540680 | tf_op jit(solution)/shard_map/ppermute | solution.py:426
  188.2 2.6 %collective-permute-start.37 = (f32[704,128]{1,0:T(8,128)S(1)}, f32[704,128]{1,0:T(8,128)S(1)}, u32[]{:S(2)}, u32[]{:S(2)}) collective-permute-start(f32[704,128]{1,0:T(8,128)S(1)} %maximum_select_fusion.1), channel_id=1, source_target_pairs={{32,0},{96,64},{160,128},{224,192},{33,1},{97,65},{161,129},{225,1... | collective-permute-start | bytes 1081352 | tf_op jit(solution)/shard_map/ppermute | solution.py:426

commit v3 on v2

--- a/solution.py
+++ b/solution.py
@@ -383,15 +383,13 @@
 
 
 THIRD = {2: 5, 5: 2, 1: 6, 6: 1, 3: 0, 0: 3, 4: 7, 7: 4}
-INWARD = [(2 * y, 2 * y + 1) for y in range(4)]
-OUTWARD = [(2 * y + 1, 2 * y) for y in range(4)]
-Y_EVEN = [(2 * y + 1, 2 * swap_even(y) + 1) for y in range(4)]
-Y_ODD = [(2 * y + 1, 2 * swap_odd(y, 4) + 1) for y in range(4)]
+CORE = [(i, i ^ 1) for i in range(8)]
+Y_EVEN = [(2 * y + core, 2 * swap_even(y) + core) for y in range(4) for core in range(2)]
+Y_ODD = [(2 * y + core, 2 * swap_odd(y, 4) + core) for y in range(4) for core in range(2)]
 
 
 def pairs_col(change):
-    pairs = [(8 * x + z, change(x, z)) for x in range(4) for z in range(8)]
-    return [(32 * row + i, 32 * row + j) for row in (1, 3, 5, 7) for i, j in pairs]
+    return [(8 * x + z, change(x, z)) for x in range(4) for z in range(8)]
 
 
 COLS = [
@@ -417,31 +415,29 @@
     row = lax.axis_index("row")
     y = row // 2
     upper = (y == 1) | (y == 2)
-    later = (y == 2) | (y == 3)
+    odd_core = row % 2 == 1
     value = grad
 
-    def beside(k, sent, axes, pairs, kept):
+    def beside(k, sent, axis, pairs, kept):
         nonlocal state
         sent, kept, state = lax.optimization_barrier((sent, kept, state))
-        other = lax.ppermute(sent, axes, pairs)
+        other = lax.ppermute(sent, axis, pairs)
         if k in side:
             state = side[k](state)
         return kept, other
 
-    kept, other = beside(0, value, "row", INWARD, value)
-    value = kept + other
-    for k, bit, pairs in ((1, upper, Y_EVEN), (2, later, Y_ODD)):
+    for k, bit, pairs in ((0, odd_core, CORE), (1, upper, Y_EVEN)):
         sent, kept = halves(value, bit)
         kept, other = beside(k, sent, "row", pairs, kept)
         value = kept + other
-    for k, pairs in enumerate(COLS):
-        kept, other = beside(3 + k, value, ("row", "col"), pairs, value)
+    steps = [("row", Y_ODD)] + [("col", pairs) for pairs in COLS]
+    for k, (axis, pairs) in enumerate(steps):
+        kept, other = beside(2 + k, value, axis, pairs, value)
         value = kept + other
-    for k, bit, pairs in ((8, later, Y_ODD), (9, upper, Y_EVEN)):
+    for k, bit, pairs in ((8, upper, Y_EVEN), (9, odd_core, CORE)):
         kept, other = beside(k, value, "row", pairs, value)
         value = joined(kept, other, bit)
-    kept, other = beside(10, value, "row", OUTWARD, value)
-    return jnp.where(row % 2 == 0, other, kept), state
+    return value, state
 
 
 def local(observed, coef_maps, dictionary, consensus, dual_vars):
@@ -495,7 +491,7 @@
             2: threshold(False, map_rows),
             3: map_rows_out,
             5: map_pack,
-            8: map_columns,
+            7: map_columns,
         },
     )
     filt, cons, duals, resid, r_top, r_bottom, grad = call(
@@ -504,7 +500,7 @@
     summed, new_maps = sum_all(
         grad,
         (resid, r_top, r_bottom, filt, maps),
-        {0: resid_rows, 3: resid_columns, 5: threshold(True, shape(M, ROWS, LANES))},
+        {2: resid_rows, 7: resid_columns, 8: threshold(True, shape(M, ROWS, LANES))},
     )
     new = call(
         last_kernel,

time: 196 us -> 159 us (0.81)
  starting transfers between devices: 111 us -> 83.4 us
  waiting for transfers between devices: 64.7 us -> 55.7 us
    ppermute x22 -> x20, starting transfers between devices: 72.4 us -> 46.3 us  [beside(): other = lax.ppermute(sent, axis, pairs)]
    ppermute x22 -> x20, waiting for transfers between devices: 43.6 us -> 32.9 us  [beside(): other = lax.ppermute(sent, axis, pairs)]
  transfers between devices with their start and end apart: 38 -> 36, of which waited for: 26 -> 23; matrix products, arithmetic and copies ran while one was open for 0% -> 0% of each run, Pallas kernels for 4% -> 4%
where the time goes in v3:
time: 159 us; the launch traced here: 158 us
  starting transfers between devices  83.4 us (52%)
  waiting for transfers between devices  55.7 us (35%)
  Pallas kernels  16.8 us (11%)
    ppermute x20, starting transfers between devices, beside(): other = lax.ppermute(sent, axis, pairs)  46.3 us
    ppermute x20, waiting for transfers between devices, beside(): other = lax.ppermute(sent, axis, pairs)  32.9 us
    ppermute x8, starting transfers between devices, neighbours(): lax.ppermute(toward_high, axis, up)  23.9 us
    ppermute x8, waiting for transfers between devices, neighbours(): lax.ppermute(toward_low, axis, down)  22.6 us
    ppermute x8, starting transfers between devices, neighbours(): lax.ppermute(toward_low, axis, down)  13.3 us
    pallas_call x1, Pallas kernels, local(): call(last_kernel, [shape(M, FLAT)] * 3, [pltpu.VMEM((3, D_ROWS, LANES), F...  4.17 us
    pallas_call x2, Pallas kernels, run(): call(functools.partial(corr_kernel, last), outs, CORR_SCRATCH)  3.21 us
  transfers between devices with their start and end apart: 36, of which 23 were waited for; matrix products, arithmetic and copies ran while one was open for 0% of the time, Pallas kernels for 4%

profile of v3, /device:TPU:1, one launch (start us, length us, event | category | flops | bytes accessed | tf_op | source)
XLA Modules:
  0.0 158.4 jit_solution(3880781259443525425)
XLA Ops:
  0.6 1.0 copy-done
  1.6 0.2 shard_map.84
  1.9 4.6 %collective-permute-start = (f32[288,128]{1,0:T(8,128)S(1)}, f32[288,128]{1,0:T(8,128)S(1)}, u32[]{:S(2)}, u32[]{:S(2)}) collective-permute-start(f32[288,128]{1,0:T(8,128)S(1)} %get-tuple-element.170), channel_id=1, source_target_pairs={{0,32},{32,64},{64,96},{96,128},{128,160},{160,192},{192,224},{1,3... | collective-permute-start | bytes 442376 | tf_op jit(solution)/shard_map/ppermute | solution.py:141
  6.5 1.9 %collective-permute-start.1 = (f32[288,128]{1,0:T(8,128)S(1)}, f32[288,128]{1,0:T(8,128)S(1)}, u32[]{:S(2)}, u32[]{:S(2)}) collective-permute-start(f32[288,128]{1,0:T(8,128)S(1)} %get-tuple-element.171), channel_id=1, source_target_pairs={{32,0},{64,32},{96,64},{128,96},{160,128},{192,160},{224,192},{33,... | collective-permute-start | bytes 442376 | tf_op jit(solution)/shard_map/ppermute | solution.py:141
  8.5 4.4 %collective-permute-done.1.below = f32[288,128]{1,0:T(8,128)S(1)} collective-permute-done((f32[288,128]{1,0:T(8,128)S(1)}, f32[288,128]{1,0:T(8,128)S(1)}, u32[]{:S(2)}, u32[]{:S(2)}) %collective-permute-start.1) | collective-permute-done | bytes 147488 | tf_op jit(solution)/shard_map/ppermute | solution.py:141
  12.9 0.4 shard_map.85
  13.3 3.5 %collective-permute-start.2 = (f32[96,128]{1,0:T(8,128)S(1)}, f32[96,128]{1,0:T(8,128)S(1)}, u32[]{:S(2)}, u32[]{:S(2)}) collective-permute-start(f32[96,128]{1,0:T(8,128)S(1)} %get-tuple-element.172), channel_id=1, source_target_pairs={{0,1},{1,2},{2,3},{3,4},{4,5},{5,6},{6,7},{7,8},{8,9},{9,10},{10,1... | collective-permute-start | bytes 147464 | tf_op jit(solution)/shard_map/ppermute | solution.py:141
  16.9 1.3 collective-permute-start.3
  18.2 3.0 %shard_map.86 = (f32[672,128]{1,0:T(8,128)S(1)}, f32[672,128]{1,0:T(8,128)S(1)}, f32[672,128]{1,0:T(8,128)S(1)}) custom-call(f32[96,784]{1,0:T(8,128)S(1)} %copy-done.1, f32[96,784]{1,0:T(8,128)S(1)} %copy-done.2, f32[96,784]{1,0:T(8,128)S(1)} %copy-done.3), custom_call_target="tpu_custom_call" | custom-call | tf_op jit(solution)/shard_map/pallas_call | solution.py:447
  21.3 0.6 collective-permute-done.3.right
  21.9 2.5 %shard_map.87 = (f32[128,128]{1,0:T(8,128)S(1)}, f32[48,128]{1,0:T(8,128)S(1)}, f32[48,128]{1,0:T(8,128)S(1)}, f32[704,128]{1,0:T(8,128)S(1)}) custom-call(f32[768,128]{1,0:T(8,128)S(1)} %get-tuple-element.203.own.maps, f32[288,128]{1,0:T(8,128)S(1)} %collective-permute-done.above, f32[288,128]{1,0:T(8,128)S(1)} %collective-permute-done.1.below, ...), custom_call_target="tpu_custom_call" | custom-call | tf_op jit(solution)/shard_map/pallas_call | solution.py:451
  24.6 3.6 %collective-permute-start.5 = (f32[48,128]{1,0:T(8,128)S(1)}, f32[48,128]{1,0:T(8,128)S(1)}, u32[]{:S(2)}, u32[]{:S(2)}) collective-permute-start(f32[48,128]{1,0:T(8,128)S(1)} %get-tuple-element.182), channel_id=1, source_target_pairs={{0,32},{32,64},{64,96},{96,128},{128,160},{160,192},{192,224},{1,3... | collective-permute-start | bytes 73736 | tf_op jit(solution)/shard_map/ppermute | solution.py:141
  28.2 1.9 %collective-permute-start.6 = (f32[48,128]{1,0:T(8,128)S(1)}, f32[48,128]{1,0:T(8,128)S(1)}, u32[]{:S(2)}, u32[]{:S(2)}) collective-permute-start(f32[48,128]{1,0:T(8,128)S(1)} %get-tuple-element.183), channel_id=1, source_target_pairs={{32,0},{64,32},{96,64},{128,96},{160,128},{192,160},{224,192},{33,... | collective-permute-start | bytes 73736 | tf_op jit(solution)/shard_map/ppermute | solution.py:141
  30.2 3.1 %collective-permute-done.6.below = f32[48,128]{1,0:T(8,128)S(1)} collective-permute-done((f32[48,128]{1,0:T(8,128)S(1)}, f32[48,128]{1,0:T(8,128)S(1)}, u32[]{:S(2)}, u32[]{:S(2)}) %collective-permute-start.6) | collective-permute-done | bytes 24608 | tf_op jit(solution)/shard_map/ppermute | solution.py:141
  33.3 1.0 collective-permute-start.7
  34.5 3.5 %collective-permute-start.8 = (f32[16,128]{1,0:T(8,128)S(1)}, f32[16,128]{1,0:T(8,128)S(1)}, u32[]{:S(2)}, u32[]{:S(2)}) collective-permute-start(f32[16,128]{1,0:T(8,128)S(1)} %get-tuple-element.191), channel_id=1, source_target_pairs={{0,1},{1,2},{2,3},{3,4},{4,5},{5,6},{6,7},{7,8},{8,9},{9,10},{10,1... | collective-permute-start | bytes 24584 | tf_op jit(solution)/shard_map/ppermute | solution.py:141
  38.0 1.3 collective-permute-start.9
  39.4 4.6 %collective-permute-done.9.right = f32[16,128]{1,0:T(8,128)S(1)} collective-permute-done((f32[16,128]{1,0:T(8,128)S(1)}, f32[16,128]{1,0:T(8,128)S(1)}, u32[]{:S(2)}, u32[]{:S(2)}) %collective-permute-start.9) | collective-permute-done | bytes 8224 | tf_op jit(solution)/shard_map/ppermute | solution.py:141
  43.9 1.1 collective-permute-start.10
  45.0 1.2 shard_map.89
  46.2 2.7 %collective-permute-done.10 = f32[176,128]{1,0:T(8,128)S(1)} collective-permute-done((f32[176,128]{1,0:T(8,128)S(1)}, f32[176,128]{1,0:T(8,128)S(1)}, u32[]{:S(2)}, u32[]{:S(2)}) %collective-permute-start.10) | collective-permute-done | bytes 90144 | tf_op jit(solution)/shard_map/ppermute | solution.py:424
  49.0 2.1 %collective-permute-start.12 = (f32[288,128]{1,0:T(8,128)S(1)}, f32[288,128]{1,0:T(8,128)S(1)}, u32[]{:S(2)}, u32[]{:S(2)}) collective-permute-start(f32[288,128]{1,0:T(8,128)S(1)} %get-tuple-element.210), channel_id=1, source_target_pairs={{0,32},{32,64},{64,96},{96,128},{128,160},{160,192},{192,224},{1,3... | collective-permute-start | bytes 442376 | tf_op jit(solution)/shard_map/ppermute | solution.py:141
  51.1 2.3 %collective-permute-start.13 = (f32[288,128]{1,0:T(8,128)S(1)}, f32[288,128]{1,0:T(8,128)S(1)}, u32[]{:S(2)}, u32[]{:S(2)}) collective-permute-start(f32[288,128]{1,0:T(8,128)S(1)} %get-tuple-element.211), channel_id=1, source_target_pairs={{32,0},{64,32},{96,64},{128,96},{160,128},{192,160},{224,192},{33,... | collective-permute-start | bytes 442376 | tf_op jit(solution)/shard_map/ppermute | solution.py:141
  53.4 3.9 %collective-permute-start.11 = (f32[176,128]{1,0:T(8,128)S(1)}, f32[176,128]{1,0:T(8,128)S(1)}, u32[]{:S(2)}, u32[]{:S(2)}) collective-permute-start(f32[176,128]{1,0:T(8,128)S(1)} %add.57), channel_id=1, source_target_pairs={{0,8},{1,9},{2,10},{3,11},{4,12},{5,13},{6,14},{7,15},{8,0},{9,1},... | collective-permute-start | bytes 270344 | tf_op jit(solution)/shard_map/ppermute | solution.py:424
  57.3 2.4 %collective-permute-done.11 = f32[176,128]{1,0:T(8,128)S(1)} collective-permute-done((f32[176,128]{1,0:T(8,128)S(1)}, f32[176,128]{1,0:T(8,128)S(1)}, u32[]{:S(2)}, u32[]{:S(2)}) %collective-permute-start.11) | collective-permute-done | bytes 90144 | tf_op jit(solution)/shard_map/ppermute | solution.py:424
  59.8 3.5 %collective-permute-start.14 = (f32[176,128]{1,0:T(8,128)S(1)}, f32[176,128]{1,0:T(8,128)S(1)}, u32[]{:S(2)}, u32[]{:S(2)}) collective-permute-start(f32[176,128]{1,0:T(8,128)S(1)} %add.58), channel_id=1, source_target_pairs={{0,24},{1,25},{2,26},{3,27},{4,28},{5,29},{6,30},{7,31},{8,16},{9,... | collective-permute-start | bytes 270344 | tf_op jit(solution)/shard_map/ppermute | solution.py:424
  63.4 2.7 %collective-permute-done.14 = f32[176,128]{1,0:T(8,128)S(1)} collective-permute-done((f32[176,128]{1,0:T(8,128)S(1)}, f32[176,128]{1,0:T(8,128)S(1)}, u32[]{:S(2)}, u32[]{:S(2)}) %collective-permute-start.14) | collective-permute-done | bytes 90144 | tf_op jit(solution)/shard_map/ppermute | solution.py:424
  66.1 0.4 shard_map.90
  66.5 3.0 %collective-permute-done.15 = f32[176,128]{1,0:T(8,128)S(1)} collective-permute-done((f32[176,128]{1,0:T(8,128)S(1)}, f32[176,128]{1,0:T(8,128)S(1)}, u32[]{:S(2)}, u32[]{:S(2)}) %collective-permute-start.15) | collective-permute-done | bytes 90144 | tf_op jit(solution)/shard_map/ppermute | solution.py:424
  69.5 3.8 %collective-permute-start.16 = (f32[176,128]{1,0:T(8,128)S(1)}, f32[176,128]{1,0:T(8,128)S(1)}, u32[]{:S(2)}, u32[]{:S(2)}) collective-permute-start(f32[176,128]{1,0:T(8,128)S(1)} %add.60), channel_id=1, source_target_pairs={{0,7},{1,2},{2,1},{3,4},{4,3},{5,6},{6,5},{7,0},{8,15},{9,10},{10,... | collective-permute-start | bytes 270344 | tf_op jit(solution)/shard_map/ppermute | solution.py:424
  73.3 1.9 %collective-permute-done.16 = f32[176,128]{1,0:T(8,128)S(1)} collective-permute-done((f32[176,128]{1,0:T(8,128)S(1)}, f32[176,128]{1,0:T(8,128)S(1)}, u32[]{:S(2)}, u32[]{:S(2)}) %collective-permute-start.16) | collective-permute-done | bytes 90144 | tf_op jit(solution)/shard_map/ppermute | solution.py:424
  75.3 2.6 %collective-permute-start.17 = (f32[176,128]{1,0:T(8,128)S(1)}, f32[176,128]{1,0:T(8,128)S(1)}, u32[]{:S(2)}, u32[]{:S(2)}) collective-permute-start(f32[176,128]{1,0:T(8,128)S(1)} %add.61), channel_id=1, source_target_pairs={{0,3},{1,6},{2,5},{3,0},{4,7},{5,2},{6,1},{7,4},{8,11},{9,14},{10,... | collective-permute-start | bytes 270344 | tf_op jit(solution)/shard_map/ppermute | solution.py:424
  77.8 2.0 %collective-permute-start.18 = (f32[96,128]{1,0:T(8,128)S(1)}, f32[96,128]{1,0:T(8,128)S(1)}, u32[]{:S(2)}, u32[]{:S(2)}) collective-permute-start(f32[96,128]{1,0:T(8,128)S(1)} %get-tuple-element.236), channel_id=1, source_target_pairs={{0,1},{1,2},{2,3},{3,4},{4,5},{5,6},{6,7},{7,8},{8,9},{9,10},{10,1... | collective-permute-start | bytes 147464 | tf_op jit(solution)/shard_map/ppermute | solution.py:141
  79.8 1.3 collective-permute-start.19
  81.1 3.7 %collective-permute-done.19.right = f32[96,128]{1,0:T(8,128)S(1)} collective-permute-done((f32[96,128]{1,0:T(8,128)S(1)}, f32[96,128]{1,0:T(8,128)S(1)}, u32[]{:S(2)}, u32[]{:S(2)}) %collective-permute-start.19) | collective-permute-done | bytes 49184 | tf_op jit(solution)/shard_map/ppermute | solution.py:141
  84.8 0.3 collective-permute-start.20
  85.2 3.0 %collective-permute-done.20 = f32[176,128]{1,0:T(8,128)S(1)} collective-permute-done((f32[176,128]{1,0:T(8,128)S(1)}, f32[176,128]{1,0:T(8,128)S(1)}, u32[]{:S(2)}, u32[]{:S(2)}) %collective-permute-start.20) | collective-permute-done | bytes 90144 | tf_op jit(solution)/shard_map/ppermute | solution.py:424
  88.2 6.0 %collective-permute-start.21 = (f32[352,128]{1,0:T(8,128)S(1)}, f32[352,128]{1,0:T(8,128)S(1)}, u32[]{:S(2)}, u32[]{:S(2)}) collective-permute-start(f32[352,128]{1,0:T(8,128)S(1)} %maximum_select_fusion.2), channel_id=1, source_target_pairs={{0,32},{32,0},{64,96},{96,64},{128,160},{160,128},{192,224},{224,1... | collective-permute-start | bytes 540680 | tf_op jit(solution)/shard_map/ppermute | solution.py:424
  94.2 1.0 collective-permute-done.21
  95.3 2.6 %shard_map.91 = (f32[672,128]{1,0:T(8,128)S(1)}, f32[672,128]{1,0:T(8,128)S(1)}, f32[672,128]{1,0:T(8,128)S(1)}, f32[128,128]{1,0:T(8,128)S(1)}, f32[48,128]{1,0...) custom-call(f32[704,128]{1,0:T(8,128)S(1)} %maximum_select_fusion.summed, ...), custom_call_target="tpu_custom_call" | custom-call | tf_op jit(solution)/shard_map/pallas_call | solution.py:497
  97.9 0.5 collective-permute-start.22
  98.4 1.0 collective-permute-done.22
  99.5 1.5 collective-permute-start.23
  101.0 2.4 %collective-permute-done.23 = f32[176,128]{1,0:T(8,128)S(1)} collective-permute-done((f32[176,128]{1,0:T(8,128)S(1)}, f32[176,128]{1,0:T(8,128)S(1)}, u32[]{:S(2)}, u32[]{:S(2)}) %collective-permute-start.23) | collective-permute-done | bytes 90144 | tf_op jit(solution)/shard_map/ppermute | solution.py:424
  103.4 3.7 %collective-permute-start.24 = (f32[176,128]{1,0:T(8,128)S(1)}, f32[176,128]{1,0:T(8,128)S(1)}, u32[]{:S(2)}, u32[]{:S(2)}) collective-permute-start(f32[176,128]{1,0:T(8,128)S(1)} %add.64), channel_id=1, source_target_pairs={{0,192},{32,224},{64,128},{96,160},{128,64},{160,96},{192,0},{224,... | collective-permute-start | bytes 270344 | tf_op jit(solution)/shard_map/ppermute | solution.py:424
  107.2 2.9 %collective-permute-start.25 = (f32[48,128]{1,0:T(8,128)S(1)}, f32[48,128]{1,0:T(8,128)S(1)}, u32[]{:S(2)}, u32[]{:S(2)}) collective-permute-start(f32[48,128]{1,0:T(8,128)S(1)} %get-tuple-element.276), channel_id=1, source_target_pairs={{0,32},{32,64},{64,96},{96,128},{128,160},{160,192},{192,224},{1,3... | collective-permute-start | bytes 73736 | tf_op jit(solution)/shard_map/ppermute | solution.py:141
  110.1 1.9 %collective-permute-start.26 = (f32[48,128]{1,0:T(8,128)S(1)}, f32[48,128]{1,0:T(8,128)S(1)}, u32[]{:S(2)}, u32[]{:S(2)}) collective-permute-start(f32[48,128]{1,0:T(8,128)S(1)} %get-tuple-element.277), channel_id=1, source_target_pairs={{32,0},{64,32},{96,64},{128,96},{160,128},{192,160},{224,192},{33,... | collective-permute-start | bytes 73736 | tf_op jit(solution)/shard_map/ppermute | solution.py:141
  112.0 3.2 %collective-permute-done.26.below = f32[48,128]{1,0:T(8,128)S(1)} collective-permute-done((f32[48,128]{1,0:T(8,128)S(1)}, f32[48,128]{1,0:T(8,128)S(1)}, u32[]{:S(2)}, u32[]{:S(2)}) %collective-permute-start.26) | collective-permute-done | bytes 24608 | tf_op jit(solution)/shard_map/ppermute | solution.py:141
  115.2 1.7 %collective-permute-start.27 = (f32[176,128]{1,0:T(8,128)S(1)}, f32[176,128]{1,0:T(8,128)S(1)}, u32[]{:S(2)}, u32[]{:S(2)}) collective-permute-start(f32[176,128]{1,0:T(8,128)S(1)} %add.65), channel_id=1, source_target_pairs={{0,8},{1,9},{2,10},{3,11},{4,12},{5,13},{6,14},{7,15},{8,0},{9,1},... | collective-permute-start | bytes 270344 | tf_op jit(solution)/shard_map/ppermute | solution.py:424
  116.9 1.9 %collective-permute-done.27 = f32[176,128]{1,0:T(8,128)S(1)} collective-permute-done((f32[176,128]{1,0:T(8,128)S(1)}, f32[176,128]{1,0:T(8,128)S(1)}, u32[]{:S(2)}, u32[]{:S(2)}) %collective-permute-start.27) | collective-permute-done | bytes 90144 | tf_op jit(solution)/shard_map/ppermute | solution.py:424
  118.8 4.1 %collective-permute-start.28 = (f32[176,128]{1,0:T(8,128)S(1)}, f32[176,128]{1,0:T(8,128)S(1)}, u32[]{:S(2)}, u32[]{:S(2)}) collective-permute-start(f32[176,128]{1,0:T(8,128)S(1)} %add.66), channel_id=1, source_target_pairs={{0,24},{1,25},{2,26},{3,27},{4,28},{5,29},{6,30},{7,31},{8,16},{9,... | collective-permute-start | bytes 270344 | tf_op jit(solution)/shard_map/ppermute | solution.py:424
  123.0 2.3 %collective-permute-done.28 = f32[176,128]{1,0:T(8,128)S(1)} collective-permute-done((f32[176,128]{1,0:T(8,128)S(1)}, f32[176,128]{1,0:T(8,128)S(1)}, u32[]{:S(2)}, u32[]{:S(2)}) %collective-permute-start.28) | collective-permute-done | bytes 90144 | tf_op jit(solution)/shard_map/ppermute | solution.py:424
  125.3 4.2 %collective-permute-done.29 = f32[176,128]{1,0:T(8,128)S(1)} collective-permute-done((f32[176,128]{1,0:T(8,128)S(1)}, f32[176,128]{1,0:T(8,128)S(1)}, u32[]{:S(2)}, u32[]{:S(2)}) %collective-permute-start.29) | collective-permute-done | bytes 90144 | tf_op jit(solution)/shard_map/ppermute | solution.py:424
  129.5 3.1 %collective-permute-start.30 = (f32[176,128]{1,0:T(8,128)S(1)}, f32[176,128]{1,0:T(8,128)S(1)}, u32[]{:S(2)}, u32[]{:S(2)}) collective-permute-start(f32[176,128]{1,0:T(8,128)S(1)} %add.68), channel_id=1, source_target_pairs={{0,7},{1,2},{2,1},{3,4},{4,3},{5,6},{6,5},{7,0},{8,15},{9,10},{10,... | collective-permute-start | bytes 270344 | tf_op jit(solution)/shard_map/ppermute | solution.py:424
  132.6 1.9 %collective-permute-done.30 = f32[176,128]{1,0:T(8,128)S(1)} collective-permute-done((f32[176,128]{1,0:T(8,128)S(1)}, f32[176,128]{1,0:T(8,128)S(1)}, u32[]{:S(2)}, u32[]{:S(2)}) %collective-permute-start.30) | collective-permute-done | bytes 90144 | tf_op jit(solution)/shard_map/ppermute | solution.py:424
  134.5 3.0 %collective-permute-start.31 = (f32[176,128]{1,0:T(8,128)S(1)}, f32[176,128]{1,0:T(8,128)S(1)}, u32[]{:S(2)}, u32[]{:S(2)}) collective-permute-start(f32[176,128]{1,0:T(8,128)S(1)} %add.69), channel_id=1, source_target_pairs={{0,3},{1,6},{2,5},{3,0},{4,7},{5,2},{6,1},{7,4},{8,11},{9,14},{10,... | collective-permute-start | bytes 270344 | tf_op jit(solution)/shard_map/ppermute | solution.py:424
  137.7 1.7 %collective-permute-start.32 = (f32[16,128]{1,0:T(8,128)S(1)}, f32[16,128]{1,0:T(8,128)S(1)}, u32[]{:S(2)}, u32[]{:S(2)}) collective-permute-start(f32[16,128]{1,0:T(8,128)S(1)} %get-tuple-element.313), channel_id=1, source_target_pairs={{0,1},{1,2},{2,3},{3,4},{4,5},{5,6},{6,7},{7,8},{8,9},{9,10},{10,1... | collective-permute-start | bytes 24584 | tf_op jit(solution)/shard_map/ppermute | solution.py:141
  139.3 1.3 collective-permute-start.33
  140.7 3.1 %collective-permute-done.33.right = f32[16,128]{1,0:T(8,128)S(1)} collective-permute-done((f32[16,128]{1,0:T(8,128)S(1)}, f32[16,128]{1,0:T(8,128)S(1)}, u32[]{:S(2)}, u32[]{:S(2)}) %collective-permute-start.33) | collective-permute-done | bytes 8224 | tf_op jit(solution)/shard_map/ppermute | solution.py:141
  143.7 2.0 %shard_map.93 = f32[96,8,128]{2,1,0:T(8,128)} custom-call(f32[128,128]{1,0:T(8,128)S(1)} %get-tuple-element.319.own.resid, f32[48,128]{1,0:T(8,128)S(1)} %collective-permute-done.25.above, f32[48,128]{1,0:T(8,128)S(1)} %collective-permute-done.26.below, f32[16,128]{1,0:T(8,128)S(1)} %collective-permute-done.32.left, ...), custom_call_target="tpu_custom_call" | custom-call | tf_op jit(solution)/shard_map/pallas_call | solution.py:467
  145.8 1.3 collective-permute-done.34
  147.1 6.0 %collective-permute-start.35 = (f32[352,128]{1,0:T(8,128)S(1)}, f32[352,128]{1,0:T(8,128)S(1)}, u32[]{:S(2)}, u32[]{:S(2)}) collective-permute-start(f32[352,128]{1,0:T(8,128)S(1)} %maximum_select_fusion.3), channel_id=1, source_target_pairs={{0,32},{32,0},{64,96},{96,64},{128,160},{160,128},{192,224},{224,1... | collective-permute-start | bytes 540680 | tf_op jit(solution)/shard_map/ppermute | solution.py:424
  153.2 1.0 collective-permute-done.35
  154.2 4.2 %shard_map.94 = (f32[96,784]{1,0:T(8,128)}, f32[96,784]{1,0:T(8,128)}, f32[96,784]{1,0:T(8,128)}) custom-call(f32[704,128]{1,0:T(8,128)S(1)} %maximum_select_fusion.1.summed, f32[672,128]{1,0:T(8,128)S(1)} %get-tuple-element.324.filt, f32[672,128]{1,0:T(8,128)S(1)} %get-tuple-element.329.cons, f32[672,128]{1,0:T(8,128)S(1)} %get-tuple-element.330.duals), custom_call_target="tpu_custom_call" | custom-call | tf_op jit(solution)/shard_map/pallas_call | solution.py:505
  (53 shorter events, 1.1 us)
Async XLA Ops:
  0.6 1.0 copy-start
  1.6 16.6 %copy-start.3 = (f32[96,784]{1,0:T(8,128)S(1)}, f32[96,784]{1,0:T(8,128)}, u32[]{:S(2)}) copy-start(f32[96,784]{1,0:T(8,128)} %duals.1) | copy-start | bytes 903172
  1.9 6.7 %collective-permute-start = (f32[288,128]{1,0:T(8,128)S(1)}, f32[288,128]{1,0:T(8,128)S(1)}, u32[]{:S(2)}, u32[]{:S(2)}) collective-permute-start(f32[288,128]{1,0:T(8,128)S(1)} %get-tuple-element.170), channel_id=1, source_target_pairs={{0,32},{32,64},{64,96},{96,128},{128,160},{160,192},{192,224},{1,3... | collective-permute-start | bytes 442376 | tf_op jit(solution)/shard_map/ppermute | solution.py:141
  6.5 6.5 %collective-permute-start.1 = (f32[288,128]{1,0:T(8,128)S(1)}, f32[288,128]{1,0:T(8,128)S(1)}, u32[]{:S(2)}, u32[]{:S(2)}) collective-permute-start(f32[288,128]{1,0:T(8,128)S(1)} %get-tuple-element.171), channel_id=1, source_target_pairs={{32,0},{64,32},{96,64},{128,96},{160,128},{192,160},{224,192},{33,... | collective-permute-start | bytes 442376 | tf_op jit(solution)/shard_map/ppermute | solution.py:141
  12.9 5.3 %copy-start.1 = (f32[96,784]{1,0:T(8,128)S(1)}, f32[96,784]{1,0:T(8,128)}, u32[]{:S(2)}) copy-start(f32[96,784]{1,0:T(8,128)} %filt.1) | copy-start | bytes 903172
  12.9 5.3 %copy-start.2 = (f32[96,784]{1,0:T(8,128)S(1)}, f32[96,784]{1,0:T(8,128)}, u32[]{:S(2)}) copy-start(f32[96,784]{1,0:T(8,128)} %cons.1) | copy-start | bytes 903172
  13.3 7.9 %collective-permute-start.2 = (f32[96,128]{1,0:T(8,128)S(1)}, f32[96,128]{1,0:T(8,128)S(1)}, u32[]{:S(2)}, u32[]{:S(2)}) collective-permute-start(f32[96,128]{1,0:T(8,128)S(1)} %get-tuple-element.172), channel_id=1, source_target_pairs={{0,1},{1,2},{2,3},{3,4},{4,5},{5,6},{6,7},{7,8},{8,9},{9,10},{10,1... | collective-permute-start | bytes 147464 | tf_op jit(solution)/shard_map/ppermute | solution.py:141
  16.9 5.0 %collective-permute-start.3 = (f32[96,128]{1,0:T(8,128)S(1)}, f32[96,128]{1,0:T(8,128)S(1)}, u32[]{:S(2)}, u32[]{:S(2)}) collective-permute-start(f32[96,128]{1,0:T(8,128)S(1)} %get-tuple-element.173), channel_id=1, source_target_pairs={{1,0},{2,1},{3,2},{4,3},{5,4},{6,5},{7,6},{8,7},{9,8},{10,9},{11,1... | collective-permute-start | bytes 147464 | tf_op jit(solution)/shard_map/ppermute | solution.py:141
  18.2 3.7 %copy-start.4 = (f32[16,8,128]{2,1,0:T(8,128)S(1)}, f32[16,8,128]{2,1,0:T(8,128)}, u32[]{:S(2)}) copy-start(f32[16,8,128]{2,1,0:T(8,128)} %observed.3) | copy-start | bytes 196612
  24.5 5.6 %collective-permute-start.4 = (f32[352,128]{1,0:T(8,128)S(1)}, f32[352,128]{1,0:T(8,128)S(1)}, u32[]{:S(2)}, u32[]{:S(2)}) collective-permute-start(f32[352,128]{1,0:T(8,128)S(1)} %get-tuple-element.180), channel_id=1, source_target_pairs={{0,32},{32,0},{64,96},{96,64},{128,160},{160,128},{192,224},{224,1... | collective-permute-start | bytes 540680 | tf_op jit(solution)/shard_map/ppermute | solution.py:424
  24.6 5.6 %collective-permute-start.5 = (f32[48,128]{1,0:T(8,128)S(1)}, f32[48,128]{1,0:T(8,128)S(1)}, u32[]{:S(2)}, u32[]{:S(2)}) collective-permute-start(f32[48,128]{1,0:T(8,128)S(1)} %get-tuple-element.182), channel_id=1, source_target_pairs={{0,32},{32,64},{64,96},{96,128},{128,160},{160,192},{192,224},{1,3... | collective-permute-start | bytes 73736 | tf_op jit(solution)/shard_map/ppermute | solution.py:141
  28.2 5.1 %collective-permute-start.6 = (f32[48,128]{1,0:T(8,128)S(1)}, f32[48,128]{1,0:T(8,128)S(1)}, u32[]{:S(2)}, u32[]{:S(2)}) collective-permute-start(f32[48,128]{1,0:T(8,128)S(1)} %get-tuple-element.183), channel_id=1, source_target_pairs={{32,0},{64,32},{96,64},{128,96},{160,128},{192,160},{224,192},{33,... | collective-permute-start | bytes 73736 | tf_op jit(solution)/shard_map/ppermute | solution.py:141
  33.3 6.0 %collective-permute-start.7 = (f32[176,128]{1,0:T(8,128)S(1)}, f32[176,128]{1,0:T(8,128)S(1)}, u32[]{:S(2)}, u32[]{:S(2)}) collective-permute-start(f32[176,128]{1,0:T(8,128)S(1)} %get-tuple-element.187), channel_id=1, source_target_pairs={{0,64},{32,96},{64,0},{96,32},{128,192},{160,224},{192,128},{224,1... | collective-permute-start | bytes 270344 | tf_op jit(solution)/shard_map/ppermute | solution.py:424
  34.5 4.9 %collective-permute-start.8 = (f32[16,128]{1,0:T(8,128)S(1)}, f32[16,128]{1,0:T(8,128)S(1)}, u32[]{:S(2)}, u32[]{:S(2)}) collective-permute-start(f32[16,128]{1,0:T(8,128)S(1)} %get-tuple-element.191), channel_id=1, source_target_pairs={{0,1},{1,2},{2,3},{3,4},{4,5},{5,6},{6,7},{7,8},{8,9},{9,10},{10,1... | collective-permute-start | bytes 24584 | tf_op jit(solution)/shard_map/ppermute | solution.py:141
  38.0 5.9 %collective-permute-start.9 = (f32[16,128]{1,0:T(8,128)S(1)}, f32[16,128]{1,0:T(8,128)S(1)}, u32[]{:S(2)}, u32[]{:S(2)}) collective-permute-start(f32[16,128]{1,0:T(8,128)S(1)} %get-tuple-element.192), channel_id=1, source_target_pairs={{1,0},{2,1},{3,2},{4,3},{5,4},{6,5},{7,6},{8,7},{9,8},{10,9},{11,1... | collective-permute-start | bytes 24584 | tf_op jit(solution)/shard_map/ppermute | solution.py:141
  43.9 5.0 %collective-permute-start.10 = (f32[176,128]{1,0:T(8,128)S(1)}, f32[176,128]{1,0:T(8,128)S(1)}, u32[]{:S(2)}, u32[]{:S(2)}) collective-permute-start(f32[176,128]{1,0:T(8,128)S(1)} %add.56), channel_id=1, source_target_pairs={{0,192},{32,224},{64,128},{96,160},{128,64},{160,96},{192,0},{224,... | collective-permute-start | bytes 270344 | tf_op jit(solution)/shard_map/ppermute | solution.py:424
  49.0 10.8 %collective-permute-start.12 = (f32[288,128]{1,0:T(8,128)S(1)}, f32[288,128]{1,0:T(8,128)S(1)}, u32[]{:S(2)}, u32[]{:S(2)}) collective-permute-start(f32[288,128]{1,0:T(8,128)S(1)} %get-tuple-element.210), channel_id=1, source_target_pairs={{0,32},{32,64},{64,96},{96,128},{128,160},{160,192},{192,224},{1,3... | collective-permute-start | bytes 442376 | tf_op jit(solution)/shard_map/ppermute | solution.py:141
  51.1 8.7 %collective-permute-start.13 = (f32[288,128]{1,0:T(8,128)S(1)}, f32[288,128]{1,0:T(8,128)S(1)}, u32[]{:S(2)}, u32[]{:S(2)}) collective-permute-start(f32[288,128]{1,0:T(8,128)S(1)} %get-tuple-element.211), channel_id=1, source_target_pairs={{32,0},{64,32},{96,64},{128,96},{160,128},{192,160},{224,192},{33,... | collective-permute-start | bytes 442376 | tf_op jit(solution)/shard_map/ppermute | solution.py:141
  53.4 6.4 %collective-permute-start.11 = (f32[176,128]{1,0:T(8,128)S(1)}, f32[176,128]{1,0:T(8,128)S(1)}, u32[]{:S(2)}, u32[]{:S(2)}) collective-permute-start(f32[176,128]{1,0:T(8,128)S(1)} %add.57), channel_id=1, source_target_pairs={{0,8},{1,9},{2,10},{3,11},{4,12},{5,13},{6,14},{7,15},{8,0},{9,1},... | collective-permute-start | bytes 270344 | tf_op jit(solution)/shard_map/ppermute | solution.py:424
  59.8 6.2 %collective-permute-start.14 = (f32[176,128]{1,0:T(8,128)S(1)}, f32[176,128]{1,0:T(8,128)S(1)}, u32[]{:S(2)}, u32[]{:S(2)}) collective-permute-start(f32[176,128]{1,0:T(8,128)S(1)} %add.58), channel_id=1, source_target_pairs={{0,24},{1,25},{2,26},{3,27},{4,28},{5,29},{6,30},{7,31},{8,16},{9,... | collective-permute-start | bytes 270344 | tf_op jit(solution)/shard_map/ppermute | solution.py:424
  66.0 3.5 %collective-permute-start.15 = (f32[176,128]{1,0:T(8,128)S(1)}, f32[176,128]{1,0:T(8,128)S(1)}, u32[]{:S(2)}, u32[]{:S(2)}) collective-permute-start(f32[176,128]{1,0:T(8,128)S(1)} %add.59), channel_id=1, source_target_pairs={{0,1},{1,0},{2,3},{3,2},{4,5},{5,4},{6,7},{7,6},{8,9},{9,8},{10,11... | collective-permute-start | bytes 270344 | tf_op jit(solution)/shard_map/ppermute | solution.py:424
  69.5 5.7 %collective-permute-start.16 = (f32[176,128]{1,0:T(8,128)S(1)}, f32[176,128]{1,0:T(8,128)S(1)}, u32[]{:S(2)}, u32[]{:S(2)}) collective-permute-start(f32[176,128]{1,0:T(8,128)S(1)} %add.60), channel_id=1, source_target_pairs={{0,7},{1,2},{2,1},{3,4},{4,3},{5,6},{6,5},{7,0},{8,15},{9,10},{10,... | collective-permute-start | bytes 270344 | tf_op jit(solution)/shard_map/ppermute | solution.py:424
  75.3 5.8 %collective-permute-start.17 = (f32[176,128]{1,0:T(8,128)S(1)}, f32[176,128]{1,0:T(8,128)S(1)}, u32[]{:S(2)}, u32[]{:S(2)}) collective-permute-start(f32[176,128]{1,0:T(8,128)S(1)} %add.61), channel_id=1, source_target_pairs={{0,3},{1,6},{2,5},{3,0},{4,7},{5,2},{6,1},{7,4},{8,11},{9,14},{10,... | collective-permute-start | bytes 270344 | tf_op jit(solution)/shard_map/ppermute | solution.py:424
  77.8 3.3 %collective-permute-start.18 = (f32[96,128]{1,0:T(8,128)S(1)}, f32[96,128]{1,0:T(8,128)S(1)}, u32[]{:S(2)}, u32[]{:S(2)}) collective-permute-start(f32[96,128]{1,0:T(8,128)S(1)} %get-tuple-element.236), channel_id=1, source_target_pairs={{0,1},{1,2},{2,3},{3,4},{4,5},{5,6},{6,7},{7,8},{8,9},{9,10},{10,1... | collective-permute-start | bytes 147464 | tf_op jit(solution)/shard_map/ppermute | solution.py:141
  79.8 5.0 %collective-permute-start.19 = (f32[96,128]{1,0:T(8,128)S(1)}, f32[96,128]{1,0:T(8,128)S(1)}, u32[]{:S(2)}, u32[]{:S(2)}) collective-permute-start(f32[96,128]{1,0:T(8,128)S(1)} %get-tuple-element.237), channel_id=1, source_target_pairs={{1,0},{2,1},{3,2},{4,3},{5,4},{6,5},{7,6},{8,7},{9,8},{10,9},{11,1... | collective-permute-start | bytes 147464 | tf_op jit(solution)/shard_map/ppermute | solution.py:141
  84.8 3.4 %collective-permute-start.20 = (f32[176,128]{1,0:T(8,128)S(1)}, f32[176,128]{1,0:T(8,128)S(1)}, u32[]{:S(2)}, u32[]{:S(2)}) collective-permute-start(f32[176,128]{1,0:T(8,128)S(1)} %add.62), channel_id=1, source_target_pairs={{0,64},{32,96},{64,0},{96,32},{128,192},{160,224},{192,128},{224,1... | collective-permute-start | bytes 270344 | tf_op jit(solution)/shard_map/ppermute | solution.py:424
  88.2 7.0 %collective-permute-start.21 = (f32[352,128]{1,0:T(8,128)S(1)}, f32[352,128]{1,0:T(8,128)S(1)}, u32[]{:S(2)}, u32[]{:S(2)}) collective-permute-start(f32[352,128]{1,0:T(8,128)S(1)} %maximum_select_fusion.2), channel_id=1, source_target_pairs={{0,32},{32,0},{64,96},{96,64},{128,160},{160,128},{192,224},{224,1... | collective-permute-start | bytes 540680 | tf_op jit(solution)/shard_map/ppermute | solution.py:424
  97.9 1.5 collective-permute-start.22
  99.5 3.9 %collective-permute-start.23 = (f32[176,128]{1,0:T(8,128)S(1)}, f32[176,128]{1,0:T(8,128)S(1)}, u32[]{:S(2)}, u32[]{:S(2)}) collective-permute-start(f32[176,128]{1,0:T(8,128)S(1)} %get-tuple-element.267), channel_id=1, source_target_pairs={{0,64},{32,96},{64,0},{96,32},{128,192},{160,224},{192,128},{224,1... | collective-permute-start | bytes 270344 | tf_op jit(solution)/shard_map/ppermute | solution.py:424
  103.4 8.6 %collective-permute-start.24 = (f32[176,128]{1,0:T(8,128)S(1)}, f32[176,128]{1,0:T(8,128)S(1)}, u32[]{:S(2)}, u32[]{:S(2)}) collective-permute-start(f32[176,128]{1,0:T(8,128)S(1)} %add.64), channel_id=1, source_target_pairs={{0,192},{32,224},{64,128},{96,160},{128,64},{160,96},{192,0},{224,... | collective-permute-start | bytes 270344 | tf_op jit(solution)/shard_map/ppermute | solution.py:424
  107.2 4.9 %collective-permute-start.25 = (f32[48,128]{1,0:T(8,128)S(1)}, f32[48,128]{1,0:T(8,128)S(1)}, u32[]{:S(2)}, u32[]{:S(2)}) collective-permute-start(f32[48,128]{1,0:T(8,128)S(1)} %get-tuple-element.276), channel_id=1, source_target_pairs={{0,32},{32,64},{64,96},{96,128},{128,160},{160,192},{192,224},{1,3... | collective-permute-start | bytes 73736 | tf_op jit(solution)/shard_map/ppermute | solution.py:141
  110.1 5.1 %collective-permute-start.26 = (f32[48,128]{1,0:T(8,128)S(1)}, f32[48,128]{1,0:T(8,128)S(1)}, u32[]{:S(2)}, u32[]{:S(2)}) collective-permute-start(f32[48,128]{1,0:T(8,128)S(1)} %get-tuple-element.277), channel_id=1, source_target_pairs={{32,0},{64,32},{96,64},{128,96},{160,128},{192,160},{224,192},{33,... | collective-permute-start | bytes 73736 | tf_op jit(solution)/shard_map/ppermute | solution.py:141
  115.2 3.6 %collective-permute-start.27 = (f32[176,128]{1,0:T(8,128)S(1)}, f32[176,128]{1,0:T(8,128)S(1)}, u32[]{:S(2)}, u32[]{:S(2)}) collective-permute-start(f32[176,128]{1,0:T(8,128)S(1)} %add.65), channel_id=1, source_target_pairs={{0,8},{1,9},{2,10},{3,11},{4,12},{5,13},{6,14},{7,15},{8,0},{9,1},... | collective-permute-start | bytes 270344 | tf_op jit(solution)/shard_map/ppermute | solution.py:424
  118.8 6.4 %collective-permute-start.28 = (f32[176,128]{1,0:T(8,128)S(1)}, f32[176,128]{1,0:T(8,128)S(1)}, u32[]{:S(2)}, u32[]{:S(2)}) collective-permute-start(f32[176,128]{1,0:T(8,128)S(1)} %add.66), channel_id=1, source_target_pairs={{0,24},{1,25},{2,26},{3,27},{4,28},{5,29},{6,30},{7,31},{8,16},{9,... | collective-permute-start | bytes 270344 | tf_op jit(solution)/shard_map/ppermute | solution.py:424
  125.2 4.3 %collective-permute-start.29 = (f32[176,128]{1,0:T(8,128)S(1)}, f32[176,128]{1,0:T(8,128)S(1)}, u32[]{:S(2)}, u32[]{:S(2)}) collective-permute-start(f32[176,128]{1,0:T(8,128)S(1)} %add.67), channel_id=1, source_target_pairs={{0,1},{1,0},{2,3},{3,2},{4,5},{5,4},{6,7},{7,6},{8,9},{9,8},{10,11... | collective-permute-start | bytes 270344 | tf_op jit(solution)/shard_map/ppermute | solution.py:424
  129.5 5.0 %collective-permute-start.30 = (f32[176,128]{1,0:T(8,128)S(1)}, f32[176,128]{1,0:T(8,128)S(1)}, u32[]{:S(2)}, u32[]{:S(2)}) collective-permute-start(f32[176,128]{1,0:T(8,128)S(1)} %add.68), channel_id=1, source_target_pairs={{0,7},{1,2},{2,1},{3,4},{4,3},{5,6},{6,5},{7,0},{8,15},{9,10},{10,... | collective-permute-start | bytes 270344 | tf_op jit(solution)/shard_map/ppermute | solution.py:424
  134.5 6.1 %collective-permute-start.31 = (f32[176,128]{1,0:T(8,128)S(1)}, f32[176,128]{1,0:T(8,128)S(1)}, u32[]{:S(2)}, u32[]{:S(2)}) collective-permute-start(f32[176,128]{1,0:T(8,128)S(1)} %add.69), channel_id=1, source_target_pairs={{0,3},{1,6},{2,5},{3,0},{4,7},{5,2},{6,1},{7,4},{8,11},{9,14},{10,... | collective-permute-start | bytes 270344 | tf_op jit(solution)/shard_map/ppermute | solution.py:424
  137.7 3.0 %collective-permute-start.32 = (f32[16,128]{1,0:T(8,128)S(1)}, f32[16,128]{1,0:T(8,128)S(1)}, u32[]{:S(2)}, u32[]{:S(2)}) collective-permute-start(f32[16,128]{1,0:T(8,128)S(1)} %get-tuple-element.313), channel_id=1, source_target_pairs={{0,1},{1,2},{2,3},{3,4},{4,5},{5,6},{6,7},{7,8},{8,9},{9,10},{10,1... | collective-permute-start | bytes 24584 | tf_op jit(solution)/shard_map/ppermute | solution.py:141
  139.3 4.4 %collective-permute-start.33 = (f32[16,128]{1,0:T(8,128)S(1)}, f32[16,128]{1,0:T(8,128)S(1)}, u32[]{:S(2)}, u32[]{:S(2)}) collective-permute-start(f32[16,128]{1,0:T(8,128)S(1)} %get-tuple-element.314), channel_id=1, source_target_pairs={{1,0},{2,1},{3,2},{4,3},{5,4},{6,5},{7,6},{8,7},{9,8},{10,9},{11,1... | collective-permute-start | bytes 24584 | tf_op jit(solution)/shard_map/ppermute | solution.py:141
  143.7 3.4 %collective-permute-start.34 = (f32[176,128]{1,0:T(8,128)S(1)}, f32[176,128]{1,0:T(8,128)S(1)}, u32[]{:S(2)}, u32[]{:S(2)}) collective-permute-start(f32[176,128]{1,0:T(8,128)S(1)} %add.70), channel_id=1, source_target_pairs={{0,64},{32,96},{64,0},{96,32},{128,192},{160,224},{192,128},{224,1... | collective-permute-start | bytes 270344 | tf_op jit(solution)/shard_map/ppermute | solution.py:424
  147.1 7.1 %collective-permute-start.35 = (f32[352,128]{1,0:T(8,128)S(1)}, f32[352,128]{1,0:T(8,128)S(1)}, u32[]{:S(2)}, u32[]{:S(2)}) collective-permute-start(f32[352,128]{1,0:T(8,128)S(1)} %maximum_select_fusion.3), channel_id=1, source_target_pairs={{0,32},{32,0},{64,96},{96,64},{128,160},{160,128},{192,224},{224,1... | collective-permute-start | bytes 540680 | tf_op jit(solution)/shard_map/ppermute | solution.py:424

commit v4 on v3

--- a/solution.py
+++ b/solution.py
@@ -20,7 +20,7 @@
 FLAT = C * TAPS
 WIDE = K * LANES
 D_ROWS = K * M
-G_ROWS = 704
+G_ROWS = D_ROWS
 SLAB = 8 * M
 
 step_coef = 0.5
@@ -49,13 +49,6 @@
 def split2(value):
     high = value.astype(BF16)
     return high, (value - high.astype(F32)).astype(BF16)
-
-
-def split3(value):
-    high = value.astype(BF16)
-    rest = value - high.astype(F32)
-    mid = rest.astype(BF16)
-    return high, mid, (rest - mid.astype(F32)).astype(BF16)
 
 
 def roll(value, shift):
@@ -94,10 +87,10 @@
 
 
 def to_rows_kernel(filt, cons, duals, filt_out, cons_out, duals_out, stacked):
-    stacked[:, 6 * LANES :] = jnp.zeros((9 * M, LANES), BF16)
+    stacked[:, 6 * LANES :] = jnp.zeros((6 * M, LANES), BF16)
     for i, ref in enumerate((filt, cons, duals)):
-        for j, part in enumerate(split3(ref[...])):
-            at = (3 * i + j) * M
+        for j, part in enumerate(split2(ref[...])):
+            at = (2 * i + j) * M
             stacked[at : at + M, :FLAT] = part
     source = lax.broadcasted_iota(jnp.int32, (WIDE, LANES), 0)
     lane = lane_of(WIDE)
@@ -105,10 +98,8 @@
         pick = (source == flat_of(lane + a * LANES)).astype(F32).astype(BF16)
         moved = matmul(stacked[...], pick)
         for i, ref in enumerate((filt_out, cons_out, duals_out)):
-            at = 3 * i * M
-            ref[a * M : (a + 1) * M, :] = (
-                moved[at : at + M] + moved[at + M : at + 2 * M] + moved[at + 2 * M : at + 3 * M]
-            )
+            at = 2 * i * M
+            ref[a * M : (a + 1) * M, :] = moved[at : at + M] + moved[at + M : at + 2 * M]
 
 
 def padded_row(y, size, own, above, below):
@@ -136,9 +127,12 @@
 
 def neighbours(axis, toward_high, toward_low):
     count = lax.axis_size(axis)
-    up = [(i, i + 1) for i in range(count - 1)]
-    down = [(i + 1, i) for i in range(count - 1)]
-    return lax.ppermute(toward_high, axis, up), lax.ppermute(toward_low, axis, down)
+    odd = lax.axis_index(axis) % 2 == 1
+    even_pairs = [(i, i ^ 1) for i in range(count)]
+    odd_pairs = [(i, i + 1 if i % 2 == 1 else i - 1) for i in range(1, count - 1)]
+    first = lax.ppermute(jnp.where(odd, toward_low, toward_high), axis, even_pairs)
+    second = lax.ppermute(jnp.where(odd, toward_high, toward_low), axis, odd_pairs)
+    return jnp.where(odd, first, second), jnp.where(odd, second, first)
 
 
 def pack(size, own, above, below):
@@ -243,8 +237,7 @@
             x_lo[y * M : y * M + D_ROWS, :],
             r_all[:, y * LANES : (y + 2) * LANES],
         )
-    grad[:D_ROWS, :] = total
-    grad[D_ROWS:, :] = jnp.zeros((G_ROWS - D_ROWS, LANES), F32)
+    grad[...] = total
 
 
 RECON_OUT = [shape(ROWS * C, LANES), shape(3 * C, LANES), shape(3 * C, LANES), shape(G_ROWS, LANES)]
@@ -303,8 +296,8 @@
     update_into(summed, filt, cons, duals, new.at[0], new.at[1], new.at[2])
     for i in range(3):
         for a in range(K):
-            for j, part in enumerate(split3(new[i, a * M : (a + 1) * M, :])):
-                at = (3 * i + j) * M
+            for j, part in enumerate(split2(new[i, a * M : (a + 1) * M, :])):
+                at = (2 * i + j) * M
                 stacked[at : at + M, a * LANES : (a + 1) * LANES] = part
     source = lax.broadcasted_iota(jnp.int32, (WIDE, LANES), 0)
     wanted = flat_of(source)
@@ -314,8 +307,8 @@
         moved = matmul(stacked[...], pick)
         width = min(LANES, FLAT - block * LANES)
         for i, ref in enumerate((filt_out, cons_out, duals_out)):
-            at = 3 * i * M
-            value = moved[at : at + M] + moved[at + M : at + 2 * M] + moved[at + 2 * M : at + 3 * M]
+            at = 2 * i * M
+            value = moved[at : at + M] + moved[at + M : at + 2 * M]
             ref[:, block * LANES : block * LANES + width] = value[:, :width]
 
 
@@ -444,7 +437,7 @@
     map_rows = [shape(ROWS * M, LANES), shape(3 * M, LANES), shape(3 * M, LANES)]
     filters = [shape(D_ROWS, LANES)] * 3
     maps, top, bottom = call(rows_kernel, map_rows)(coef_maps)
-    filt, cons, duals = call(to_rows_kernel, filters, [pltpu.VMEM((9 * M, WIDE), BF16)])(
+    filt, cons, duals = call(to_rows_kernel, filters, [pltpu.VMEM((6 * M, WIDE), BF16)])(
         dictionary, consensus, dual_vars
     )
     edges = halos(M, maps, top, bottom)
@@ -505,7 +498,7 @@
     new = call(
         last_kernel,
         [shape(M, FLAT)] * 3,
-        [pltpu.VMEM((3, D_ROWS, LANES), F32), pltpu.VMEM((9 * M, WIDE), BF16)],
+        [pltpu.VMEM((3, D_ROWS, LANES), F32), pltpu.VMEM((6 * M, WIDE), BF16)],
     )(summed, filt, cons, duals)
     return (new_maps, *new)
 

time: 159 us -> 146 us (0.918)
  waiting for transfers between devices: 55.7 us -> 42.5 us
  Pallas kernels: 16.8 us -> 14.9 us
    ppermute x16, waiting for transfers between devices: 22.8 us -> 3.63 us  [the longest x8 3.61 us: neighbours(): lax.ppermute(jnp.where(odd, toward_high, toward_low), axis, odd_pairs)]
    ppermute x20, waiting for transfers between devices: 32.9 us -> 38.9 us  [beside(): other = lax.ppermute(sent, axis, pairs)]
  transfers between devices with their start and end apart: 36 -> 36, of which waited for: 23 -> 22; matrix products, arithmetic and copies ran while one was open for 0% -> 0% of each run, Pallas kernels for 4% -> 4%
where the time goes in v4:
time: 146 us; the launch traced here: 145 us
  starting transfers between devices  83.8 us (57%)
  waiting for transfers between devices  42.5 us (29%)
  Pallas kernels  14.9 us (10%)
  local copies, waits for them, and re-layouts  1.8 us (1%)
    ppermute x20, starting transfers between devices, beside(): other = lax.ppermute(sent, axis, pairs)  47.6 us
    ppermute x20, waiting for transfers between devices, beside(): other = lax.ppermute(sent, axis, pairs)  38.9 us
    ppermute x8, starting transfers between devices, neighbours(): lax.ppermute(jnp.where(odd, toward_high, toward_low), axis, odd_pairs)  20.9 us
    ppermute x8, starting transfers between devices, neighbours(): lax.ppermute(jnp.where(odd, toward_low, toward_high), axis, even_pairs)  15.3 us
    ppermute x8, waiting for transfers between devices, neighbours(): lax.ppermute(jnp.where(odd, toward_high, toward_low), axis, odd_pairs)  3.61 us
    pallas_call x1, Pallas kernels, local(): call(last_kernel, [shape(M, FLAT)] * 3, [pltpu.VMEM((3, D_ROWS, LANES), F...  3.26 us
    pallas_call x2, Pallas kernels, run(): call(functools.partial(corr_kernel, last), outs, CORR_SCRATCH)  3.21 us
  transfers between devices with their start and end apart: 36, of which 22 were waited for; matrix products, arithmetic and copies ran while one was open for 0% of the time, Pallas kernels for 4%

profile of v4, /device:TPU:1, one launch (start us, length us, event | category | flops | bytes accessed | tf_op | source)
XLA Modules:
  0.0 144.7 jit_solution(2694358421540407116)
XLA Ops:
  0.7 1.0 copy-done
  1.6 0.2 shard_map.84
  1.9 4.6 %collective-permute-start.1 = (f32[288,128]{1,0:T(8,128)S(1)}, f32[288,128]{1,0:T(8,128)S(1)}, u32[]{:S(2)}, u32[]{:S(2)}) collective-permute-start(f32[288,128]{1,0:T(8,128)S(1)} %get-tuple-element.344), channel_id=1, source_target_pairs={{32,64},{64,32},{96,128},{128,96},{160,192},{192,160},{33,65},{65,... | collective-permute-start | bytes 442376 | tf_op jit(solution)/shard_map/ppermute | solution.py:134
  6.6 2.7 %collective-permute-done.1 = f32[288,128]{1,0:T(8,128)S(1)} collective-permute-done((f32[288,128]{1,0:T(8,128)S(1)}, f32[288,128]{1,0:T(8,128)S(1)}, u32[]{:S(2)}, u32[]{:S(2)}) %collective-permute-start.1) | collective-permute-done | bytes 147488 | tf_op jit(solution)/shard_map/ppermute | solution.py:134
  9.4 0.4 shard_map.85
  9.8 0.7 collective-permute-start.3
  10.5 4.6 %collective-permute-start.2 = (f32[96,128]{1,0:T(8,128)S(1)}, f32[96,128]{1,0:T(8,128)S(1)}, u32[]{:S(2)}, u32[]{:S(2)}) collective-permute-start(f32[96,128]{1,0:T(8,128)S(1)} %get-tuple-element.357), channel_id=1, source_target_pairs={{0,1},{1,0},{2,3},{3,2},{4,5},{5,4},{6,7},{7,6},{8,9},{9,8},{10,11... | collective-permute-start | bytes 147464 | tf_op jit(solution)/shard_map/ppermute | solution.py:133
  15.1 2.1 %shard_map.86 = (f32[672,128]{1,0:T(8,128)S(1)}, f32[672,128]{1,0:T(8,128)S(1)}, f32[672,128]{1,0:T(8,128)S(1)}) custom-call(f32[96,784]{1,0:T(8,128)S(1)} %copy-done.1, f32[96,784]{1,0:T(8,128)S(1)} %copy-done.2, f32[96,784]{1,0:T(8,128)S(1)} %copy-done.3), custom_call_target="tpu_custom_call" | custom-call | tf_op jit(solution)/shard_map/pallas_call | solution.py:440
  17.2 0.8 copy-done.4
  18.0 2.5 %shard_map.87 = (f32[128,128]{1,0:T(8,128)S(1)}, f32[48,128]{1,0:T(8,128)S(1)}, f32[48,128]{1,0:T(8,128)S(1)}, f32[672,128]{1,0:T(8,128)S(1)}) custom-call(f32[768,128]{1,0:T(8,128)S(1)} %get-tuple-element.203.own.maps, f32[288,128]{1,0:T(8,128)S(1)} %get-tuple-element.343.above, f32[288,128]{1,0:T(8,128)S(1)} %get-tuple-element.342.below, ...), custom_call_target="tpu_custom_call" | custom-call | tf_op jit(solution)/shard_map/pallas_call | solution.py:444
  20.6 4.2 %collective-permute-start.6 = (f32[48,128]{1,0:T(8,128)S(1)}, f32[48,128]{1,0:T(8,128)S(1)}, u32[]{:S(2)}, u32[]{:S(2)}) collective-permute-start(f32[48,128]{1,0:T(8,128)S(1)} %get-tuple-element.364), channel_id=1, source_target_pairs={{32,64},{64,32},{96,128},{128,96},{160,192},{192,160},{33,65},{65,... | collective-permute-start | bytes 73736 | tf_op jit(solution)/shard_map/ppermute | solution.py:134
  24.9 0.5 collective-permute-start.4
  25.4 0.9 collective-permute-done.6
  26.6 0.7 collective-permute-start.9
  27.3 5.8 %collective-permute-start.8 = (f32[16,128]{1,0:T(8,128)S(1)}, f32[16,128]{1,0:T(8,128)S(1)}, u32[]{:S(2)}, u32[]{:S(2)}) collective-permute-start(f32[16,128]{1,0:T(8,128)S(1)} %get-tuple-element.373), channel_id=1, source_target_pairs={{0,1},{1,0},{2,3},{3,2},{4,5},{5,4},{6,7},{7,6},{8,9},{9,8},{10,11... | collective-permute-start | bytes 24584 | tf_op jit(solution)/shard_map/ppermute | solution.py:133
  33.1 1.3 collective-permute-start.7
  34.5 2.0 %collective-permute-done.7 = f32[168,128]{1,0:T(8,128)S(1)} collective-permute-done((f32[168,128]{1,0:T(8,128)S(1)}, f32[168,128]{1,0:T(8,128)S(1)}, u32[]{:S(2)}, u32[]{:S(2)}) %collective-permute-start.7) | collective-permute-done | bytes 86048 | tf_op jit(solution)/shard_map/ppermute | solution.py:417
  36.5 1.7 %collective-permute-start.10 = (f32[168,128]{1,0:T(8,128)S(1)}, f32[168,128]{1,0:T(8,128)S(1)}, u32[]{:S(2)}, u32[]{:S(2)}) collective-permute-start(f32[168,128]{1,0:T(8,128)S(1)} %add.67), channel_id=1, source_target_pairs={{0,192},{32,224},{64,128},{96,160},{128,64},{160,96},{192,0},{224,... | collective-permute-start | bytes 258056 | tf_op jit(solution)/shard_map/ppermute | solution.py:417
  38.2 1.2 shard_map.89
  39.4 1.7 %collective-permute-done.10 = f32[168,128]{1,0:T(8,128)S(1)} collective-permute-done((f32[168,128]{1,0:T(8,128)S(1)}, f32[168,128]{1,0:T(8,128)S(1)}, u32[]{:S(2)}, u32[]{:S(2)}) %collective-permute-start.10) | collective-permute-done | bytes 86048 | tf_op jit(solution)/shard_map/ppermute | solution.py:417
  41.1 5.2 %collective-permute-start.13 = (f32[288,128]{1,0:T(8,128)S(1)}, f32[288,128]{1,0:T(8,128)S(1)}, u32[]{:S(2)}, u32[]{:S(2)}) collective-permute-start(f32[288,128]{1,0:T(8,128)S(1)} %get-tuple-element.340), channel_id=1, source_target_pairs={{32,64},{64,32},{96,128},{128,96},{160,192},{192,160},{33,65},{65,... | collective-permute-start | bytes 442376 | tf_op jit(solution)/shard_map/ppermute | solution.py:134
  46.4 1.5 %collective-permute-start.11 = (f32[168,128]{1,0:T(8,128)S(1)}, f32[168,128]{1,0:T(8,128)S(1)}, u32[]{:S(2)}, u32[]{:S(2)}) collective-permute-start(f32[168,128]{1,0:T(8,128)S(1)} %add.68), channel_id=1, source_target_pairs={{0,8},{1,9},{2,10},{3,11},{4,12},{5,13},{6,14},{7,15},{8,0},{9,1},... | collective-permute-start | bytes 258056 | tf_op jit(solution)/shard_map/ppermute | solution.py:417
  48.0 2.3 %collective-permute-done.11 = f32[168,128]{1,0:T(8,128)S(1)} collective-permute-done((f32[168,128]{1,0:T(8,128)S(1)}, f32[168,128]{1,0:T(8,128)S(1)}, u32[]{:S(2)}, u32[]{:S(2)}) %collective-permute-start.11) | collective-permute-done | bytes 86048 | tf_op jit(solution)/shard_map/ppermute | solution.py:417
  50.3 3.1 %collective-permute-start.14 = (f32[168,128]{1,0:T(8,128)S(1)}, f32[168,128]{1,0:T(8,128)S(1)}, u32[]{:S(2)}, u32[]{:S(2)}) collective-permute-start(f32[168,128]{1,0:T(8,128)S(1)} %add.69), channel_id=1, source_target_pairs={{0,24},{1,25},{2,26},{3,27},{4,28},{5,29},{6,30},{7,31},{8,16},{9,... | collective-permute-start | bytes 258056 | tf_op jit(solution)/shard_map/ppermute | solution.py:417
  53.4 1.9 %collective-permute-done.14 = f32[168,128]{1,0:T(8,128)S(1)} collective-permute-done((f32[168,128]{1,0:T(8,128)S(1)}, f32[168,128]{1,0:T(8,128)S(1)}, u32[]{:S(2)}, u32[]{:S(2)}) %collective-permute-start.14) | collective-permute-done | bytes 86048 | tf_op jit(solution)/shard_map/ppermute | solution.py:417
  55.3 1.9 %collective-permute-start.15 = (f32[168,128]{1,0:T(8,128)S(1)}, f32[168,128]{1,0:T(8,128)S(1)}, u32[]{:S(2)}, u32[]{:S(2)}) collective-permute-start(f32[168,128]{1,0:T(8,128)S(1)} %add.70), channel_id=1, source_target_pairs={{0,1},{1,0},{2,3},{3,2},{4,5},{5,4},{6,7},{7,6},{8,9},{9,8},{10,11... | collective-permute-start | bytes 258056 | tf_op jit(solution)/shard_map/ppermute | solution.py:417
  57.2 0.4 shard_map.90
  57.6 1.5 %collective-permute-done.15 = f32[168,128]{1,0:T(8,128)S(1)} collective-permute-done((f32[168,128]{1,0:T(8,128)S(1)}, f32[168,128]{1,0:T(8,128)S(1)}, u32[]{:S(2)}, u32[]{:S(2)}) %collective-permute-start.15) | collective-permute-done | bytes 86048 | tf_op jit(solution)/shard_map/ppermute | solution.py:417
  59.1 1.9 %collective-permute-start.16 = (f32[168,128]{1,0:T(8,128)S(1)}, f32[168,128]{1,0:T(8,128)S(1)}, u32[]{:S(2)}, u32[]{:S(2)}) collective-permute-start(f32[168,128]{1,0:T(8,128)S(1)} %add.71), channel_id=1, source_target_pairs={{0,7},{1,2},{2,1},{3,4},{4,3},{5,6},{6,5},{7,0},{8,15},{9,10},{10,... | collective-permute-start | bytes 258056 | tf_op jit(solution)/shard_map/ppermute | solution.py:417
  60.9 2.8 %collective-permute-done.16 = f32[168,128]{1,0:T(8,128)S(1)} collective-permute-done((f32[168,128]{1,0:T(8,128)S(1)}, f32[168,128]{1,0:T(8,128)S(1)}, u32[]{:S(2)}, u32[]{:S(2)}) %collective-permute-start.16) | collective-permute-done | bytes 86048 | tf_op jit(solution)/shard_map/ppermute | solution.py:417
  63.8 0.7 collective-permute-start.19
  64.4 1.6 %collective-permute-start.18 = (f32[96,128]{1,0:T(8,128)S(1)}, f32[96,128]{1,0:T(8,128)S(1)}, u32[]{:S(2)}, u32[]{:S(2)}) collective-permute-start(f32[96,128]{1,0:T(8,128)S(1)} %get-tuple-element.353), channel_id=1, source_target_pairs={{0,1},{1,0},{2,3},{3,2},{4,5},{5,4},{6,7},{7,6},{8,9},{9,8},{10,11... | collective-permute-start | bytes 147464 | tf_op jit(solution)/shard_map/ppermute | solution.py:133
  66.0 2.4 %collective-permute-start.17 = (f32[168,128]{1,0:T(8,128)S(1)}, f32[168,128]{1,0:T(8,128)S(1)}, u32[]{:S(2)}, u32[]{:S(2)}) collective-permute-start(f32[168,128]{1,0:T(8,128)S(1)} %add.72), channel_id=1, source_target_pairs={{0,3},{1,6},{2,5},{3,0},{4,7},{5,2},{6,1},{7,4},{8,11},{9,14},{10,... | collective-permute-start | bytes 258056 | tf_op jit(solution)/shard_map/ppermute | solution.py:417
  68.4 2.8 %collective-permute-done.17 = f32[168,128]{1,0:T(8,128)S(1)} collective-permute-done((f32[168,128]{1,0:T(8,128)S(1)}, f32[168,128]{1,0:T(8,128)S(1)}, u32[]{:S(2)}, u32[]{:S(2)}) %collective-permute-start.17) | collective-permute-done | bytes 86048 | tf_op jit(solution)/shard_map/ppermute | solution.py:417
  71.2 1.4 collective-permute-start.20
  72.5 2.0 %collective-permute-done.20 = f32[168,128]{1,0:T(8,128)S(1)} collective-permute-done((f32[168,128]{1,0:T(8,128)S(1)}, f32[168,128]{1,0:T(8,128)S(1)}, u32[]{:S(2)}, u32[]{:S(2)}) %collective-permute-start.20) | collective-permute-done | bytes 86048 | tf_op jit(solution)/shard_map/ppermute | solution.py:417
  74.6 7.4 %collective-permute-start.21 = (f32[336,128]{1,0:T(8,128)S(1)}, f32[336,128]{1,0:T(8,128)S(1)}, u32[]{:S(2)}, u32[]{:S(2)}) collective-permute-start(f32[336,128]{1,0:T(8,128)S(1)} %maximum_select_fusion.2), channel_id=1, source_target_pairs={{0,32},{32,0},{64,96},{96,64},{128,160},{160,128},{192,224},{224,1... | collective-permute-start | bytes 516104 | tf_op jit(solution)/shard_map/ppermute | solution.py:417
  82.0 1.0 collective-permute-done.21
  83.1 2.6 %shard_map.91 = (f32[672,128]{1,0:T(8,128)S(1)}, f32[672,128]{1,0:T(8,128)S(1)}, f32[672,128]{1,0:T(8,128)S(1)}, f32[128,128]{1,0:T(8,128)S(1)}, f32[48,128]{1,0...) custom-call(f32[672,128]{1,0:T(8,128)S(1)} %maximum_select_fusion.summed, ...), custom_call_target="tpu_custom_call" | custom-call | tf_op jit(solution)/shard_map/pallas_call | solution.py:490
  85.7 0.5 collective-permute-start.22
  86.1 1.0 collective-permute-done.22
  87.2 1.4 collective-permute-start.23
  88.6 2.4 %collective-permute-done.23 = f32[168,128]{1,0:T(8,128)S(1)} collective-permute-done((f32[168,128]{1,0:T(8,128)S(1)}, f32[168,128]{1,0:T(8,128)S(1)}, u32[]{:S(2)}, u32[]{:S(2)}) %collective-permute-start.23) | collective-permute-done | bytes 86048 | tf_op jit(solution)/shard_map/ppermute | solution.py:417
  91.1 4.3 %collective-permute-start.26 = (f32[48,128]{1,0:T(8,128)S(1)}, f32[48,128]{1,0:T(8,128)S(1)}, u32[]{:S(2)}, u32[]{:S(2)}) collective-permute-start(f32[48,128]{1,0:T(8,128)S(1)} %get-tuple-element.360), channel_id=1, source_target_pairs={{32,64},{64,32},{96,128},{128,96},{160,192},{192,160},{33,65},{65,... | collective-permute-start | bytes 73736 | tf_op jit(solution)/shard_map/ppermute | solution.py:134
  95.5 2.1 %collective-permute-start.24 = (f32[168,128]{1,0:T(8,128)S(1)}, f32[168,128]{1,0:T(8,128)S(1)}, u32[]{:S(2)}, u32[]{:S(2)}) collective-permute-start(f32[168,128]{1,0:T(8,128)S(1)} %add.75), channel_id=1, source_target_pairs={{0,192},{32,224},{64,128},{96,160},{128,64},{160,96},{192,0},{224,... | collective-permute-start | bytes 258056 | tf_op jit(solution)/shard_map/ppermute | solution.py:417
  97.7 2.8 %collective-permute-done.24 = f32[168,128]{1,0:T(8,128)S(1)} collective-permute-done((f32[168,128]{1,0:T(8,128)S(1)}, f32[168,128]{1,0:T(8,128)S(1)}, u32[]{:S(2)}, u32[]{:S(2)}) %collective-permute-start.24) | collective-permute-done | bytes 86048 | tf_op jit(solution)/shard_map/ppermute | solution.py:417
  100.5 2.7 %collective-permute-start.27 = (f32[168,128]{1,0:T(8,128)S(1)}, f32[168,128]{1,0:T(8,128)S(1)}, u32[]{:S(2)}, u32[]{:S(2)}) collective-permute-start(f32[168,128]{1,0:T(8,128)S(1)} %add.76), channel_id=1, source_target_pairs={{0,8},{1,9},{2,10},{3,11},{4,12},{5,13},{6,14},{7,15},{8,0},{9,1},... | collective-permute-start | bytes 258056 | tf_op jit(solution)/shard_map/ppermute | solution.py:417
  103.3 1.9 %collective-permute-done.27 = f32[168,128]{1,0:T(8,128)S(1)} collective-permute-done((f32[168,128]{1,0:T(8,128)S(1)}, f32[168,128]{1,0:T(8,128)S(1)}, u32[]{:S(2)}, u32[]{:S(2)}) %collective-permute-start.27) | collective-permute-done | bytes 86048 | tf_op jit(solution)/shard_map/ppermute | solution.py:417
  105.2 1.8 %collective-permute-start.28 = (f32[168,128]{1,0:T(8,128)S(1)}, f32[168,128]{1,0:T(8,128)S(1)}, u32[]{:S(2)}, u32[]{:S(2)}) collective-permute-start(f32[168,128]{1,0:T(8,128)S(1)} %add.77), channel_id=1, source_target_pairs={{0,24},{1,25},{2,26},{3,27},{4,28},{5,29},{6,30},{7,31},{8,16},{9,... | collective-permute-start | bytes 258056 | tf_op jit(solution)/shard_map/ppermute | solution.py:417
  107.0 2.8 %collective-permute-done.28 = f32[168,128]{1,0:T(8,128)S(1)} collective-permute-done((f32[168,128]{1,0:T(8,128)S(1)}, f32[168,128]{1,0:T(8,128)S(1)}, u32[]{:S(2)}, u32[]{:S(2)}) %collective-permute-start.28) | collective-permute-done | bytes 86048 | tf_op jit(solution)/shard_map/ppermute | solution.py:417
  109.8 2.8 %collective-permute-start.29 = (f32[168,128]{1,0:T(8,128)S(1)}, f32[168,128]{1,0:T(8,128)S(1)}, u32[]{:S(2)}, u32[]{:S(2)}) collective-permute-start(f32[168,128]{1,0:T(8,128)S(1)} %add.78), channel_id=1, source_target_pairs={{0,1},{1,0},{2,3},{3,2},{4,5},{5,4},{6,7},{7,6},{8,9},{9,8},{10,11... | collective-permute-start | bytes 258056 | tf_op jit(solution)/shard_map/ppermute | solution.py:417
  112.6 1.9 %collective-permute-done.29 = f32[168,128]{1,0:T(8,128)S(1)} collective-permute-done((f32[168,128]{1,0:T(8,128)S(1)}, f32[168,128]{1,0:T(8,128)S(1)}, u32[]{:S(2)}, u32[]{:S(2)}) %collective-permute-start.29) | collective-permute-done | bytes 86048 | tf_op jit(solution)/shard_map/ppermute | solution.py:417
  114.5 1.6 %collective-permute-start.30 = (f32[168,128]{1,0:T(8,128)S(1)}, f32[168,128]{1,0:T(8,128)S(1)}, u32[]{:S(2)}, u32[]{:S(2)}) collective-permute-start(f32[168,128]{1,0:T(8,128)S(1)} %add.79), channel_id=1, source_target_pairs={{0,7},{1,2},{2,1},{3,4},{4,3},{5,6},{6,5},{7,0},{8,15},{9,10},{10,... | collective-permute-start | bytes 258056 | tf_op jit(solution)/shard_map/ppermute | solution.py:417
  116.1 3.1 %collective-permute-done.30 = f32[168,128]{1,0:T(8,128)S(1)} collective-permute-done((f32[168,128]{1,0:T(8,128)S(1)}, f32[168,128]{1,0:T(8,128)S(1)}, u32[]{:S(2)}, u32[]{:S(2)}) %collective-permute-start.30) | collective-permute-done | bytes 86048 | tf_op jit(solution)/shard_map/ppermute | solution.py:417
  119.3 0.7 collective-permute-start.33
  120.0 2.9 %collective-permute-start.32 = (f32[16,128]{1,0:T(8,128)S(1)}, f32[16,128]{1,0:T(8,128)S(1)}, u32[]{:S(2)}, u32[]{:S(2)}) collective-permute-start(f32[16,128]{1,0:T(8,128)S(1)} %get-tuple-element.369), channel_id=1, source_target_pairs={{0,1},{1,0},{2,3},{3,2},{4,5},{5,4},{6,7},{7,6},{8,9},{9,8},{10,11... | collective-permute-start | bytes 24584 | tf_op jit(solution)/shard_map/ppermute | solution.py:133
  122.9 1.7 %collective-permute-start.31 = (f32[168,128]{1,0:T(8,128)S(1)}, f32[168,128]{1,0:T(8,128)S(1)}, u32[]{:S(2)}, u32[]{:S(2)}) collective-permute-start(f32[168,128]{1,0:T(8,128)S(1)} %add.80), channel_id=1, source_target_pairs={{0,3},{1,6},{2,5},{3,0},{4,7},{5,2},{6,1},{7,4},{8,11},{9,14},{10,... | collective-permute-start | bytes 258056 | tf_op jit(solution)/shard_map/ppermute | solution.py:417
  124.6 3.5 %collective-permute-done.31 = f32[168,128]{1,0:T(8,128)S(1)} collective-permute-done((f32[168,128]{1,0:T(8,128)S(1)}, f32[168,128]{1,0:T(8,128)S(1)}, u32[]{:S(2)}, u32[]{:S(2)}) %collective-permute-start.31) | collective-permute-done | bytes 86048 | tf_op jit(solution)/shard_map/ppermute | solution.py:417
  128.1 1.3 collective-permute-start.34
  129.4 2.0 %shard_map.93 = f32[96,8,128]{2,1,0:T(8,128)} custom-call(f32[128,128]{1,0:T(8,128)S(1)} %get-tuple-element.319.own.resid, f32[48,128]{1,0:T(8,128)S(1)} %get-tuple-element.320.above, f32[48,128]{1,0:T(8,128)S(1)} %get-tuple-element.321.below, f32[16,128]{1,0:T(8,128)S(1)} %get-tuple-element.322.left, f32[16,128]{1,0:T(8,128)S(1)} %get-tuple-element.323.right, ...), custom_call_target="tpu_custom_call" | custom-call | tf_op jit(solution)/shard_map/pallas_call | solution.py:460
  131.5 0.3 collective-permute-done.34
  131.8 8.6 %collective-permute-start.35 = (f32[336,128]{1,0:T(8,128)S(1)}, f32[336,128]{1,0:T(8,128)S(1)}, u32[]{:S(2)}, u32[]{:S(2)}) collective-permute-start(f32[336,128]{1,0:T(8,128)S(1)} %maximum_select_fusion.3), channel_id=1, source_target_pairs={{0,32},{32,0},{64,96},{96,64},{128,160},{160,128},{192,224},{224,1... | collective-permute-start | bytes 516104 | tf_op jit(solution)/shard_map/ppermute | solution.py:417
  140.4 1.0 collective-permute-done.35
  141.4 3.3 %shard_map.94 = (f32[96,784]{1,0:T(8,128)}, f32[96,784]{1,0:T(8,128)}, f32[96,784]{1,0:T(8,128)}) custom-call(f32[672,128]{1,0:T(8,128)S(1)} %maximum_select_fusion.1.summed, f32[672,128]{1,0:T(8,128)S(1)} %get-tuple-element.324.filt, f32[672,128]{1,0:T(8,128)S(1)} %get-tuple-element.329.cons, f32[672,128]{1,0:T(8,128)S(1)} %get-tuple-element.330.duals), custom_call_target="tpu_custom_call" | custom-call | tf_op jit(solution)/shard_map/pallas_call | solution.py:498
  (69 shorter events, 1.4 us)
Async XLA Ops:
  0.6 1.0 copy-start
  1.9 7.4 %collective-permute-start.1 = (f32[288,128]{1,0:T(8,128)S(1)}, f32[288,128]{1,0:T(8,128)S(1)}, u32[]{:S(2)}, u32[]{:S(2)}) collective-permute-start(f32[288,128]{1,0:T(8,128)S(1)} %get-tuple-element.344), channel_id=1, source_target_pairs={{32,64},{64,32},{96,128},{128,96},{160,192},{192,160},{33,65},{65,... | collective-permute-start | bytes 442376 | tf_op jit(solution)/shard_map/ppermute | solution.py:134
  6.5 2.8 %collective-permute-start = (f32[288,128]{1,0:T(8,128)S(1)}, f32[288,128]{1,0:T(8,128)S(1)}, u32[]{:S(2)}, u32[]{:S(2)}) collective-permute-start(f32[288,128]{1,0:T(8,128)S(1)} %get-tuple-element.345), channel_id=1, source_target_pairs={{0,32},{32,0},{64,96},{96,64},{128,160},{160,128},{192,224},{224,1... | collective-permute-start | bytes 442376 | tf_op jit(solution)/shard_map/ppermute | solution.py:133
  9.3 5.8 %copy-start.3 = (f32[96,784]{1,0:T(8,128)S(1)}, f32[96,784]{1,0:T(8,128)}, u32[]{:S(2)}) copy-start(f32[96,784]{1,0:T(8,128)} %duals.1) | copy-start | bytes 903172
  9.3 5.7 %copy-start.1 = (f32[96,784]{1,0:T(8,128)S(1)}, f32[96,784]{1,0:T(8,128)}, u32[]{:S(2)}) copy-start(f32[96,784]{1,0:T(8,128)} %filt.1) | copy-start | bytes 903172
  9.4 5.7 %copy-start.2 = (f32[96,784]{1,0:T(8,128)S(1)}, f32[96,784]{1,0:T(8,128)}, u32[]{:S(2)}) copy-start(f32[96,784]{1,0:T(8,128)} %cons.1) | copy-start | bytes 903172
  9.8 7.4 %collective-permute-start.3 = (f32[96,128]{1,0:T(8,128)S(1)}, f32[96,128]{1,0:T(8,128)S(1)}, u32[]{:S(2)}, u32[]{:S(2)}) collective-permute-start(f32[96,128]{1,0:T(8,128)S(1)} %get-tuple-element.356), channel_id=1, source_target_pairs={{1,2},{2,1},{3,4},{4,3},{5,6},{6,5},{7,8},{8,7},{9,10},{10,9},{11,... | collective-permute-start | bytes 147464 | tf_op jit(solution)/shard_map/ppermute | solution.py:134
  10.5 6.7 %collective-permute-start.2 = (f32[96,128]{1,0:T(8,128)S(1)}, f32[96,128]{1,0:T(8,128)S(1)}, u32[]{:S(2)}, u32[]{:S(2)}) collective-permute-start(f32[96,128]{1,0:T(8,128)S(1)} %get-tuple-element.357), channel_id=1, source_target_pairs={{0,1},{1,0},{2,3},{3,2},{4,5},{5,4},{6,7},{7,6},{8,9},{9,8},{10,11... | collective-permute-start | bytes 147464 | tf_op jit(solution)/shard_map/ppermute | solution.py:133
  17.2 0.8 copy-start.4
  20.6 5.7 %collective-permute-start.6 = (f32[48,128]{1,0:T(8,128)S(1)}, f32[48,128]{1,0:T(8,128)S(1)}, u32[]{:S(2)}, u32[]{:S(2)}) collective-permute-start(f32[48,128]{1,0:T(8,128)S(1)} %get-tuple-element.364), channel_id=1, source_target_pairs={{32,64},{64,32},{96,128},{128,96},{160,192},{192,160},{33,65},{65,... | collective-permute-start | bytes 73736 | tf_op jit(solution)/shard_map/ppermute | solution.py:134
  24.8 1.5 %collective-permute-start.5 = (f32[48,128]{1,0:T(8,128)S(1)}, f32[48,128]{1,0:T(8,128)S(1)}, u32[]{:S(2)}, u32[]{:S(2)}) collective-permute-start(f32[48,128]{1,0:T(8,128)S(1)} %get-tuple-element.365), channel_id=1, source_target_pairs={{0,32},{32,0},{64,96},{96,64},{128,160},{160,128},{192,224},{224,1... | collective-permute-start | bytes 73736 | tf_op jit(solution)/shard_map/ppermute | solution.py:133
  24.9 1.5 %collective-permute-start.4 = (f32[336,128]{1,0:T(8,128)S(1)}, f32[336,128]{1,0:T(8,128)S(1)}, u32[]{:S(2)}, u32[]{:S(2)}) collective-permute-start(f32[336,128]{1,0:T(8,128)S(1)} %get-tuple-element.180), channel_id=1, source_target_pairs={{0,32},{32,0},{64,96},{96,64},{128,160},{160,128},{192,224},{224,1... | collective-permute-start | bytes 516104 | tf_op jit(solution)/shard_map/ppermute | solution.py:417
  26.6 7.8 %collective-permute-start.9 = (f32[16,128]{1,0:T(8,128)S(1)}, f32[16,128]{1,0:T(8,128)S(1)}, u32[]{:S(2)}, u32[]{:S(2)}) collective-permute-start(f32[16,128]{1,0:T(8,128)S(1)} %get-tuple-element.372), channel_id=1, source_target_pairs={{1,2},{2,1},{3,4},{4,3},{5,6},{6,5},{7,8},{8,7},{9,10},{10,9},{11,... | collective-permute-start | bytes 24584 | tf_op jit(solution)/shard_map/ppermute | solution.py:134
  27.3 7.2 %collective-permute-start.8 = (f32[16,128]{1,0:T(8,128)S(1)}, f32[16,128]{1,0:T(8,128)S(1)}, u32[]{:S(2)}, u32[]{:S(2)}) collective-permute-start(f32[16,128]{1,0:T(8,128)S(1)} %get-tuple-element.373), channel_id=1, source_target_pairs={{0,1},{1,0},{2,3},{3,2},{4,5},{5,4},{6,7},{7,6},{8,9},{9,8},{10,11... | collective-permute-start | bytes 24584 | tf_op jit(solution)/shard_map/ppermute | solution.py:133
  33.1 3.3 %collective-permute-start.7 = (f32[168,128]{1,0:T(8,128)S(1)}, f32[168,128]{1,0:T(8,128)S(1)}, u32[]{:S(2)}, u32[]{:S(2)}) collective-permute-start(f32[168,128]{1,0:T(8,128)S(1)} %get-tuple-element.187), channel_id=1, source_target_pairs={{0,64},{32,96},{64,0},{96,32},{128,192},{160,224},{192,128},{224,1... | collective-permute-start | bytes 258056 | tf_op jit(solution)/shard_map/ppermute | solution.py:417
  36.5 4.6 %collective-permute-start.10 = (f32[168,128]{1,0:T(8,128)S(1)}, f32[168,128]{1,0:T(8,128)S(1)}, u32[]{:S(2)}, u32[]{:S(2)}) collective-permute-start(f32[168,128]{1,0:T(8,128)S(1)} %add.67), channel_id=1, source_target_pairs={{0,192},{32,224},{64,128},{96,160},{128,64},{160,96},{192,0},{224,... | collective-permute-start | bytes 258056 | tf_op jit(solution)/shard_map/ppermute | solution.py:417
  41.1 9.1 %collective-permute-start.13 = (f32[288,128]{1,0:T(8,128)S(1)}, f32[288,128]{1,0:T(8,128)S(1)}, u32[]{:S(2)}, u32[]{:S(2)}) collective-permute-start(f32[288,128]{1,0:T(8,128)S(1)} %get-tuple-element.340), channel_id=1, source_target_pairs={{32,64},{64,32},{96,128},{128,96},{160,192},{192,160},{33,65},{65,... | collective-permute-start | bytes 442376 | tf_op jit(solution)/shard_map/ppermute | solution.py:134
  46.3 3.9 %collective-permute-start.12 = (f32[288,128]{1,0:T(8,128)S(1)}, f32[288,128]{1,0:T(8,128)S(1)}, u32[]{:S(2)}, u32[]{:S(2)}) collective-permute-start(f32[288,128]{1,0:T(8,128)S(1)} %get-tuple-element.341), channel_id=1, source_target_pairs={{0,32},{32,0},{64,96},{96,64},{128,160},{160,128},{192,224},{224,1... | collective-permute-start | bytes 442376 | tf_op jit(solution)/shard_map/ppermute | solution.py:133
  46.4 3.8 %collective-permute-start.11 = (f32[168,128]{1,0:T(8,128)S(1)}, f32[168,128]{1,0:T(8,128)S(1)}, u32[]{:S(2)}, u32[]{:S(2)}) collective-permute-start(f32[168,128]{1,0:T(8,128)S(1)} %add.68), channel_id=1, source_target_pairs={{0,8},{1,9},{2,10},{3,11},{4,12},{5,13},{6,14},{7,15},{8,0},{9,1},... | collective-permute-start | bytes 258056 | tf_op jit(solution)/shard_map/ppermute | solution.py:417
  50.3 5.0 %collective-permute-start.14 = (f32[168,128]{1,0:T(8,128)S(1)}, f32[168,128]{1,0:T(8,128)S(1)}, u32[]{:S(2)}, u32[]{:S(2)}) collective-permute-start(f32[168,128]{1,0:T(8,128)S(1)} %add.69), channel_id=1, source_target_pairs={{0,24},{1,25},{2,26},{3,27},{4,28},{5,29},{6,30},{7,31},{8,16},{9,... | collective-permute-start | bytes 258056 | tf_op jit(solution)/shard_map/ppermute | solution.py:417
  55.3 3.8 %collective-permute-start.15 = (f32[168,128]{1,0:T(8,128)S(1)}, f32[168,128]{1,0:T(8,128)S(1)}, u32[]{:S(2)}, u32[]{:S(2)}) collective-permute-start(f32[168,128]{1,0:T(8,128)S(1)} %add.70), channel_id=1, source_target_pairs={{0,1},{1,0},{2,3},{3,2},{4,5},{5,4},{6,7},{7,6},{8,9},{9,8},{10,11... | collective-permute-start | bytes 258056 | tf_op jit(solution)/shard_map/ppermute | solution.py:417
  59.1 4.6 %collective-permute-start.16 = (f32[168,128]{1,0:T(8,128)S(1)}, f32[168,128]{1,0:T(8,128)S(1)}, u32[]{:S(2)}, u32[]{:S(2)}) collective-permute-start(f32[168,128]{1,0:T(8,128)S(1)} %add.71), channel_id=1, source_target_pairs={{0,7},{1,2},{2,1},{3,4},{4,3},{5,6},{6,5},{7,0},{8,15},{9,10},{10,... | collective-permute-start | bytes 258056 | tf_op jit(solution)/shard_map/ppermute | solution.py:417
  63.8 4.6 %collective-permute-start.19 = (f32[96,128]{1,0:T(8,128)S(1)}, f32[96,128]{1,0:T(8,128)S(1)}, u32[]{:S(2)}, u32[]{:S(2)}) collective-permute-start(f32[96,128]{1,0:T(8,128)S(1)} %get-tuple-element.352), channel_id=1, source_target_pairs={{1,2},{2,1},{3,4},{4,3},{5,6},{6,5},{7,8},{8,7},{9,10},{10,9},{11,... | collective-permute-start | bytes 147464 | tf_op jit(solution)/shard_map/ppermute | solution.py:134
  64.4 4.0 %collective-permute-start.18 = (f32[96,128]{1,0:T(8,128)S(1)}, f32[96,128]{1,0:T(8,128)S(1)}, u32[]{:S(2)}, u32[]{:S(2)}) collective-permute-start(f32[96,128]{1,0:T(8,128)S(1)} %get-tuple-element.353), channel_id=1, source_target_pairs={{0,1},{1,0},{2,3},{3,2},{4,5},{5,4},{6,7},{7,6},{8,9},{9,8},{10,11... | collective-permute-start | bytes 147464 | tf_op jit(solution)/shard_map/ppermute | solution.py:133
  66.0 5.1 %collective-permute-start.17 = (f32[168,128]{1,0:T(8,128)S(1)}, f32[168,128]{1,0:T(8,128)S(1)}, u32[]{:S(2)}, u32[]{:S(2)}) collective-permute-start(f32[168,128]{1,0:T(8,128)S(1)} %add.72), channel_id=1, source_target_pairs={{0,3},{1,6},{2,5},{3,0},{4,7},{5,2},{6,1},{7,4},{8,11},{9,14},{10,... | collective-permute-start | bytes 258056 | tf_op jit(solution)/shard_map/ppermute | solution.py:417
  71.2 3.4 %collective-permute-start.20 = (f32[168,128]{1,0:T(8,128)S(1)}, f32[168,128]{1,0:T(8,128)S(1)}, u32[]{:S(2)}, u32[]{:S(2)}) collective-permute-start(f32[168,128]{1,0:T(8,128)S(1)} %add.73), channel_id=1, source_target_pairs={{0,64},{32,96},{64,0},{96,32},{128,192},{160,224},{192,128},{224,1... | collective-permute-start | bytes 258056 | tf_op jit(solution)/shard_map/ppermute | solution.py:417
  74.6 8.4 %collective-permute-start.21 = (f32[336,128]{1,0:T(8,128)S(1)}, f32[336,128]{1,0:T(8,128)S(1)}, u32[]{:S(2)}, u32[]{:S(2)}) collective-permute-start(f32[336,128]{1,0:T(8,128)S(1)} %maximum_select_fusion.2), channel_id=1, source_target_pairs={{0,32},{32,0},{64,96},{96,64},{128,160},{160,128},{192,224},{224,1... | collective-permute-start | bytes 516104 | tf_op jit(solution)/shard_map/ppermute | solution.py:417
  85.7 1.5 %collective-permute-start.22 = (f32[336,128]{1,0:T(8,128)S(1)}, f32[336,128]{1,0:T(8,128)S(1)}, u32[]{:S(2)}, u32[]{:S(2)}) collective-permute-start(f32[336,128]{1,0:T(8,128)S(1)} %get-tuple-element.260), channel_id=1, source_target_pairs={{0,32},{32,0},{64,96},{96,64},{128,160},{160,128},{192,224},{224,1... | collective-permute-start | bytes 516104 | tf_op jit(solution)/shard_map/ppermute | solution.py:417
  87.2 3.8 %collective-permute-start.23 = (f32[168,128]{1,0:T(8,128)S(1)}, f32[168,128]{1,0:T(8,128)S(1)}, u32[]{:S(2)}, u32[]{:S(2)}) collective-permute-start(f32[168,128]{1,0:T(8,128)S(1)} %get-tuple-element.267), channel_id=1, source_target_pairs={{0,64},{32,96},{64,0},{96,32},{128,192},{160,224},{192,128},{224,1... | collective-permute-start | bytes 258056 | tf_op jit(solution)/shard_map/ppermute | solution.py:417
  91.1 6.5 %collective-permute-start.26 = (f32[48,128]{1,0:T(8,128)S(1)}, f32[48,128]{1,0:T(8,128)S(1)}, u32[]{:S(2)}, u32[]{:S(2)}) collective-permute-start(f32[48,128]{1,0:T(8,128)S(1)} %get-tuple-element.360), channel_id=1, source_target_pairs={{32,64},{64,32},{96,128},{128,96},{160,192},{192,160},{33,65},{65,... | collective-permute-start | bytes 73736 | tf_op jit(solution)/shard_map/ppermute | solution.py:134
  95.4 2.2 %collective-permute-start.25 = (f32[48,128]{1,0:T(8,128)S(1)}, f32[48,128]{1,0:T(8,128)S(1)}, u32[]{:S(2)}, u32[]{:S(2)}) collective-permute-start(f32[48,128]{1,0:T(8,128)S(1)} %get-tuple-element.361), channel_id=1, source_target_pairs={{0,32},{32,0},{64,96},{96,64},{128,160},{160,128},{192,224},{224,1... | collective-permute-start | bytes 73736 | tf_op jit(solution)/shard_map/ppermute | solution.py:133
  95.5 5.0 %collective-permute-start.24 = (f32[168,128]{1,0:T(8,128)S(1)}, f32[168,128]{1,0:T(8,128)S(1)}, u32[]{:S(2)}, u32[]{:S(2)}) collective-permute-start(f32[168,128]{1,0:T(8,128)S(1)} %add.75), channel_id=1, source_target_pairs={{0,192},{32,224},{64,128},{96,160},{128,64},{160,96},{192,0},{224,... | collective-permute-start | bytes 258056 | tf_op jit(solution)/shard_map/ppermute | solution.py:417
  100.5 4.6 %collective-permute-start.27 = (f32[168,128]{1,0:T(8,128)S(1)}, f32[168,128]{1,0:T(8,128)S(1)}, u32[]{:S(2)}, u32[]{:S(2)}) collective-permute-start(f32[168,128]{1,0:T(8,128)S(1)} %add.76), channel_id=1, source_target_pairs={{0,8},{1,9},{2,10},{3,11},{4,12},{5,13},{6,14},{7,15},{8,0},{9,1},... | collective-permute-start | bytes 258056 | tf_op jit(solution)/shard_map/ppermute | solution.py:417
  105.2 4.6 %collective-permute-start.28 = (f32[168,128]{1,0:T(8,128)S(1)}, f32[168,128]{1,0:T(8,128)S(1)}, u32[]{:S(2)}, u32[]{:S(2)}) collective-permute-start(f32[168,128]{1,0:T(8,128)S(1)} %add.77), channel_id=1, source_target_pairs={{0,24},{1,25},{2,26},{3,27},{4,28},{5,29},{6,30},{7,31},{8,16},{9,... | collective-permute-start | bytes 258056 | tf_op jit(solution)/shard_map/ppermute | solution.py:417
  109.8 4.7 %collective-permute-start.29 = (f32[168,128]{1,0:T(8,128)S(1)}, f32[168,128]{1,0:T(8,128)S(1)}, u32[]{:S(2)}, u32[]{:S(2)}) collective-permute-start(f32[168,128]{1,0:T(8,128)S(1)} %add.78), channel_id=1, source_target_pairs={{0,1},{1,0},{2,3},{3,2},{4,5},{5,4},{6,7},{7,6},{8,9},{9,8},{10,11... | collective-permute-start | bytes 258056 | tf_op jit(solution)/shard_map/ppermute | solution.py:417
  114.5 4.6 %collective-permute-start.30 = (f32[168,128]{1,0:T(8,128)S(1)}, f32[168,128]{1,0:T(8,128)S(1)}, u32[]{:S(2)}, u32[]{:S(2)}) collective-permute-start(f32[168,128]{1,0:T(8,128)S(1)} %add.79), channel_id=1, source_target_pairs={{0,7},{1,2},{2,1},{3,4},{4,3},{5,6},{6,5},{7,0},{8,15},{9,10},{10,... | collective-permute-start | bytes 258056 | tf_op jit(solution)/shard_map/ppermute | solution.py:417
  119.3 5.2 %collective-permute-start.33 = (f32[16,128]{1,0:T(8,128)S(1)}, f32[16,128]{1,0:T(8,128)S(1)}, u32[]{:S(2)}, u32[]{:S(2)}) collective-permute-start(f32[16,128]{1,0:T(8,128)S(1)} %get-tuple-element.368), channel_id=1, source_target_pairs={{1,2},{2,1},{3,4},{4,3},{5,6},{6,5},{7,8},{8,7},{9,10},{10,9},{11,... | collective-permute-start | bytes 24584 | tf_op jit(solution)/shard_map/ppermute | solution.py:134
  120.0 4.6 %collective-permute-start.32 = (f32[16,128]{1,0:T(8,128)S(1)}, f32[16,128]{1,0:T(8,128)S(1)}, u32[]{:S(2)}, u32[]{:S(2)}) collective-permute-start(f32[16,128]{1,0:T(8,128)S(1)} %get-tuple-element.369), channel_id=1, source_target_pairs={{0,1},{1,0},{2,3},{3,2},{4,5},{5,4},{6,7},{7,6},{8,9},{9,8},{10,11... | collective-permute-start | bytes 24584 | tf_op jit(solution)/shard_map/ppermute | solution.py:133
  122.9 5.2 %collective-permute-start.31 = (f32[168,128]{1,0:T(8,128)S(1)}, f32[168,128]{1,0:T(8,128)S(1)}, u32[]{:S(2)}, u32[]{:S(2)}) collective-permute-start(f32[168,128]{1,0:T(8,128)S(1)} %add.80), channel_id=1, source_target_pairs={{0,3},{1,6},{2,5},{3,0},{4,7},{5,2},{6,1},{7,4},{8,11},{9,14},{10,... | collective-permute-start | bytes 258056 | tf_op jit(solution)/shard_map/ppermute | solution.py:417
  128.1 3.6 %collective-permute-start.34 = (f32[168,128]{1,0:T(8,128)S(1)}, f32[168,128]{1,0:T(8,128)S(1)}, u32[]{:S(2)}, u32[]{:S(2)}) collective-permute-start(f32[168,128]{1,0:T(8,128)S(1)} %add.81), channel_id=1, source_target_pairs={{0,64},{32,96},{64,0},{96,32},{128,192},{160,224},{192,128},{224,1... | collective-permute-start | bytes 258056 | tf_op jit(solution)/shard_map/ppermute | solution.py:417
  131.8 9.6 %collective-permute-start.35 = (f32[336,128]{1,0:T(8,128)S(1)}, f32[336,128]{1,0:T(8,128)S(1)}, u32[]{:S(2)}, u32[]{:S(2)}) collective-permute-start(f32[336,128]{1,0:T(8,128)S(1)} %maximum_select_fusion.3), channel_id=1, source_target_pairs={{0,32},{32,0},{64,96},{96,64},{128,160},{160,128},{192,224},{224,1... | collective-permute-start | bytes 516104 | tf_op jit(solution)/shard_map/ppermute | solution.py:417

commit v5 on v4

--- a/solution.py
+++ b/solution.py
@@ -493,7 +493,7 @@
     summed, new_maps = sum_all(
         grad,
         (resid, r_top, r_bottom, filt, maps),
-        {2: resid_rows, 7: resid_columns, 8: threshold(True, shape(M, ROWS, LANES))},
+        {0: resid_rows, 1: resid_columns, 2: threshold(True, shape(M, ROWS, LANES))},
     )
     new = call(
         last_kernel,

time: 146 us -> 147 us (level)
  waiting for transfers between devices: 42.5 us -> 44.2 us
    ppermute x8, starting transfers between devices: 15.3 us -> 18.7 us  [neighbours(): lax.ppermute(jnp.where(odd, toward_low, toward_high), axis, even_pairs)]
    ppermute x20, starting transfers between devices: 47.6 us -> 45.6 us  [beside(): other = lax.ppermute(sent, axis, pairs)]
where the time goes in v5:
time: 147 us
  starting transfers between devices  84.4 us (57%)
  waiting for transfers between devices  44.2 us (30%)
  Pallas kernels  14.9 us (10%)
  local copies, waits for them, and re-layouts  1.8 us (1%)
    ppermute x20, starting transfers between devices, beside(): other = lax.ppermute(sent, axis, pairs)  45.6 us
    ppermute x20, waiting for transfers between devices, beside(): other = lax.ppermute(sent, axis, pairs)  39.5 us
    ppermute x8, starting transfers between devices, neighbours(): lax.ppermute(jnp.where(odd, toward_high, toward_low), axis, odd_pairs)  20.1 us
    ppermute x8, starting transfers between devices, neighbours(): lax.ppermute(jnp.where(odd, toward_low, toward_high), axis, even_pairs)  18.7 us
    ppermute x8, waiting for transfers between devices, neighbours(): lax.ppermute(jnp.where(odd, toward_high, toward_low), axis, odd_pairs)  4.69 us
    pallas_call x1, Pallas kernels, local(): call(last_kernel, [shape(M, FLAT)] * 3, [pltpu.VMEM((3, D_ROWS, LANES), F...  3.25 us
    pallas_call x2, Pallas kernels, run(): call(functools.partial(corr_kernel, last), outs, CORR_SCRATCH)  3.21 us
  transfers between devices with their start and end apart: 36, of which 22 were waited for; matrix products, arithmetic and copies ran while one was open for 0% of the time, Pallas kernels for 4%

profile of v5, /device:TPU:1, one launch (start us, length us, event | category | flops | bytes accessed | tf_op | source)
XLA Modules:
  0.0 147.0 jit_solution(14092385303735193343)
XLA Ops:
  0.7 1.0 copy-done
  1.6 0.2 shard_map.84
  1.9 4.6 %collective-permute-start.1 = (f32[288,128]{1,0:T(8,128)S(1)}, f32[288,128]{1,0:T(8,128)S(1)}, u32[]{:S(2)}, u32[]{:S(2)}) collective-permute-start(f32[288,128]{1,0:T(8,128)S(1)} %get-tuple-element.296), channel_id=1, source_target_pairs={{32,64},{64,32},{96,128},{128,96},{160,192},{192,160},{33,65},{65,... | collective-permute-start | bytes 442376 | tf_op jit(solution)/shard_map/ppermute | solution.py:134
  6.6 2.7 %collective-permute-done.1 = f32[288,128]{1,0:T(8,128)S(1)} collective-permute-done((f32[288,128]{1,0:T(8,128)S(1)}, f32[288,128]{1,0:T(8,128)S(1)}, u32[]{:S(2)}, u32[]{:S(2)}) %collective-permute-start.1) | collective-permute-done | bytes 147488 | tf_op jit(solution)/shard_map/ppermute | solution.py:134
  9.4 0.4 shard_map.85
  9.8 0.7 collective-permute-start.3
  10.5 4.6 %collective-permute-start.2 = (f32[96,128]{1,0:T(8,128)S(1)}, f32[96,128]{1,0:T(8,128)S(1)}, u32[]{:S(2)}, u32[]{:S(2)}) collective-permute-start(f32[96,128]{1,0:T(8,128)S(1)} %get-tuple-element.309), channel_id=1, source_target_pairs={{0,1},{1,0},{2,3},{3,2},{4,5},{5,4},{6,7},{7,6},{8,9},{9,8},{10,11... | collective-permute-start | bytes 147464 | tf_op jit(solution)/shard_map/ppermute | solution.py:133
  15.1 2.1 %shard_map.86 = (f32[672,128]{1,0:T(8,128)S(1)}, f32[672,128]{1,0:T(8,128)S(1)}, f32[672,128]{1,0:T(8,128)S(1)}) custom-call(f32[96,784]{1,0:T(8,128)S(1)} %copy-done.1, f32[96,784]{1,0:T(8,128)S(1)} %copy-done.2, f32[96,784]{1,0:T(8,128)S(1)} %copy-done.3), custom_call_target="tpu_custom_call" | custom-call | tf_op jit(solution)/shard_map/pallas_call | solution.py:440
  17.2 0.8 copy-done.4
  18.0 2.5 %shard_map.87 = (f32[128,128]{1,0:T(8,128)S(1)}, f32[48,128]{1,0:T(8,128)S(1)}, f32[48,128]{1,0:T(8,128)S(1)}, f32[672,128]{1,0:T(8,128)S(1)}) custom-call(f32[768,128]{1,0:T(8,128)S(1)} %get-tuple-element.179.own.maps, f32[288,128]{1,0:T(8,128)S(1)} %get-tuple-element.295.above, f32[288,128]{1,0:T(8,128)S(1)} %get-tuple-element.294.below, ...), custom_call_target="tpu_custom_call" | custom-call | tf_op jit(solution)/shard_map/pallas_call | solution.py:444
  20.6 4.2 %collective-permute-start.6 = (f32[48,128]{1,0:T(8,128)S(1)}, f32[48,128]{1,0:T(8,128)S(1)}, u32[]{:S(2)}, u32[]{:S(2)}) collective-permute-start(f32[48,128]{1,0:T(8,128)S(1)} %get-tuple-element.316), channel_id=1, source_target_pairs={{32,64},{64,32},{96,128},{128,96},{160,192},{192,160},{33,65},{65,... | collective-permute-start | bytes 73736 | tf_op jit(solution)/shard_map/ppermute | solution.py:134
  24.9 0.5 collective-permute-start.4
  25.4 0.9 collective-permute-done.6
  26.6 0.7 collective-permute-start.9
  27.3 5.8 %collective-permute-start.8 = (f32[16,128]{1,0:T(8,128)S(1)}, f32[16,128]{1,0:T(8,128)S(1)}, u32[]{:S(2)}, u32[]{:S(2)}) collective-permute-start(f32[16,128]{1,0:T(8,128)S(1)} %get-tuple-element.325), channel_id=1, source_target_pairs={{0,1},{1,0},{2,3},{3,2},{4,5},{5,4},{6,7},{7,6},{8,9},{9,8},{10,11... | collective-permute-start | bytes 24584 | tf_op jit(solution)/shard_map/ppermute | solution.py:133
  33.1 1.3 collective-permute-start.7
  34.5 2.0 %collective-permute-done.7 = f32[168,128]{1,0:T(8,128)S(1)} collective-permute-done((f32[168,128]{1,0:T(8,128)S(1)}, f32[168,128]{1,0:T(8,128)S(1)}, u32[]{:S(2)}, u32[]{:S(2)}) %collective-permute-start.7) | collective-permute-done | bytes 86048 | tf_op jit(solution)/shard_map/ppermute | solution.py:417
  36.5 1.7 %collective-permute-start.10 = (f32[168,128]{1,0:T(8,128)S(1)}, f32[168,128]{1,0:T(8,128)S(1)}, u32[]{:S(2)}, u32[]{:S(2)}) collective-permute-start(f32[168,128]{1,0:T(8,128)S(1)} %add.67), channel_id=1, source_target_pairs={{0,192},{32,224},{64,128},{96,160},{128,64},{160,96},{192,0},{224,... | collective-permute-start | bytes 258056 | tf_op jit(solution)/shard_map/ppermute | solution.py:417
  38.2 1.2 shard_map.89
  39.4 1.7 %collective-permute-done.10 = f32[168,128]{1,0:T(8,128)S(1)} collective-permute-done((f32[168,128]{1,0:T(8,128)S(1)}, f32[168,128]{1,0:T(8,128)S(1)}, u32[]{:S(2)}, u32[]{:S(2)}) %collective-permute-start.10) | collective-permute-done | bytes 86048 | tf_op jit(solution)/shard_map/ppermute | solution.py:417
  41.1 5.2 %collective-permute-start.13 = (f32[288,128]{1,0:T(8,128)S(1)}, f32[288,128]{1,0:T(8,128)S(1)}, u32[]{:S(2)}, u32[]{:S(2)}) collective-permute-start(f32[288,128]{1,0:T(8,128)S(1)} %get-tuple-element.292), channel_id=1, source_target_pairs={{32,64},{64,32},{96,128},{128,96},{160,192},{192,160},{33,65},{65,... | collective-permute-start | bytes 442376 | tf_op jit(solution)/shard_map/ppermute | solution.py:134
  46.4 1.5 %collective-permute-start.11 = (f32[168,128]{1,0:T(8,128)S(1)}, f32[168,128]{1,0:T(8,128)S(1)}, u32[]{:S(2)}, u32[]{:S(2)}) collective-permute-start(f32[168,128]{1,0:T(8,128)S(1)} %add.68), channel_id=1, source_target_pairs={{0,8},{1,9},{2,10},{3,11},{4,12},{5,13},{6,14},{7,15},{8,0},{9,1},... | collective-permute-start | bytes 258056 | tf_op jit(solution)/shard_map/ppermute | solution.py:417
  48.0 2.3 %collective-permute-done.11 = f32[168,128]{1,0:T(8,128)S(1)} collective-permute-done((f32[168,128]{1,0:T(8,128)S(1)}, f32[168,128]{1,0:T(8,128)S(1)}, u32[]{:S(2)}, u32[]{:S(2)}) %collective-permute-start.11) | collective-permute-done | bytes 86048 | tf_op jit(solution)/shard_map/ppermute | solution.py:417
  50.3 3.1 %collective-permute-start.14 = (f32[168,128]{1,0:T(8,128)S(1)}, f32[168,128]{1,0:T(8,128)S(1)}, u32[]{:S(2)}, u32[]{:S(2)}) collective-permute-start(f32[168,128]{1,0:T(8,128)S(1)} %add.69), channel_id=1, source_target_pairs={{0,24},{1,25},{2,26},{3,27},{4,28},{5,29},{6,30},{7,31},{8,16},{9,... | collective-permute-start | bytes 258056 | tf_op jit(solution)/shard_map/ppermute | solution.py:417
  53.4 1.9 %collective-permute-done.14 = f32[168,128]{1,0:T(8,128)S(1)} collective-permute-done((f32[168,128]{1,0:T(8,128)S(1)}, f32[168,128]{1,0:T(8,128)S(1)}, u32[]{:S(2)}, u32[]{:S(2)}) %collective-permute-start.14) | collective-permute-done | bytes 86048 | tf_op jit(solution)/shard_map/ppermute | solution.py:417
  55.3 1.9 %collective-permute-start.15 = (f32[168,128]{1,0:T(8,128)S(1)}, f32[168,128]{1,0:T(8,128)S(1)}, u32[]{:S(2)}, u32[]{:S(2)}) collective-permute-start(f32[168,128]{1,0:T(8,128)S(1)} %add.70), channel_id=1, source_target_pairs={{0,1},{1,0},{2,3},{3,2},{4,5},{5,4},{6,7},{7,6},{8,9},{9,8},{10,11... | collective-permute-start | bytes 258056 | tf_op jit(solution)/shard_map/ppermute | solution.py:417
  57.2 0.4 shard_map.90
  57.6 1.5 collective-permute-done.15
  59.1 1.9 %collective-permute-start.16 = (f32[168,128]{1,0:T(8,128)S(1)}, f32[168,128]{1,0:T(8,128)S(1)}, u32[]{:S(2)}, u32[]{:S(2)}) collective-permute-start(f32[168,128]{1,0:T(8,128)S(1)} %add.71), channel_id=1, source_target_pairs={{0,7},{1,2},{2,1},{3,4},{4,3},{5,6},{6,5},{7,0},{8,15},{9,10},{10,... | collective-permute-start | bytes 258056 | tf_op jit(solution)/shard_map/ppermute | solution.py:417
  60.9 2.8 %collective-permute-done.16 = f32[168,128]{1,0:T(8,128)S(1)} collective-permute-done((f32[168,128]{1,0:T(8,128)S(1)}, f32[168,128]{1,0:T(8,128)S(1)}, u32[]{:S(2)}, u32[]{:S(2)}) %collective-permute-start.16) | collective-permute-done | bytes 86048 | tf_op jit(solution)/shard_map/ppermute | solution.py:417
  63.8 0.7 collective-permute-start.19
  64.4 1.6 %collective-permute-start.18 = (f32[96,128]{1,0:T(8,128)S(1)}, f32[96,128]{1,0:T(8,128)S(1)}, u32[]{:S(2)}, u32[]{:S(2)}) collective-permute-start(f32[96,128]{1,0:T(8,128)S(1)} %get-tuple-element.305), channel_id=1, source_target_pairs={{0,1},{1,0},{2,3},{3,2},{4,5},{5,4},{6,7},{7,6},{8,9},{9,8},{10,11... | collective-permute-start | bytes 147464 | tf_op jit(solution)/shard_map/ppermute | solution.py:133
  66.0 2.4 %collective-permute-start.17 = (f32[168,128]{1,0:T(8,128)S(1)}, f32[168,128]{1,0:T(8,128)S(1)}, u32[]{:S(2)}, u32[]{:S(2)}) collective-permute-start(f32[168,128]{1,0:T(8,128)S(1)} %add.72), channel_id=1, source_target_pairs={{0,3},{1,6},{2,5},{3,0},{4,7},{5,2},{6,1},{7,4},{8,11},{9,14},{10,... | collective-permute-start | bytes 258056 | tf_op jit(solution)/shard_map/ppermute | solution.py:417
  68.4 2.8 %collective-permute-done.17 = f32[168,128]{1,0:T(8,128)S(1)} collective-permute-done((f32[168,128]{1,0:T(8,128)S(1)}, f32[168,128]{1,0:T(8,128)S(1)}, u32[]{:S(2)}, u32[]{:S(2)}) %collective-permute-start.17) | collective-permute-done | bytes 86048 | tf_op jit(solution)/shard_map/ppermute | solution.py:417
  71.2 1.4 collective-permute-start.20
  72.5 2.0 %collective-permute-done.20 = f32[168,128]{1,0:T(8,128)S(1)} collective-permute-done((f32[168,128]{1,0:T(8,128)S(1)}, f32[168,128]{1,0:T(8,128)S(1)}, u32[]{:S(2)}, u32[]{:S(2)}) %collective-permute-start.20) | collective-permute-done | bytes 86048 | tf_op jit(solution)/shard_map/ppermute | solution.py:417
  74.6 7.4 %collective-permute-start.21 = (f32[336,128]{1,0:T(8,128)S(1)}, f32[336,128]{1,0:T(8,128)S(1)}, u32[]{:S(2)}, u32[]{:S(2)}) collective-permute-start(f32[336,128]{1,0:T(8,128)S(1)} %maximum_select_fusion.2), channel_id=1, source_target_pairs={{0,32},{32,0},{64,96},{96,64},{128,160},{160,128},{192,224},{224,1... | collective-permute-start | bytes 516104 | tf_op jit(solution)/shard_map/ppermute | solution.py:417
  82.0 1.0 collective-permute-done.21
  83.1 2.6 %shard_map.91 = (f32[672,128]{1,0:T(8,128)S(1)}, f32[672,128]{1,0:T(8,128)S(1)}, f32[672,128]{1,0:T(8,128)S(1)}, f32[128,128]{1,0:T(8,128)S(1)}, f32[48,128]{1,0...) custom-call(f32[672,128]{1,0:T(8,128)S(1)} %maximum_select_fusion.summed, ...), custom_call_target="tpu_custom_call" | custom-call | tf_op jit(solution)/shard_map/pallas_call | solution.py:490
  85.7 3.5 %collective-permute-start.24 = (f32[48,128]{1,0:T(8,128)S(1)}, f32[48,128]{1,0:T(8,128)S(1)}, u32[]{:S(2)}, u32[]{:S(2)}) collective-permute-start(f32[48,128]{1,0:T(8,128)S(1)} %get-tuple-element.312), channel_id=1, source_target_pairs={{32,64},{64,32},{96,128},{128,96},{160,192},{192,160},{33,65},{65,... | collective-permute-start | bytes 73736 | tf_op jit(solution)/shard_map/ppermute | solution.py:134
  89.3 0.5 collective-permute-start.22
  89.8 1.1 collective-permute-done.24
  91.1 0.7 collective-permute-start.27
  91.7 6.3 %collective-permute-start.26 = (f32[16,128]{1,0:T(8,128)S(1)}, f32[16,128]{1,0:T(8,128)S(1)}, u32[]{:S(2)}, u32[]{:S(2)}) collective-permute-start(f32[16,128]{1,0:T(8,128)S(1)} %get-tuple-element.321), channel_id=1, source_target_pairs={{0,1},{1,0},{2,3},{3,2},{4,5},{5,4},{6,7},{7,6},{8,9},{9,8},{10,11... | collective-permute-start | bytes 24584 | tf_op jit(solution)/shard_map/ppermute | solution.py:133
  98.1 2.1 %collective-permute-start.25 = (f32[168,128]{1,0:T(8,128)S(1)}, f32[168,128]{1,0:T(8,128)S(1)}, u32[]{:S(2)}, u32[]{:S(2)}) collective-permute-start(f32[168,128]{1,0:T(8,128)S(1)} %get-tuple-element.243), channel_id=1, source_target_pairs={{0,64},{32,96},{64,0},{96,32},{128,192},{160,224},{192,128},{224,1... | collective-permute-start | bytes 258056 | tf_op jit(solution)/shard_map/ppermute | solution.py:417
  100.2 1.9 %collective-permute-done.25 = f32[168,128]{1,0:T(8,128)S(1)} collective-permute-done((f32[168,128]{1,0:T(8,128)S(1)}, f32[168,128]{1,0:T(8,128)S(1)}, u32[]{:S(2)}, u32[]{:S(2)}) %collective-permute-start.25) | collective-permute-done | bytes 86048 | tf_op jit(solution)/shard_map/ppermute | solution.py:417
  102.1 2.2 %collective-permute-start.28 = (f32[168,128]{1,0:T(8,128)S(1)}, f32[168,128]{1,0:T(8,128)S(1)}, u32[]{:S(2)}, u32[]{:S(2)}) collective-permute-start(f32[168,128]{1,0:T(8,128)S(1)} %add.75), channel_id=1, source_target_pairs={{0,192},{32,224},{64,128},{96,160},{128,64},{160,96},{192,0},{224,... | collective-permute-start | bytes 258056 | tf_op jit(solution)/shard_map/ppermute | solution.py:417
  104.2 2.0 %shard_map.93 = f32[96,8,128]{2,1,0:T(8,128)} custom-call(f32[128,128]{1,0:T(8,128)S(1)} %get-tuple-element.253.own.resid, f32[48,128]{1,0:T(8,128)S(1)} %get-tuple-element.254.above, f32[48,128]{1,0:T(8,128)S(1)} %get-tuple-element.255.below, f32[16,128]{1,0:T(8,128)S(1)} %get-tuple-element.256.left, f32[16,128]{1,0:T(8,128)S(1)} %get-tuple-element.257.right, ...), custom_call_target="tpu_custom_call" | custom-call | tf_op jit(solution)/shard_map/pallas_call | solution.py:460
  106.3 0.4 collective-permute-done.28
  106.7 0.9 collective-permute-start.29
  107.7 2.5 %collective-permute-done.29 = f32[168,128]{1,0:T(8,128)S(1)} collective-permute-done((f32[168,128]{1,0:T(8,128)S(1)}, f32[168,128]{1,0:T(8,128)S(1)}, u32[]{:S(2)}, u32[]{:S(2)}) %collective-permute-start.29) | collective-permute-done | bytes 86048 | tf_op jit(solution)/shard_map/ppermute | solution.py:417
  110.2 2.3 %collective-permute-start.30 = (f32[168,128]{1,0:T(8,128)S(1)}, f32[168,128]{1,0:T(8,128)S(1)}, u32[]{:S(2)}, u32[]{:S(2)}) collective-permute-start(f32[168,128]{1,0:T(8,128)S(1)} %add.77), channel_id=1, source_target_pairs={{0,24},{1,25},{2,26},{3,27},{4,28},{5,29},{6,30},{7,31},{8,16},{9,... | collective-permute-start | bytes 258056 | tf_op jit(solution)/shard_map/ppermute | solution.py:417
  112.5 2.3 %collective-permute-done.30 = f32[168,128]{1,0:T(8,128)S(1)} collective-permute-done((f32[168,128]{1,0:T(8,128)S(1)}, f32[168,128]{1,0:T(8,128)S(1)}, u32[]{:S(2)}, u32[]{:S(2)}) %collective-permute-start.30) | collective-permute-done | bytes 86048 | tf_op jit(solution)/shard_map/ppermute | solution.py:417
  114.8 0.6 collective-permute-start.31
  115.4 2.8 %collective-permute-done.31 = f32[168,128]{1,0:T(8,128)S(1)} collective-permute-done((f32[168,128]{1,0:T(8,128)S(1)}, f32[168,128]{1,0:T(8,128)S(1)}, u32[]{:S(2)}, u32[]{:S(2)}) %collective-permute-start.31) | collective-permute-done | bytes 86048 | tf_op jit(solution)/shard_map/ppermute | solution.py:417
  118.3 1.6 %collective-permute-start.32 = (f32[168,128]{1,0:T(8,128)S(1)}, f32[168,128]{1,0:T(8,128)S(1)}, u32[]{:S(2)}, u32[]{:S(2)}) collective-permute-start(f32[168,128]{1,0:T(8,128)S(1)} %add.79), channel_id=1, source_target_pairs={{0,7},{1,2},{2,1},{3,4},{4,3},{5,6},{6,5},{7,0},{8,15},{9,10},{10,... | collective-permute-start | bytes 258056 | tf_op jit(solution)/shard_map/ppermute | solution.py:417
  119.8 3.0 %collective-permute-done.32 = f32[168,128]{1,0:T(8,128)S(1)} collective-permute-done((f32[168,128]{1,0:T(8,128)S(1)}, f32[168,128]{1,0:T(8,128)S(1)}, u32[]{:S(2)}, u32[]{:S(2)}) %collective-permute-start.32) | collective-permute-done | bytes 86048 | tf_op jit(solution)/shard_map/ppermute | solution.py:417
  122.9 1.9 %collective-permute-start.33 = (f32[168,128]{1,0:T(8,128)S(1)}, f32[168,128]{1,0:T(8,128)S(1)}, u32[]{:S(2)}, u32[]{:S(2)}) collective-permute-start(f32[168,128]{1,0:T(8,128)S(1)} %add.80), channel_id=1, source_target_pairs={{0,3},{1,6},{2,5},{3,0},{4,7},{5,2},{6,1},{7,4},{8,11},{9,14},{10,... | collective-permute-start | bytes 258056 | tf_op jit(solution)/shard_map/ppermute | solution.py:417
  124.8 4.4 %collective-permute-done.33 = f32[168,128]{1,0:T(8,128)S(1)} collective-permute-done((f32[168,128]{1,0:T(8,128)S(1)}, f32[168,128]{1,0:T(8,128)S(1)}, u32[]{:S(2)}, u32[]{:S(2)}) %collective-permute-start.33) | collective-permute-done | bytes 86048 | tf_op jit(solution)/shard_map/ppermute | solution.py:417
  129.3 0.4 collective-permute-start.34
  129.7 3.0 %collective-permute-done.34 = f32[168,128]{1,0:T(8,128)S(1)} collective-permute-done((f32[168,128]{1,0:T(8,128)S(1)}, f32[168,128]{1,0:T(8,128)S(1)}, u32[]{:S(2)}, u32[]{:S(2)}) %collective-permute-start.34) | collective-permute-done | bytes 86048 | tf_op jit(solution)/shard_map/ppermute | solution.py:417
  132.7 9.9 %collective-permute-start.35 = (f32[336,128]{1,0:T(8,128)S(1)}, f32[336,128]{1,0:T(8,128)S(1)}, u32[]{:S(2)}, u32[]{:S(2)}) collective-permute-start(f32[336,128]{1,0:T(8,128)S(1)} %maximum_select_fusion.3), channel_id=1, source_target_pairs={{0,32},{32,0},{64,96},{96,64},{128,160},{160,128},{192,224},{224,1... | collective-permute-start | bytes 516104 | tf_op jit(solution)/shard_map/ppermute | solution.py:417
  142.7 1.0 collective-permute-done.35
  143.7 3.3 %shard_map.94 = (f32[96,784]{1,0:T(8,128)}, f32[96,784]{1,0:T(8,128)}, f32[96,784]{1,0:T(8,128)}) custom-call(f32[672,128]{1,0:T(8,128)S(1)} %maximum_select_fusion.1.summed, f32[672,128]{1,0:T(8,128)S(1)} %get-tuple-element.258.filt, f32[672,128]{1,0:T(8,128)S(1)} %get-tuple-element.281.cons, f32[672,128]{1,0:T(8,128)S(1)} %get-tuple-element.282.duals), custom_call_target="tpu_custom_call" | custom-call | tf_op jit(solution)/shard_map/pallas_call | solution.py:498
  (69 shorter events, 1.4 us)
Async XLA Ops:
  0.6 1.0 copy-start
  1.9 7.4 %collective-permute-start.1 = (f32[288,128]{1,0:T(8,128)S(1)}, f32[288,128]{1,0:T(8,128)S(1)}, u32[]{:S(2)}, u32[]{:S(2)}) collective-permute-start(f32[288,128]{1,0:T(8,128)S(1)} %get-tuple-element.296), channel_id=1, source_target_pairs={{32,64},{64,32},{96,128},{128,96},{160,192},{192,160},{33,65},{65,... | collective-permute-start | bytes 442376 | tf_op jit(solution)/shard_map/ppermute | solution.py:134
  6.5 2.8 %collective-permute-start = (f32[288,128]{1,0:T(8,128)S(1)}, f32[288,128]{1,0:T(8,128)S(1)}, u32[]{:S(2)}, u32[]{:S(2)}) collective-permute-start(f32[288,128]{1,0:T(8,128)S(1)} %get-tuple-element.297), channel_id=1, source_target_pairs={{0,32},{32,0},{64,96},{96,64},{128,160},{160,128},{192,224},{224,1... | collective-permute-start | bytes 442376 | tf_op jit(solution)/shard_map/ppermute | solution.py:133
  9.3 5.8 %copy-start.3 = (f32[96,784]{1,0:T(8,128)S(1)}, f32[96,784]{1,0:T(8,128)}, u32[]{:S(2)}) copy-start(f32[96,784]{1,0:T(8,128)} %duals.1) | copy-start | bytes 903172
  9.3 5.7 %copy-start.1 = (f32[96,784]{1,0:T(8,128)S(1)}, f32[96,784]{1,0:T(8,128)}, u32[]{:S(2)}) copy-start(f32[96,784]{1,0:T(8,128)} %filt.1) | copy-start | bytes 903172
  9.4 5.7 %copy-start.2 = (f32[96,784]{1,0:T(8,128)S(1)}, f32[96,784]{1,0:T(8,128)}, u32[]{:S(2)}) copy-start(f32[96,784]{1,0:T(8,128)} %cons.1) | copy-start | bytes 903172
  9.8 7.4 %collective-permute-start.3 = (f32[96,128]{1,0:T(8,128)S(1)}, f32[96,128]{1,0:T(8,128)S(1)}, u32[]{:S(2)}, u32[]{:S(2)}) collective-permute-start(f32[96,128]{1,0:T(8,128)S(1)} %get-tuple-element.308), channel_id=1, source_target_pairs={{1,2},{2,1},{3,4},{4,3},{5,6},{6,5},{7,8},{8,7},{9,10},{10,9},{11,... | collective-permute-start | bytes 147464 | tf_op jit(solution)/shard_map/ppermute | solution.py:134
  10.5 6.7 %collective-permute-start.2 = (f32[96,128]{1,0:T(8,128)S(1)}, f32[96,128]{1,0:T(8,128)S(1)}, u32[]{:S(2)}, u32[]{:S(2)}) collective-permute-start(f32[96,128]{1,0:T(8,128)S(1)} %get-tuple-element.309), channel_id=1, source_target_pairs={{0,1},{1,0},{2,3},{3,2},{4,5},{5,4},{6,7},{7,6},{8,9},{9,8},{10,11... | collective-permute-start | bytes 147464 | tf_op jit(solution)/shard_map/ppermute | solution.py:133
  17.2 0.8 copy-start.4
  20.6 5.7 %collective-permute-start.6 = (f32[48,128]{1,0:T(8,128)S(1)}, f32[48,128]{1,0:T(8,128)S(1)}, u32[]{:S(2)}, u32[]{:S(2)}) collective-permute-start(f32[48,128]{1,0:T(8,128)S(1)} %get-tuple-element.316), channel_id=1, source_target_pairs={{32,64},{64,32},{96,128},{128,96},{160,192},{192,160},{33,65},{65,... | collective-permute-start | bytes 73736 | tf_op jit(solution)/shard_map/ppermute | solution.py:134
  24.8 1.5 %collective-permute-start.5 = (f32[48,128]{1,0:T(8,128)S(1)}, f32[48,128]{1,0:T(8,128)S(1)}, u32[]{:S(2)}, u32[]{:S(2)}) collective-permute-start(f32[48,128]{1,0:T(8,128)S(1)} %get-tuple-element.317), channel_id=1, source_target_pairs={{0,32},{32,0},{64,96},{96,64},{128,160},{160,128},{192,224},{224,1... | collective-permute-start | bytes 73736 | tf_op jit(solution)/shard_map/ppermute | solution.py:133
  24.9 1.5 %collective-permute-start.4 = (f32[336,128]{1,0:T(8,128)S(1)}, f32[336,128]{1,0:T(8,128)S(1)}, u32[]{:S(2)}, u32[]{:S(2)}) collective-permute-start(f32[336,128]{1,0:T(8,128)S(1)} %get-tuple-element.156), channel_id=1, source_target_pairs={{0,32},{32,0},{64,96},{96,64},{128,160},{160,128},{192,224},{224,1... | collective-permute-start | bytes 516104 | tf_op jit(solution)/shard_map/ppermute | solution.py:417
  26.6 7.8 %collective-permute-start.9 = (f32[16,128]{1,0:T(8,128)S(1)}, f32[16,128]{1,0:T(8,128)S(1)}, u32[]{:S(2)}, u32[]{:S(2)}) collective-permute-start(f32[16,128]{1,0:T(8,128)S(1)} %get-tuple-element.324), channel_id=1, source_target_pairs={{1,2},{2,1},{3,4},{4,3},{5,6},{6,5},{7,8},{8,7},{9,10},{10,9},{11,... | collective-permute-start | bytes 24584 | tf_op jit(solution)/shard_map/ppermute | solution.py:134
  27.3 7.2 %collective-permute-start.8 = (f32[16,128]{1,0:T(8,128)S(1)}, f32[16,128]{1,0:T(8,128)S(1)}, u32[]{:S(2)}, u32[]{:S(2)}) collective-permute-start(f32[16,128]{1,0:T(8,128)S(1)} %get-tuple-element.325), channel_id=1, source_target_pairs={{0,1},{1,0},{2,3},{3,2},{4,5},{5,4},{6,7},{7,6},{8,9},{9,8},{10,11... | collective-permute-start | bytes 24584 | tf_op jit(solution)/shard_map/ppermute | solution.py:133
  33.1 3.3 %collective-permute-start.7 = (f32[168,128]{1,0:T(8,128)S(1)}, f32[168,128]{1,0:T(8,128)S(1)}, u32[]{:S(2)}, u32[]{:S(2)}) collective-permute-start(f32[168,128]{1,0:T(8,128)S(1)} %get-tuple-element.163), channel_id=1, source_target_pairs={{0,64},{32,96},{64,0},{96,32},{128,192},{160,224},{192,128},{224,1... | collective-permute-start | bytes 258056 | tf_op jit(solution)/shard_map/ppermute | solution.py:417
  36.5 4.6 %collective-permute-start.10 = (f32[168,128]{1,0:T(8,128)S(1)}, f32[168,128]{1,0:T(8,128)S(1)}, u32[]{:S(2)}, u32[]{:S(2)}) collective-permute-start(f32[168,128]{1,0:T(8,128)S(1)} %add.67), channel_id=1, source_target_pairs={{0,192},{32,224},{64,128},{96,160},{128,64},{160,96},{192,0},{224,... | collective-permute-start | bytes 258056 | tf_op jit(solution)/shard_map/ppermute | solution.py:417
  41.1 9.1 %collective-permute-start.13 = (f32[288,128]{1,0:T(8,128)S(1)}, f32[288,128]{1,0:T(8,128)S(1)}, u32[]{:S(2)}, u32[]{:S(2)}) collective-permute-start(f32[288,128]{1,0:T(8,128)S(1)} %get-tuple-element.292), channel_id=1, source_target_pairs={{32,64},{64,32},{96,128},{128,96},{160,192},{192,160},{33,65},{65,... | collective-permute-start | bytes 442376 | tf_op jit(solution)/shard_map/ppermute | solution.py:134
  46.3 3.9 %collective-permute-start.12 = (f32[288,128]{1,0:T(8,128)S(1)}, f32[288,128]{1,0:T(8,128)S(1)}, u32[]{:S(2)}, u32[]{:S(2)}) collective-permute-start(f32[288,128]{1,0:T(8,128)S(1)} %get-tuple-element.293), channel_id=1, source_target_pairs={{0,32},{32,0},{64,96},{96,64},{128,160},{160,128},{192,224},{224,1... | collective-permute-start | bytes 442376 | tf_op jit(solution)/shard_map/ppermute | solution.py:133
  46.4 3.8 %collective-permute-start.11 = (f32[168,128]{1,0:T(8,128)S(1)}, f32[168,128]{1,0:T(8,128)S(1)}, u32[]{:S(2)}, u32[]{:S(2)}) collective-permute-start(f32[168,128]{1,0:T(8,128)S(1)} %add.68), channel_id=1, source_target_pairs={{0,8},{1,9},{2,10},{3,11},{4,12},{5,13},{6,14},{7,15},{8,0},{9,1},... | collective-permute-start | bytes 258056 | tf_op jit(solution)/shard_map/ppermute | solution.py:417
  50.3 5.0 %collective-permute-start.14 = (f32[168,128]{1,0:T(8,128)S(1)}, f32[168,128]{1,0:T(8,128)S(1)}, u32[]{:S(2)}, u32[]{:S(2)}) collective-permute-start(f32[168,128]{1,0:T(8,128)S(1)} %add.69), channel_id=1, source_target_pairs={{0,24},{1,25},{2,26},{3,27},{4,28},{5,29},{6,30},{7,31},{8,16},{9,... | collective-permute-start | bytes 258056 | tf_op jit(solution)/shard_map/ppermute | solution.py:417
  55.3 3.8 %collective-permute-start.15 = (f32[168,128]{1,0:T(8,128)S(1)}, f32[168,128]{1,0:T(8,128)S(1)}, u32[]{:S(2)}, u32[]{:S(2)}) collective-permute-start(f32[168,128]{1,0:T(8,128)S(1)} %add.70), channel_id=1, source_target_pairs={{0,1},{1,0},{2,3},{3,2},{4,5},{5,4},{6,7},{7,6},{8,9},{9,8},{10,11... | collective-permute-start | bytes 258056 | tf_op jit(solution)/shard_map/ppermute | solution.py:417
  59.1 4.6 %collective-permute-start.16 = (f32[168,128]{1,0:T(8,128)S(1)}, f32[168,128]{1,0:T(8,128)S(1)}, u32[]{:S(2)}, u32[]{:S(2)}) collective-permute-start(f32[168,128]{1,0:T(8,128)S(1)} %add.71), channel_id=1, source_target_pairs={{0,7},{1,2},{2,1},{3,4},{4,3},{5,6},{6,5},{7,0},{8,15},{9,10},{10,... | collective-permute-start | bytes 258056 | tf_op jit(solution)/shard_map/ppermute | solution.py:417
  63.8 4.6 %collective-permute-start.19 = (f32[96,128]{1,0:T(8,128)S(1)}, f32[96,128]{1,0:T(8,128)S(1)}, u32[]{:S(2)}, u32[]{:S(2)}) collective-permute-start(f32[96,128]{1,0:T(8,128)S(1)} %get-tuple-element.304), channel_id=1, source_target_pairs={{1,2},{2,1},{3,4},{4,3},{5,6},{6,5},{7,8},{8,7},{9,10},{10,9},{11,... | collective-permute-start | bytes 147464 | tf_op jit(solution)/shard_map/ppermute | solution.py:134
  64.4 4.0 %collective-permute-start.18 = (f32[96,128]{1,0:T(8,128)S(1)}, f32[96,128]{1,0:T(8,128)S(1)}, u32[]{:S(2)}, u32[]{:S(2)}) collective-permute-start(f32[96,128]{1,0:T(8,128)S(1)} %get-tuple-element.305), channel_id=1, source_target_pairs={{0,1},{1,0},{2,3},{3,2},{4,5},{5,4},{6,7},{7,6},{8,9},{9,8},{10,11... | collective-permute-start | bytes 147464 | tf_op jit(solution)/shard_map/ppermute | solution.py:133
  66.0 5.1 %collective-permute-start.17 = (f32[168,128]{1,0:T(8,128)S(1)}, f32[168,128]{1,0:T(8,128)S(1)}, u32[]{:S(2)}, u32[]{:S(2)}) collective-permute-start(f32[168,128]{1,0:T(8,128)S(1)} %add.72), channel_id=1, source_target_pairs={{0,3},{1,6},{2,5},{3,0},{4,7},{5,2},{6,1},{7,4},{8,11},{9,14},{10,... | collective-permute-start | bytes 258056 | tf_op jit(solution)/shard_map/ppermute | solution.py:417
  71.2 3.4 %collective-permute-start.20 = (f32[168,128]{1,0:T(8,128)S(1)}, f32[168,128]{1,0:T(8,128)S(1)}, u32[]{:S(2)}, u32[]{:S(2)}) collective-permute-start(f32[168,128]{1,0:T(8,128)S(1)} %add.73), channel_id=1, source_target_pairs={{0,64},{32,96},{64,0},{96,32},{128,192},{160,224},{192,128},{224,1... | collective-permute-start | bytes 258056 | tf_op jit(solution)/shard_map/ppermute | solution.py:417
  74.6 8.4 %collective-permute-start.21 = (f32[336,128]{1,0:T(8,128)S(1)}, f32[336,128]{1,0:T(8,128)S(1)}, u32[]{:S(2)}, u32[]{:S(2)}) collective-permute-start(f32[336,128]{1,0:T(8,128)S(1)} %maximum_select_fusion.2), channel_id=1, source_target_pairs={{0,32},{32,0},{64,96},{96,64},{128,160},{160,128},{192,224},{224,1... | collective-permute-start | bytes 516104 | tf_op jit(solution)/shard_map/ppermute | solution.py:417
  85.7 5.1 %collective-permute-start.24 = (f32[48,128]{1,0:T(8,128)S(1)}, f32[48,128]{1,0:T(8,128)S(1)}, u32[]{:S(2)}, u32[]{:S(2)}) collective-permute-start(f32[48,128]{1,0:T(8,128)S(1)} %get-tuple-element.312), channel_id=1, source_target_pairs={{32,64},{64,32},{96,128},{128,96},{160,192},{192,160},{33,65},{65,... | collective-permute-start | bytes 73736 | tf_op jit(solution)/shard_map/ppermute | solution.py:134
  89.2 1.7 %collective-permute-start.23 = (f32[48,128]{1,0:T(8,128)S(1)}, f32[48,128]{1,0:T(8,128)S(1)}, u32[]{:S(2)}, u32[]{:S(2)}) collective-permute-start(f32[48,128]{1,0:T(8,128)S(1)} %get-tuple-element.313), channel_id=1, source_target_pairs={{0,32},{32,0},{64,96},{96,64},{128,160},{160,128},{192,224},{224,1... | collective-permute-start | bytes 73736 | tf_op jit(solution)/shard_map/ppermute | solution.py:133
  89.3 1.6 %collective-permute-start.22 = (f32[336,128]{1,0:T(8,128)S(1)}, f32[336,128]{1,0:T(8,128)S(1)}, u32[]{:S(2)}, u32[]{:S(2)}) collective-permute-start(f32[336,128]{1,0:T(8,128)S(1)} %get-tuple-element.236), channel_id=1, source_target_pairs={{0,32},{32,0},{64,96},{96,64},{128,160},{160,128},{192,224},{224,1... | collective-permute-start | bytes 516104 | tf_op jit(solution)/shard_map/ppermute | solution.py:417
  91.1 9.1 %collective-permute-start.27 = (f32[16,128]{1,0:T(8,128)S(1)}, f32[16,128]{1,0:T(8,128)S(1)}, u32[]{:S(2)}, u32[]{:S(2)}) collective-permute-start(f32[16,128]{1,0:T(8,128)S(1)} %get-tuple-element.320), channel_id=1, source_target_pairs={{1,2},{2,1},{3,4},{4,3},{5,6},{6,5},{7,8},{8,7},{9,10},{10,9},{11,... | collective-permute-start | bytes 24584 | tf_op jit(solution)/shard_map/ppermute | solution.py:134
  91.7 8.5 %collective-permute-start.26 = (f32[16,128]{1,0:T(8,128)S(1)}, f32[16,128]{1,0:T(8,128)S(1)}, u32[]{:S(2)}, u32[]{:S(2)}) collective-permute-start(f32[16,128]{1,0:T(8,128)S(1)} %get-tuple-element.321), channel_id=1, source_target_pairs={{0,1},{1,0},{2,3},{3,2},{4,5},{5,4},{6,7},{7,6},{8,9},{9,8},{10,11... | collective-permute-start | bytes 24584 | tf_op jit(solution)/shard_map/ppermute | solution.py:133
  98.1 4.0 %collective-permute-start.25 = (f32[168,128]{1,0:T(8,128)S(1)}, f32[168,128]{1,0:T(8,128)S(1)}, u32[]{:S(2)}, u32[]{:S(2)}) collective-permute-start(f32[168,128]{1,0:T(8,128)S(1)} %get-tuple-element.243), channel_id=1, source_target_pairs={{0,64},{32,96},{64,0},{96,32},{128,192},{160,224},{192,128},{224,1... | collective-permute-start | bytes 258056 | tf_op jit(solution)/shard_map/ppermute | solution.py:417
  102.1 4.6 %collective-permute-start.28 = (f32[168,128]{1,0:T(8,128)S(1)}, f32[168,128]{1,0:T(8,128)S(1)}, u32[]{:S(2)}, u32[]{:S(2)}) collective-permute-start(f32[168,128]{1,0:T(8,128)S(1)} %add.75), channel_id=1, source_target_pairs={{0,192},{32,224},{64,128},{96,160},{128,64},{160,96},{192,0},{224,... | collective-permute-start | bytes 258056 | tf_op jit(solution)/shard_map/ppermute | solution.py:417
  106.7 3.4 %collective-permute-start.29 = (f32[168,128]{1,0:T(8,128)S(1)}, f32[168,128]{1,0:T(8,128)S(1)}, u32[]{:S(2)}, u32[]{:S(2)}) collective-permute-start(f32[168,128]{1,0:T(8,128)S(1)} %add.76), channel_id=1, source_target_pairs={{0,8},{1,9},{2,10},{3,11},{4,12},{5,13},{6,14},{7,15},{8,0},{9,1},... | collective-permute-start | bytes 258056 | tf_op jit(solution)/shard_map/ppermute | solution.py:417
  110.2 4.6 %collective-permute-start.30 = (f32[168,128]{1,0:T(8,128)S(1)}, f32[168,128]{1,0:T(8,128)S(1)}, u32[]{:S(2)}, u32[]{:S(2)}) collective-permute-start(f32[168,128]{1,0:T(8,128)S(1)} %add.77), channel_id=1, source_target_pairs={{0,24},{1,25},{2,26},{3,27},{4,28},{5,29},{6,30},{7,31},{8,16},{9,... | collective-permute-start | bytes 258056 | tf_op jit(solution)/shard_map/ppermute | solution.py:417
  114.8 3.4 %collective-permute-start.31 = (f32[168,128]{1,0:T(8,128)S(1)}, f32[168,128]{1,0:T(8,128)S(1)}, u32[]{:S(2)}, u32[]{:S(2)}) collective-permute-start(f32[168,128]{1,0:T(8,128)S(1)} %add.78), channel_id=1, source_target_pairs={{0,1},{1,0},{2,3},{3,2},{4,5},{5,4},{6,7},{7,6},{8,9},{9,8},{10,11... | collective-permute-start | bytes 258056 | tf_op jit(solution)/shard_map/ppermute | solution.py:417
  118.3 4.6 %collective-permute-start.32 = (f32[168,128]{1,0:T(8,128)S(1)}, f32[168,128]{1,0:T(8,128)S(1)}, u32[]{:S(2)}, u32[]{:S(2)}) collective-permute-start(f32[168,128]{1,0:T(8,128)S(1)} %add.79), channel_id=1, source_target_pairs={{0,7},{1,2},{2,1},{3,4},{4,3},{5,6},{6,5},{7,0},{8,15},{9,10},{10,... | collective-permute-start | bytes 258056 | tf_op jit(solution)/shard_map/ppermute | solution.py:417
  122.9 6.4 %collective-permute-start.33 = (f32[168,128]{1,0:T(8,128)S(1)}, f32[168,128]{1,0:T(8,128)S(1)}, u32[]{:S(2)}, u32[]{:S(2)}) collective-permute-start(f32[168,128]{1,0:T(8,128)S(1)} %add.80), channel_id=1, source_target_pairs={{0,3},{1,6},{2,5},{3,0},{4,7},{5,2},{6,1},{7,4},{8,11},{9,14},{10,... | collective-permute-start | bytes 258056 | tf_op jit(solution)/shard_map/ppermute | solution.py:417
  129.3 3.4 %collective-permute-start.34 = (f32[168,128]{1,0:T(8,128)S(1)}, f32[168,128]{1,0:T(8,128)S(1)}, u32[]{:S(2)}, u32[]{:S(2)}) collective-permute-start(f32[168,128]{1,0:T(8,128)S(1)} %add.81), channel_id=1, source_target_pairs={{0,64},{32,96},{64,0},{96,32},{128,192},{160,224},{192,128},{224,1... | collective-permute-start | bytes 258056 | tf_op jit(solution)/shard_map/ppermute | solution.py:417
  132.7 11.0 %collective-permute-start.35 = (f32[336,128]{1,0:T(8,128)S(1)}, f32[336,128]{1,0:T(8,128)S(1)}, u32[]{:S(2)}, u32[]{:S(2)}) collective-permute-start(f32[336,128]{1,0:T(8,128)S(1)} %maximum_select_fusion.3), channel_id=1, source_target_pairs={{0,32},{32,0},{64,96},{96,64},{128,160},{160,128},{192,224},{224,1... | collective-permute-start | bytes 516104 | tf_op jit(solution)/shard_map/ppermute | solution.py:417
